TPU v7x, 32 devices: a whole 2x2x4 slice. The times are simulated.
32 devices in a mesh: dates: 2 (over x), cols: 16 (over z, y, core).
Axes of the slice: x: 2, y: 2, z: 4, core: 2. Of those that a mesh axis runs over, the one named last changes fastest.
Arguments:
- complex_images: bfloat16 [296, 32, 2, 8192], P('dates', None, None, 'cols'), may hold values from -4 to 4
- pair_list: int32 [1480, 2], replicated, may hold values from 0 to 295, as said below
Outputs:
- refined_series: float32 [296, 16, 2, 2048], P(None, 'dates', None, 'cols')
Inputs may be any that keep to these rules, and one draw needn't show every extreme that they name: `pair_list`: each row holds a reference date and a later secondary date at most 12 dates after it; some pair starts at date 0 and some ends at date 296 - 1.
All inputs are finite; a program needn't handle non-finite values.
Results may differ from a plain program's by a relative error of at most 0.0045.
Values may be sent and summed in bfloat16 or wider, within the bound.
No kernel may reach another device: no remote copies, remote signals or barrier semaphores. Data moves between devices by JAX's collectives and lax.ppermute only.
A program may use at most 128 MiB of HBM per device.

v0:
```python
import jax
import jax.numpy as jnp
from jax import lax
from jax.sharding import PartitionSpec as P

LOOKR = 2
LOOKC = 4
PAIR_BLOCK = 37


ridge = 0.5
highest = lax.Precision.HIGHEST


def pseudo_inverse(pair_list, count):
    date_ids = jnp.arange(count, dtype=jnp.int32)
    design = (pair_list[:, 0:1] == date_ids[None, :]).astype(jnp.float32) - (
        pair_list[:, 1:2] == date_ids[None, :]
    ).astype(jnp.float32)
    normal = jnp.dot(design.T, design, precision=highest) + ridge * jnp.eye(
        count, dtype=jnp.float32
    )
    factor = jnp.linalg.cholesky(normal)
    return jax.scipy.linalg.cho_solve((factor, True), design.T)


def pool_looks(plane):
    count, rows, cols = plane.shape
    rows_pooled = jnp.sum(plane.reshape(count, rows // LOOKR, LOOKR, cols), axis=2)
    return jnp.sum(rows_pooled.reshape(count, rows // LOOKR, cols // LOOKC, LOOKC), axis=3)


def multilook_pairs(tile_stack, pair_list, pair_block):
    real_planes = tile_stack[:, :, 0, :]
    imag_planes = tile_stack[:, :, 1, :]
    groups = pair_list.reshape(-1, pair_block, 2)
    scale = 1.0 / float(LOOKR * LOOKC)

    def one_group(group):
        first_real = jnp.take(real_planes, group[:, 0], axis=0).astype(jnp.float32)
        first_imag = jnp.take(imag_planes, group[:, 0], axis=0).astype(jnp.float32)
        second_real = jnp.take(real_planes, group[:, 1], axis=0).astype(jnp.float32)
        second_imag = jnp.take(imag_planes, group[:, 1], axis=0).astype(jnp.float32)
        real_part = pool_looks(first_real * second_real + first_imag * second_imag)
        imag_part = pool_looks(first_imag * second_real - first_real * second_imag)
        return (jnp.stack([real_part, imag_part], axis=2) * scale).astype(jnp.bfloat16)

    looked = lax.map(one_group, groups)
    return looked.reshape((pair_list.shape[0],) + looked.shape[2:])


def coordinates(start, count, total):
    return (2.0 * (start + jnp.arange(count, dtype=jnp.int32)).astype(jnp.float32) + 1.0) / float(
        total
    ) - 1.0


def basis_planes(row_coord, col_coord):
    constant = jnp.ones((row_coord.shape[0], col_coord.shape[0]), jnp.float32)
    return jnp.stack([constant, row_coord[:, None] * constant, col_coord[None, :] * constant])


def weighted(widened, planes, pair_count):
    weights = jnp.sum(widened * widened, axis=(0, 2)) / float(pair_count)
    weighted_planes = planes * weights[None]
    normal = jnp.einsum("jrc,krc->jk", weighted_planes, planes, precision=highest)
    return (weighted_planes, normal)


def inverse3(matrix):

    def cyclic(row_at, col_at):
        return (
            matrix[(row_at + 1) % 3, (col_at + 1) % 3] * matrix[(row_at + 2) % 3, (col_at + 2) % 3]
            - matrix[(row_at + 1) % 3, (col_at + 2) % 3]
            * matrix[(row_at + 2) % 3, (col_at + 1) % 3]
        )

    cofacts = jnp.stack(
        [jnp.stack([cyclic(row_at, col_at) for col_at in range(3)]) for row_at in range(3)]
    )
    determinant = jnp.sum(matrix[0] * cofacts[0])
    return cofacts.T / determinant


def refine(series, ramp_rhs, normal, planes):
    ramp_coef = jnp.einsum("jk,dkh->djh", inverse3(normal), ramp_rhs, precision=highest)
    return series - jnp.einsum("djh,jrc->drhc", ramp_coef, planes, precision=highest)


def body(complex_images, pair_list):
    date_count = lax.axis_size("dates")
    date_index = lax.axis_index("dates")
    col_index = lax.axis_index("cols")
    pair_count = pair_list.shape[0]
    date_total = complex_images.shape[0] * date_count
    rounded_pseudo = pseudo_inverse(pair_list, date_total).astype(jnp.bfloat16)
    regrouped = lax.all_to_all(complex_images, "dates", split_axis=1, concat_axis=0, tiled=True)
    interferograms = multilook_pairs(regrouped, pair_list, PAIR_BLOCK * date_count)
    ml_rows = interferograms.shape[1]
    ml_cols = interferograms.shape[3]
    planes = basis_planes(
        coordinates(date_index * ml_rows, ml_rows, ml_rows * date_count),
        coordinates(col_index * ml_cols, ml_cols, ml_cols * lax.axis_size("cols")),
    )
    widened = interferograms.astype(jnp.float32)
    weighted_planes, normal_part = weighted(widened, planes, pair_count)
    flat_pairs = interferograms.reshape(pair_count, -1)
    series = jnp.dot(rounded_pseudo, flat_pairs, preferred_element_type=jnp.float32).reshape(
        (date_total,) + interferograms.shape[1:]
    )
    rhs_part = jnp.einsum("jrc,drhc->djh", weighted_planes, series, precision=highest)
    normal, ramp_rhs = lax.psum((normal_part, rhs_part), ("dates", "cols"))
    return refine(series, ramp_rhs, normal, planes)


def solution(mesh):
    return jax.shard_map(
        body,
        mesh=mesh,
        in_specs=(P("dates", None, None, "cols"), P()),
        out_specs=P(None, "dates", None, "cols"),
        check_vma=False,
    )
```

profile of v0, /device:TPU:0, one launch (start us, length us, event | category | flops | bytes accessed | tf_op | source)
XLA Modules:
  0.0 1204.6 jit_solution(11292636294556829429)
XLA Ops:
  0.0 12.6 %copy.74 = bf16[148,32,2,512]{3,2,0,1:T(2,128)(2,1)} copy(bf16[148,32,2,512]{3,2,1,0:T(2,128)(2,1)} %param.6) | data formatting | bytes 19398656 | tf_op args[0]
  12.6 7.6 all-to-all-start
  26.2 11.7 cholesky.77
  38.0 9.8 custom-call.26
  48.4 11.9 cholesky.162
  60.3 9.8 custom-call.27
  81.7 30.0 %custom-call.28 = f32[3,128,128]{1,2,0:T(8,128)S(1)} custom-call(f32[3,128,128]{2,1,0:T(8,128)S(1)} %pad_maximum_fusion), custom_call_target="InvertDiagBlocksLowerTriangular" | custom-call | tf_op jit(solution)/shard_map/jit(_cho_solve)/triangular_solve | solution.py:24
  128.0 10.8 copy.75
  138.9 8.7 slice_bitcast_fusion
  147.5 929.0 %while.11 = (s32[]{:T(128)}, bf16[20,74,8,2,128]{1,2,4,3,0:T(8,128)(2,1)}, s32[20,74,2]{1,0,2:T(8,128)S(1)}, bf16[296,16,512]{2,1,0:T(8,128)(2,1)}, bf16[296,16,512]{2,1,0:T(8,128)(2,1)}, /*index=5*/s32[]{:T(128)}, f32[]{:T(128)}) while((s32[]{:T(128)}, bf16[20,74,8,2,128]{1,2,4,3,0:T(8,128)(2,1)}, s32[20,74,2]{1,0,2:T(8,128)S(1)}, ...), condition=%wide.region_11.13_spmd, body=%wide.region_6.12_spmd.sunk | while | flops 10005370 | bytes 46608856 | solution.py:48
  265.2 5.8 reduce_sum.66
  311.6 5.8 reduce_sum.66
  358.1 5.8 reduce_sum.66
  543.9 5.8 reduce_sum.66
  590.3 5.8 reduce_sum.66
  683.2 5.8 reduce_sum.66
  776.1 5.8 reduce_sum.66
  869.0 5.8 reduce_sum.66
  915.4 5.8 reduce_sum.66
  1076.5 18.2 %copy.77 = bf16[20,74,8,2,128]{4,3,2,1,0:T(2,128)(2,1)} copy(bf16[20,74,8,2,128]{1,2,4,3,0:T(8,128)(2,1)} %get-tuple-element.33) | data formatting | bytes 12124160 | tf_op jit(solution)/shard_map/while | solution.py:48
  1094.7 6.8 multiply_reduce_fusion
  1101.5 14.1 %reshape_reshape.3 = bf16[1480,2048]{1,0:T(8,128)(2,1)} reshape(bf16[20,74,8,2,128]{4,3,2,1,0:T(2,128)(2,1)} %copy.77) | data formatting | bytes 12124160 | tf_op jit(solution)/shard_map/reshape;reshape | solution.py:108
  1115.6 8.7 copy.78
  1131.9 42.2 %all-reduce.3 = (f32[296,3,2]{0,1,2:T(4,128)S(1)}, f32[3,3]{1,0:T(4,128)S(1)}) all-reduce(f32[296,3,2]{0,1,2:T(4,128)S(1)} %convolution_bitcast_fusion.1, f32[3,3]{1,0:T(4,128)S(1)} %convolution_bitcast_fusion.2), channel_id=1, replica_groups=mesh['dates'=2,'cols'=16] {'dates','cols'}, use_global_device_ids=true, to_apply=%region_13.15 | all-reduce | flops 1785 | bytes 14280 | tf_op jit(solution)/shard_map/psum | solution.py:113
  (446 shorter events, 927.8 us)
Async XLA Ops:
  12.6 7.6 copy-start.3
  12.6 115.4 %all-to-all-start = ((bf16[148,32,2,512]{3,2,0,1:T(2,128)(2,1)}), bf16[148,32,2,512]{3,2,0,1:T(2,128)(2,1)}, u32[]{:S(2)}, u32[]{:S(2)}) async-start(bf16[148,32,2,512]{3,2,0,1:T(2,128)(2,1)} %copy.74), calls=%async_computation | async-start | bytes 19398656 | tf_op jit(solution)/shard_map/all_to_all | solution.py:98
  192.0 1.0 copy-start
  238.4 1.0 copy-start
  284.9 1.0 copy-start
  331.3 1.0 copy-start
  377.8 1.0 copy-start
  424.2 1.0 copy-start
  470.7 1.0 copy-start
  517.1 1.0 copy-start
  563.5 1.0 copy-start
  610.0 1.0 copy-start
  656.4 1.0 copy-start
  702.9 1.0 copy-start
  749.3 1.0 copy-start
  795.8 1.0 copy-start
  842.2 1.0 copy-start
  888.7 1.0 copy-start
  935.1 1.0 copy-start
  981.6 1.0 copy-start
  1028.1 1.0 copy-start
  1074.5 1.0 copy-start
  1115.6 8.8 copy-start.1
  1115.6 8.8 copy-start.2
where the time goes:
time: 1220 us; the launch traced here: 1200 us
  local copies, waits for them, and re-layouts  639 us (52%)
  other arithmetic  458 us (38%)
  blocking collectives  42.2 us (3%)
  matrix products  30.7 us (3%)
  between operations  25.2 us (2%)
    reduce_sum x40, other arithmetic, pool_looks(): jnp.sum(plane.reshape(count, rows // LOOKR, LOOKR, cols), axis=2)  209 us
    reshape x40, local copies, waits for them, and re-layouts, pool_looks(): plane.reshape(count, rows // LOOKR, LOOKR, cols)  130 us
    gather x20, local copies, waits for them, and re-layouts, one_group(): first_imag = jnp.take(imag_planes, group[:, 0], axis=0).astype(jnp.float32)  84.2 us
    gather x20, local copies, waits for them, and re-layouts, one_group(): first_real = jnp.take(real_planes, group[:, 0], axis=0).astype(jnp.float32)  83.4 us
    gather x20, local copies, waits for them, and re-layouts, one_group(): second_real = jnp.take(real_planes, group[:, 1], axis=0).astype(jnp.float32)  83.3 us
    gather x20, local copies, waits for them, and re-layouts, one_group(): second_imag = jnp.take(imag_planes, group[:, 1], axis=0).astype(jnp.float32)  83 us
    add x20, other arithmetic, one_group(): real_part = pool_looks(first_real * second_real + first_imag * second_imag)  80.5 us
    reduce_sum x40, local copies, waits for them, and re-layouts, pool_looks(): jnp.sum(plane.reshape(count, rows // LOOKR, LOOKR, cols), axis=2)  78.3 us
  transfers between devices with their start and end apart: 1, of which 1 were waited for; matrix products, arithmetic and copies ran while one was open for 9% of the time, Pallas kernels for 0%

commit v1 on v0

--- a/solution.py
+++ b/solution.py
@@ -1,14 +1,523 @@
 import jax
 import jax.numpy as jnp
+import numpy as np
 from jax import lax
+from jax.experimental import pallas as pl
+from jax.experimental.pallas import tpu as pltpu
 from jax.sharding import PartitionSpec as P
 
 LOOKR = 2
 LOOKC = 4
 PAIR_BLOCK = 37
-
-
-ridge = 0.5
+GAP = 12
+RIDGE = 0.5
+MAX_STEP = 40
+UNROLL = 8
+CHOOSE_UNROLL = 8
+LANES = 128
+SPLIT = 4
+VMEM_LIMIT = 56 * 1024 * 1024
+NN = (((1,), (0,)), ((), ()))
+NT = (((1,), (1,)), ((), ()))
+
+
+def look_matrix():
+    row = np.arange(SPLIT * LANES)
+    lane, sub = row % LANES, row // LANES
+    target = (lane % LOOKC) * LANES + sub * (LANES // SPLIT) + lane // LOOKC
+    return (target[:, None] == row[None, :]).astype(np.float32)
+
+
+def split_bf16(value):
+    high = value.astype(jnp.bfloat16)
+    return high, (value - high.astype(jnp.float32)).astype(jnp.bfloat16)
+
+
+def dot32(first, second, dims):
+    return lax.dot_general(first, second, dims, preferred_element_type=jnp.float32)
+
+
+def spread_looks(source, date, slot, step, looks, planes):
+    raw = source[pl.ds(date, step)].reshape(step, 2, SPLIT, 16, LANES)
+    left = jnp.concatenate(
+        [raw[:, :, sub].reshape(step * 32, LANES) for sub in range(SPLIT)], axis=1
+    )
+    spread = dot32(left, looks[...], NN)
+    for at in range(step):
+        base = pl.multiple_of((slot + at) * 128, 128)
+        for group in range(2):
+            for rlook in range(LOOKR):
+                top = (at * 2 + group) * 16 + rlook * 8
+                for look in range(LOOKC):
+                    planes[pl.ds(base + (rlook * LOOKC + look) * 16 + group * 8, 8), :] = spread[
+                        top : top + 8, look * LANES : (look + 1) * LANES
+                    ]
+
+
+def pair_kernel(pair_count, with_halo, step, *refs):
+    if with_halo:
+        (bounds, listed, counts, images, halo, looks, series, weights, raw, raw_halo, planes, sems) = refs
+    else:
+        (bounds, pairs, images, looks, series, listed, counts, raw, planes, sems, sums) = refs
+    dates = images.shape[0]
+    steps = dates // step
+    row_start, own_slot, halo_slot = bounds[0], bounds[1], bounds[2]
+    copies = [
+        pltpu.make_async_copy(
+            images.at[pl.ds(at * step, step), pl.ds(row_start, 8)],
+            raw.at[pl.ds(at * step, step)],
+            sems.at[at],
+        )
+        for at in range(steps)
+    ]
+    if with_halo:
+        copies.append(pltpu.make_async_copy(halo, raw_halo, sems.at[steps]))
+    for copy in copies:
+        copy.start()
+
+    total = series if with_halo else sums
+    spare = dates + GAP
+    total[...] = jnp.zeros_like(total)
+    planes[pl.ds(spare * 128, 128), :] = jnp.zeros((128, LANES), jnp.float32)
+
+    if not with_halo:
+        def choose(at, found):
+            inside, across = found
+            packed = pairs[at]
+            listed[inside] = packed
+            listed[pair_count + UNROLL + across] = packed
+            return (inside + ((packed >> 20) & 1), across + (packed >> 21))
+
+        found = lax.fori_loop(
+            0, pair_count, choose, (jnp.int32(0), jnp.int32(0)), unroll=CHOOSE_UNROLL
+        )
+        for part in range(2):
+            counts[part] = found[part]
+            for at in range(UNROLL):
+                listed[part * (pair_count + UNROLL) + found[part] + at] = jnp.int32(spare * 1025)
+
+    def spread_step(at, carry):
+        spread_looks(raw, at * step, own_slot + at * step, step, looks, planes)
+        return carry
+
+    for at in range(steps):
+        copies[at].wait()
+        spread_step(at, 0)
+    if with_halo:
+        copies[steps].wait()
+        spread_looks(raw_halo, 0, halo_slot, GAP, looks, planes)
+
+    def one_pair(packed, power):
+        first = packed & 1023
+        second = (packed >> 10) & 1023
+        a_row = pl.multiple_of(first * 128, 128)
+        b_row = pl.multiple_of(second * 128, 128)
+        terms_re, terms_im = [], []
+        for look in range(LOOKR * LOOKC):
+            a_re = planes[pl.ds(a_row + look * 16, 8, stride=2), :]
+            a_im = planes[pl.ds(a_row + look * 16 + 1, 8, stride=2), :]
+            b_re = planes[pl.ds(b_row + look * 16, 8, stride=2), :]
+            b_im = planes[pl.ds(b_row + look * 16 + 1, 8, stride=2), :]
+            terms_re.append(a_re * b_re + a_im * b_im)
+            terms_im.append(a_im * b_re - a_re * b_im)
+        while len(terms_re) > 1:
+            terms_re = [terms_re[k] + terms_re[k + 1] for k in range(0, len(terms_re), 2)]
+            terms_im = [terms_im[k] + terms_im[k + 1] for k in range(0, len(terms_im), 2)]
+        real = terms_re[0].astype(jnp.bfloat16).astype(jnp.float32)
+        imag = terms_im[0].astype(jnp.bfloat16).astype(jnp.float32)
+        a_at = pl.multiple_of(first * 16, 16)
+        b_at = pl.multiple_of(second * 16, 16)
+        total[pl.ds(a_at, 8), :] += real
+        total[pl.ds(a_at + 8, 8), :] += imag
+        total[pl.ds(b_at, 8), :] -= real
+        total[pl.ds(b_at + 8, 8), :] -= imag
+        return power + (real * real + imag * imag)
+
+    power = jnp.zeros((8, LANES), jnp.float32)
+    for part in range(2 if with_halo else 1):
+
+        def some_pairs(at, power, part=part):
+            for k in range(UNROLL):
+                power = one_pair(listed[part * (pair_count + UNROLL) + at * UNROLL + k], power)
+            return power
+
+        power = lax.fori_loop(0, (counts[part] + UNROLL - 1) // UNROLL, some_pairs, power)
+    scale = 1.0 / float(LOOKR * LOOKC)
+    if with_halo:
+        weights[...] = power * (scale * scale / float(pair_count))
+    else:
+        def narrow(date, carry):
+            value = sums[pl.ds(pl.multiple_of((own_slot + date) * 16, 16), 16), :] * scale + carry
+            rounded = value.astype(jnp.bfloat16)
+            series[pl.ds(pl.multiple_of(date * 16, 16), 16), :] = rounded
+            return value - rounded.astype(jnp.float32)
+
+        lax.fori_loop(0, dates, narrow, jnp.zeros((16, LANES), jnp.float32), unroll=4)
+        high, low = split_bf16(power * (scale * scale / float(pair_count)))
+        series[pl.ds(dates * 16, 16), :] = jnp.concatenate(
+            [high.astype(jnp.float32), low.astype(jnp.float32)], axis=0
+        ).astype(jnp.bfloat16)
+
+
+def in_vmem():
+    return pl.BlockSpec(memory_space=pltpu.VMEM)
+
+
+def in_smem():
+    return pl.BlockSpec(memory_space=pltpu.SMEM)
+
+
+def in_hbm():
+    return pl.BlockSpec(memory_space=pl.ANY)
+
+
+def call_pairs(bounds, pairs, images, looks, given=None):
+    dates = images.shape[0]
+    pair_count = pairs.shape[0]
+    step = max(k for k in range(1, MAX_STEP + 1) if dates % k == 0)
+    slots = dates + GAP + 1
+    scratch = [
+        pltpu.VMEM((dates, 8, 16, LANES), jnp.bfloat16),
+        pltpu.VMEM((slots * 128, LANES), jnp.float32),
+        pltpu.SemaphoreType.DMA((dates // step + 1,)),
+    ]
+    sums = jax.ShapeDtypeStruct((slots * 16, LANES), jnp.float32)
+    if given is not None:
+        halo, listed, counts = given
+        out_shape = (sums, jax.ShapeDtypeStruct((8, LANES), jnp.float32))
+        scratch.insert(1, pltpu.VMEM((GAP, 8, 16, LANES), jnp.bfloat16))
+        in_specs = [in_smem()] * 3 + [in_hbm(), in_hbm(), in_vmem()]
+        out_specs = (in_vmem(), in_vmem())
+        args = (bounds, listed, counts, images, halo, looks)
+    else:
+        out_shape = (
+            jax.ShapeDtypeStruct(((dates + 1) * 16, LANES), jnp.bfloat16),
+            jax.ShapeDtypeStruct((2 * (pair_count + UNROLL),), jnp.int32),
+            jax.ShapeDtypeStruct((2,), jnp.int32),
+        )
+        scratch.append(pltpu.VMEM(sums.shape, sums.dtype))
+        in_specs = [in_smem(), in_smem(), in_hbm(), in_vmem()]
+        out_specs = (in_vmem(), in_smem(), in_smem())
+        args = (bounds, pairs, images, looks)
+    return pl.pallas_call(
+        lambda *refs: pair_kernel(pair_count, given is not None, step, *refs),
+        out_shape=out_shape,
+        in_specs=in_specs,
+        out_specs=out_specs,
+        scratch_shapes=scratch,
+        compiler_params=pltpu.CompilerParams(vmem_limit_bytes=VMEM_LIMIT),
+        cost_estimate=pl.CostEstimate(
+            flops=pair_count * 70 * 1024, bytes_accessed=dates * 8 * 16 * 256, transcendentals=0
+        ),
+        name="pairs_other" if given is None else "pairs_own",
+    )(*args)
+
+
+def half_basis(row_start, col_start, row_total, col_total):
+    sub = lax.broadcasted_iota(jnp.int32, (8, LANES), 0)
+    lane = lax.broadcasted_iota(jnp.int32, (8, LANES), 1)
+    width = LANES // SPLIT
+    row = row_start + (sub // SPLIT) * SPLIT + lane // width
+    col = col_start + (sub % SPLIT) * width + lane % width
+    return centred(row, row_total), centred(col, col_total)
+
+
+def centred(place, total):
+    return (2.0 * place.astype(jnp.float32) + 1.0) / float(total) - 1.0
+
+
+def combine_kernel(dates, row_total, col_total, *refs):
+    (bounds, own, own_weights, other, high, low, moments, full, weighted_rows) = refs
+    count = dates * 2
+    span = dates + GAP
+    scale = 1.0 / float(LOOKR * LOOKC)
+
+    def rows(start, size):
+        return pl.ds(pl.multiple_of(start * 16, 16), size * 16)
+
+    full[rows(bounds[0], span), :] = own[pl.ds(0, span * 16), :] * scale
+    rest = dates - GAP
+    full[rows(bounds[1], rest), :] = other[rows(bounds[2], rest), :].astype(jnp.float32)
+    full[rows(bounds[3], GAP), :] += other[rows(bounds[4], GAP), :].astype(jnp.float32)
+    y_plane, x_plane = half_basis(bounds[5], bounds[6], row_total, col_total)
+    basis = (jnp.ones((8, LANES), jnp.float32), y_plane, x_plane)
+    padded = full.shape[0] // 16
+    full[pl.ds(count * 16, (padded - count) * 16), :] = jnp.zeros(
+        ((padded - count) * 16, LANES), jnp.float32
+    )
+    for at in range(3):
+        full[pl.ds((count + at) * 16, 8), :] = basis[at]
+    sent = other[pl.ds(dates * 16, 16), :].astype(jnp.float32)
+    weights = own_weights[...] + (sent[:8] + sent[8:])
+    weighted_rows[...] = jnp.zeros_like(weighted_rows)
+    for at in range(3):
+        plane = weights * basis[at]
+        for part in range(2):
+            for sub in range(8):
+                weighted_rows[part * 3 + at : part * 3 + at + 1, pl.ds((part * 8 + sub) * LANES, LANES)] = (
+                    plane[sub : sub + 1]
+                )
+    for at in range(16):
+        value = full[pl.ds(at, padded, stride=16), :]
+        upper, lower = split_bf16(value)
+        high[:, at * LANES : (at + 1) * LANES] = upper
+        low[:, at * LANES : (at + 1) * LANES] = lower
+    upper, lower = split_bf16(weighted_rows[...])
+    moments[...] = (
+        dot32(upper, high[...], NT) + dot32(lower, high[...], NT) + dot32(upper, low[...], NT)
+    )
+
+
+def call_combine(bounds, own, own_weights, other, dates, row_total, col_total):
+    padded = pad_dates(dates * 2)
+    wide = jax.ShapeDtypeStruct((padded, 16 * LANES), jnp.bfloat16)
+    return pl.pallas_call(
+        lambda *refs: combine_kernel(dates, row_total, col_total, *refs),
+        out_shape=(wide, wide, jax.ShapeDtypeStruct((8, padded), jnp.float32)),
+        in_specs=[in_smem()] + [in_vmem()] * 3,
+        out_specs=(in_vmem(),) * 3,
+        scratch_shapes=[
+            pltpu.VMEM((padded * 16, LANES), jnp.float32),
+            pltpu.VMEM((8, 16 * LANES), jnp.float32),
+        ],
+        compiler_params=pltpu.CompilerParams(vmem_limit_bytes=VMEM_LIMIT),
+        cost_estimate=pl.CostEstimate(flops=padded * 8 * 12288, bytes_accessed=8 << 20, transcendentals=0),
+        name="combine",
+    )(bounds, own, own_weights, other)
+
+
+def pad_dates(count):
+    return (count + 3 + 15) // 16 * 16
+
+
+def inverse_kernel(pairs, high, low, state, normal_high, normal_low):
+    padded = high.shape[0]
+    date = lax.broadcasted_iota(jnp.int32, (padded, pairs.shape[1]), 0)
+    design = (
+        jnp.where(date == pairs[0:1, :], 1.0, 0.0) - jnp.where(date == pairs[1:2, :], 1.0, 0.0)
+    ).astype(jnp.bfloat16)
+    eye = jnp.where(
+        lax.broadcasted_iota(jnp.int32, (padded, padded), 0)
+        == lax.broadcasted_iota(jnp.int32, (padded, padded), 1),
+        1.0,
+        0.0,
+    )
+    normal = dot32(design, design, NT) + RIDGE * eye
+    normal_high[...], normal_low[...] = split_bf16(normal)
+    largest = jnp.max(jnp.sum(jnp.abs(normal), axis=1))
+    state[...] = eye * (2.0 / (largest + RIDGE))
+    error = (largest - RIDGE) / (largest + RIDGE)
+
+    def product(first, second):
+        return (
+            dot32(first[0], second[0], NN) + dot32(first[0], second[1], NN) + dot32(first[1], second[0], NN)
+        )
+
+    def step(error):
+        scale = 2.0 / (2.0 - error * error)
+        now = split_bf16(state[...])
+        residual = split_bf16(eye - product((normal_high[...], normal_low[...]), now))
+        state[...] = scale * (state[...] + product(now, residual))
+        return scale - 1.0
+
+    lax.while_loop(lambda error: error > 1e-6, step, error)
+    step(jnp.float32(0.0))
+    high[...], low[...] = split_bf16(state[...])
+
+
+def call_inverse(pair_rows, count):
+    padded = pad_dates(count)
+    square = jax.ShapeDtypeStruct((padded, padded), jnp.bfloat16)
+    return pl.pallas_call(
+        inverse_kernel,
+        out_shape=(square, square),
+        in_specs=[in_vmem()],
+        out_specs=(in_vmem(),) * 2,
+        scratch_shapes=[
+            pltpu.VMEM((padded, padded), jnp.float32),
+            pltpu.VMEM((padded, padded), jnp.bfloat16),
+            pltpu.VMEM((padded, padded), jnp.bfloat16),
+        ],
+        compiler_params=pltpu.CompilerParams(vmem_limit_bytes=VMEM_LIMIT),
+        cost_estimate=pl.CostEstimate(flops=100 * padded**3, bytes_accessed=8 << 20, transcendentals=0),
+        name="inverse",
+    )(pair_rows)
+
+
+def solve_kernel(inverse_high, inverse_low, high, low, series):
+    padded = high.shape[0]
+    lane = lax.broadcasted_iota(jnp.int32, (padded, LANES), 1)
+    width = LANES // SPLIT
+    for group in range(4):
+        cols = pl.ds(group * SPLIT * LANES, SPLIT * LANES)
+        solved = (
+            dot32(inverse_high[...], high[:, cols], NN)
+            + dot32(inverse_high[...], low[:, cols], NN)
+            + dot32(inverse_low[...], high[:, cols], NN)
+        )
+        blocks = [solved[:, k * LANES : (k + 1) * LANES] for k in range(SPLIT)]
+        for bit in (1, 2):
+            shift = bit * width
+            even = (lane // shift) % 2 == 0
+            swapped = list(blocks)
+            for k in range(SPLIT):
+                if k & bit == 0:
+                    first, second = blocks[k], blocks[k | bit]
+                    swapped[k] = jnp.where(even, first, pltpu.roll(second, shift, 1))
+                    swapped[k | bit] = jnp.where(even, pltpu.roll(first, LANES - shift, 1), second)
+            blocks = swapped
+        part, half = group // 2, group % 2
+        for k in range(SPLIT):
+            series[(half * SPLIT + k) * 2 + part] = blocks[k]
+
+
+def call_solve(inverse, values):
+    padded = values[0].shape[0]
+    return pl.pallas_call(
+        solve_kernel,
+        out_shape=jax.ShapeDtypeStruct((16, padded, LANES), jnp.float32),
+        in_specs=[in_vmem()] * 4,
+        out_specs=in_vmem(),
+        compiler_params=pltpu.CompilerParams(vmem_limit_bytes=VMEM_LIMIT),
+        cost_estimate=pl.CostEstimate(
+            flops=6 * padded * padded * 16 * LANES, bytes_accessed=6 << 20, transcendentals=0
+        ),
+        name="solve",
+    )(*inverse, *values)
+
+
+def refine_kernel(count, row_total, col_total, *refs):
+    (bounds, series, moments, inverse_high, inverse_low, refined) = refs
+    padded = series.shape[1]
+    normal = [
+        [moments[at : at + 1, count + k : count + k + 1] for k in range(3)] for at in range(3)
+    ]
+
+    def cyclic(row_at, col_at):
+        a, b = (row_at + 1) % 3, (row_at + 2) % 3
+        c, d = (col_at + 1) % 3, (col_at + 2) % 3
+        return normal[a][c] * normal[b][d] - normal[a][d] * normal[b][c]
+
+    cofacts = [[cyclic(row_at, col_at) for col_at in range(3)] for row_at in range(3)]
+    determinant = sum(normal[0][k] * cofacts[0][k] for k in range(3))
+    rows = []
+    for part in range(2):
+        for at in range(3):
+            rows.append(
+                sum(
+                    (cofacts[k][at] / determinant) * moments[part * 3 + k : part * 3 + k + 1, :]
+                    for k in range(3)
+                )
+            )
+    rows.append(jnp.zeros((2, padded), jnp.float32))
+    upper, lower = split_bf16(jnp.concatenate(rows, axis=0))
+    ramps = (
+        dot32(inverse_high[...], upper, NT)
+        + dot32(inverse_high[...], lower, NT)
+        + dot32(inverse_low[...], upper, NT)
+    )[:count]
+    lane = lax.broadcasted_iota(jnp.int32, (1, LANES), 1)
+    x_row = centred(bounds[1] + lane, col_total)
+    for part in range(2):
+        level, along_y, along_x = (
+            jnp.broadcast_to(ramps[:, part * 3 + at : part * 3 + at + 1], (count, LANES))
+            for at in range(3)
+        )
+        level = level + along_x * x_row
+        for row in range(8):
+            y = centred(bounds[0] + row, row_total)
+            refined[pl.ds(row * 2 + part, count, stride=16), :] = series[row * 2 + part, :count] - (
+                level + along_y * y
+            )
+
+
+def call_refine(bounds, series, moments, inverse, count, row_total, col_total):
+    return pl.pallas_call(
+        lambda *refs: refine_kernel(count, row_total, col_total, *refs),
+        out_shape=jax.ShapeDtypeStruct((count * 16, LANES), jnp.float32),
+        in_specs=[in_smem()] + [in_vmem()] * 4,
+        out_specs=in_vmem(),
+        compiler_params=pltpu.CompilerParams(vmem_limit_bytes=VMEM_LIMIT),
+        cost_estimate=pl.CostEstimate(flops=count * 16 * LANES * 6, bytes_accessed=5 << 20, transcendentals=0),
+        name="refine",
+    )(bounds, series, moments, *inverse)
+
+
+def sum_devices(value):
+    cols = lax.axis_size("cols")
+    if cols & (cols - 1):
+        return lax.psum(value, ("dates", "cols"))
+    bit = 1
+    while bit < cols:
+        value = value + lax.ppermute(value, "cols", [(at, at ^ bit) for at in range(cols)])
+        bit *= 2
+        if bit == 2:
+            value = value + swap_dates(value)
+    return value
+
+
+def swap_dates(value):
+    return lax.ppermute(value, "dates", [(0, 1), (1, 0)])
+
+
+def two_halves(complex_images, pair_list):
+    dates, rows, _, cols = complex_images.shape
+    me = lax.axis_index("dates")
+    half = rows // LOOKR // 2
+    row_total, col_total = half * 2, cols // LOOKC * lax.axis_size("cols")
+    images = complex_images.reshape(dates, rows, 2, SPLIT, cols // SPLIT)
+    images = images.transpose(0, 1, 3, 2, 4).reshape(dates, rows // LOOKR, 16, LANES)
+    first, second = pair_list[:, 0], pair_list[:, 1]
+    low, base = dates * me, (dates - GAP) * me
+    first_own = (first >= low) & (first < low + dates)
+    second_own = (second >= low) & (second < low + dates)
+    inside = (first_own & second_own).astype(jnp.int32)
+    across = (first_own ^ second_own).astype(jnp.int32)
+    packed = (first - base) | ((second - base) << 10)
+    packed = jnp.where(first_own | second_own, packed | (inside << 20) | (across << 21), 0)
+
+    edge = lax.dynamic_slice(
+        images, ((dates - GAP) * (1 - me), half * (1 - me), 0, 0), (GAP, half, 16, LANES)
+    )
+    halo = swap_dates(edge)
+    looks = jnp.asarray(look_matrix(), jnp.bfloat16)
+    own_slot, halo_slot = GAP * me, dates * (1 - me)
+    other, listed, counts = call_pairs(
+        jnp.stack([half * (1 - me), own_slot, halo_slot]), packed, images, looks
+    )
+    other = swap_dates(other)
+    own, own_weights = call_pairs(
+        jnp.stack([half * me, own_slot, halo_slot]), packed, images, looks, (halo, listed, counts)
+    )
+    row_start, col_start = half * me, LANES * lax.axis_index("cols")
+    high, lowpart, moments = call_combine(
+        jnp.stack(
+            [
+                base,
+                (dates + GAP) * (1 - me),
+                GAP * (1 - me),
+                dates - GAP * me,
+                (dates - GAP) * me,
+                row_start,
+                col_start,
+            ]
+        ),
+        own,
+        own_weights,
+        other,
+        dates,
+        row_total,
+        col_total,
+    )
+    inverse = call_inverse(pair_list.T, dates * 2)
+    moments = sum_devices(moments)
+    series = call_solve(inverse, (high, lowpart))
+    refined = call_refine(
+        jnp.stack([row_start, col_start]), series, moments, inverse, dates * 2, row_total, col_total
+    )
+    return refined.reshape(dates * 2, half, 2, LANES)
+
+
 highest = lax.Precision.HIGHEST
 
 
@@ -17,7 +526,7 @@
     design = (pair_list[:, 0:1] == date_ids[None, :]).astype(jnp.float32) - (
         pair_list[:, 1:2] == date_ids[None, :]
     ).astype(jnp.float32)
-    normal = jnp.dot(design.T, design, precision=highest) + ridge * jnp.eye(
+    normal = jnp.dot(design.T, design, precision=highest) + RIDGE * jnp.eye(
         count, dtype=jnp.float32
     )
     factor = jnp.linalg.cholesky(normal)
@@ -88,7 +597,7 @@
     return series - jnp.einsum("djh,jrc->drhc", ramp_coef, planes, precision=highest)
 
 
-def body(complex_images, pair_list):
+def any_dates(complex_images, pair_list):
     date_count = lax.axis_size("dates")
     date_index = lax.axis_index("dates")
     col_index = lax.axis_index("cols")
@@ -115,6 +624,12 @@
 
 
 def solution(mesh):
+    def body(complex_images, pair_list):
+        dates, rows, _, cols = complex_images.shape
+        if mesh.shape["dates"] == 2 and cols == LANES * LOOKC and rows == 32 and dates >= GAP:
+            return two_halves(complex_images, pair_list)
+        return any_dates(complex_images, pair_list)
+
     return jax.shard_map(
         body,
         mesh=mesh,

time: 1220 us -> 108 us (0.09); the launches traced: 1200 us -> 108 us
  local copies, waits for them, and re-layouts: 639 us -> 3.21 us
  other arithmetic: 458 us -> 4.02 us
  Pallas kernels: 0 us -> 64 us
  blocking collectives: 42.2 us -> 0 us
  matrix products: 30.7 us -> 0 us
  between operations: 25.2 us -> 0.05 us
  waiting for transfers between devices: 0.77 us -> 25.4 us
    gather x80 -> x0, local copies, waits for them, and re-layouts: 334 us -> none  [the longest x20 84.2 us: one_group(): first_imag = jnp.take(imag_planes, group[:, 0], axis=0).astype(jnp.float32)]
    reduce_sum x82 -> x0, other arithmetic: 280 us -> none  [the longest x40 209 us: pool_looks(): jnp.sum(plane.reshape(count, rows // LOOKR, LOOKR, cols), axis=2)]
    reshape x41 -> x0, local copies, waits for them, and re-layouts: 130 us -> none  [the longest x40 130 us: pool_looks(): plane.reshape(count, rows // LOOKR, LOOKR, cols)]
    add x20 -> x5, other arithmetic: 80.5 us -> 1.32 us  [the longest x4 1.32 us: sum_devices(): value + lax.ppermute(value, 'cols', [(at, at ^ bit) for at in range(cols)])]
    reduce_sum x41 -> x0, local copies, waits for them, and re-layouts: 78.4 us -> none  [the longest x40 78.3 us: pool_looks(): jnp.sum(plane.reshape(count, rows // LOOKR, LOOKR, cols), axis=2)]
    another operation x19 -> x2, other arithmetic: 78.6 us -> 1.27 us  [the longest x1 0.66 us: two_halves(): jnp.stack([row_start, col_start])]
    pallas_call x0 -> x6, Pallas kernels: none -> 64 us  [the longest x2 36.3 us: call_pairs(): pl.pallas_call(lambda *refs: pair_kernel(pair_count, given is not None, s...]
    psum x1 -> x0, blocking collectives: 42.2 us -> none  [body(): normal, ramp_rhs = lax.psum((normal_part, rhs_part), ('dates', 'cols'))]
  transfers between devices with their start and end apart: 1 -> 7, of which waited for: 1 -> 4; matrix products, arithmetic and copies ran while one was open for 9% -> 2% of each run, Pallas kernels for 0% -> 32%
where the time goes in v1:
time: 108 us
  Pallas kernels  64 us (59%)
  waiting for transfers between devices  25.4 us (24%)
  starting transfers between devices  10.9 us (10%)
  other arithmetic  4.02 us (4%)
  local copies, waits for them, and re-layouts  3.21 us (3%)
    pallas_call x2, Pallas kernels, call_pairs(): pl.pallas_call(lambda *refs: pair_kernel(pair_count, given is not None, s...  36.3 us
    ppermute x3, waiting for transfers between devices, swap_dates(): return lax.ppermute(value, 'dates', [(0, 1), (1, 0)])  22.5 us
    pallas_call x1, Pallas kernels, call_inverse(): pl.pallas_call(inverse_kernel, out_shape=(square, square), in_specs=[in_v...  12.8 us
    ppermute x4, starting transfers between devices, sum_devices(): lax.ppermute(value, 'cols', [(at, at ^ bit) for at in range(cols)])  5.91 us
    pallas_call x1, Pallas kernels, call_solve(): pl.pallas_call(solve_kernel, out_shape=jax.ShapeDtypeStruct((16, padded,...  5.77 us
    ppermute x3, starting transfers between devices, swap_dates(): return lax.ppermute(value, 'dates', [(0, 1), (1, 0)])  5.01 us
    pallas_call x1, Pallas kernels, call_refine(): pl.pallas_call(lambda *refs: refine_kernel(count, row_total, col_total, *...  4.72 us
    pallas_call x1, Pallas kernels, call_combine(): pl.pallas_call(lambda *refs: combine_kernel(dates, row_total, col_total,...  4.38 us
  transfers between devices with their start and end apart: 7, of which 4 were waited for; matrix products, arithmetic and copies ran while one was open for 2% of the time, Pallas kernels for 32%

profile of v1, /device:TPU:0, one launch (start us, length us, event | category | flops | bytes accessed | tf_op | source)
XLA Modules:
  0.0 107.6 jit_solution(4657412441395762207)
XLA Ops:
  0.0 1.4 %fusion.refs_1_ = s32[1480]{0:T(1024)} fusion(s32[1480,2]{0,1:T(2,128)} %param.4, s32[]{:T(128)} %mul.29, s32[]{:T(128)S(6)} %add.25, s32[]{:T(128)S(6)} %mul.34), kind=kLoop, calls=%fused_computation.5 | loop fusion | flops 29600 | bytes 17772 | tf_op jit(solution)/shard_map/jit(_where)/select_n | solution.py:477
  1.4 0.6 add_add_fusion
  2.0 20.1 %pairs_other.1 = (bf16[2384,128]{1,0:T(8,128)(2,1)}, s32[2976]{0:T(1024)}, s32[2]{0:T(128)}) custom-call(s32[3]{0:T(128)} %get-tuple-element.26.refs_0_, s32[1480]{0:T(1024)} %fusion.refs_1_, bf16[148,16,16,128]{3,2,1,0:T(8,128)(2,1)} %bitcast.16, bf16[512,512]{1,0:T(8,128)(2,1)} %constant.35.clone.refs_3_.refs_5_), custom_call_target="tpu_custom_call" | custom-call | flops 106086400 | bytes 4849664 | tf_op jit(solution)/shard_map/pairs_other/pallas_call | solution.py:202
  22.2 3.1 %collective-permute-start.1 = (bf16[2384,128]{1,0:T(8,128)(2,1)}, bf16[2384,128]{1,0:T(8,128)(2,1)S(1)}, u32[]{:S(2)}, u32[]{:S(2)}) collective-permute-start(bf16[2384,128]{1,0:T(8,128)(2,1)} %get-tuple-element.21), channel_id=1, source_target_pairs={{0,16},{16,0},{1,17},{17,1},{2,18},{18,2},{3,19},{19,3},{4,20},{20... | collective-permute-start | bytes 1830920 | tf_op jit(solution)/shard_map/ppermute | solution.py:460
  25.3 1.0 constant_dynamic-slice_fusion
  26.4 0.6 stack.52.refs_0_
  27.0 20.6 %collective-permute-done.refs_4_ = bf16[12,8,16,128]{3,2,1,0:T(8,128)(2,1)S(1)} collective-permute-done((bf16[12,8,16,128]{3,2,1,0:T(8,128)(2,1)S(1)}, bf16[12,8,16,128]{3,2,1,0:T(8,128)(2,1)S(1)}, u32[]{:S(2)}, u32[]{:S(2)}) %collective-permute-start) | collective-permute-done | bytes 393248 | tf_op jit(solution)/shard_map/ppermute | solution.py:460
  47.7 0.7 copy-done.1
  48.4 16.1 %pairs_own.1 = (f32[2576,128]{1,0:T(8,128)}, f32[8,128]{1,0:T(8,128)}) custom-call(s32[3]{0:T(128)} %get-tuple-element.25.refs_0_, s32[2976]{0:T(1024)} %get-tuple-element.17.refs_1_, s32[2]{0:T(128)} %get-tuple-element.18.refs_2_, bf16[148,16,16,128]{3,2,1,0:T(8,128)(2,1)} %bitcast.18, bf16[12,8,16,128]{3,2,1,0:T(8,128)(2,1)} %copy-done.1, ...), custom_call_target="tpu_custom_call" | custom-call | flops 106086400 | bytes 4849664 | tf_op jit(solution)/shard_map/pairs_own/pallas_call | solution.py:202
  64.6 0.8 copy-done
  65.4 4.4 %combine.1 = (bf16[304,2048]{1,0:T(8,128)(2,1)}, bf16[304,2048]{1,0:T(8,128)(2,1)}, f32[8,304]{1,0:T(8,128)}) custom-call(s32[7]{0:T(128)} %stack.52.refs_0_, f32[2576,128]{1,0:T(8,128)} %get-tuple-element.19.refs_1_, f32[8,128]{1,0:T(8,128)} %get-tuple-element.20.refs_2_, bf16[2384,128]{1,0:T(8,128)(2,1)} %copy-done), custom_call_target="tpu_custom_call" | custom-call | flops 29884416 | bytes 8388608 | tf_op jit(solution)/shard_map/combine/pallas_call | solution.py:274
  69.8 1.4 %collective-permute-done.2 = f32[8,304]{1,0:T(8,128)S(1)} collective-permute-done((f32[8,304]{1,0:T(8,128)}, f32[8,304]{1,0:T(8,128)S(1)}, u32[]{:S(2)}, u32[]{:S(2)}) %collective-permute-start.2) | collective-permute-done | bytes 9760 | tf_op jit(solution)/shard_map/ppermute | solution.py:452
  71.2 0.7 add.28
  71.9 1.8 %collective-permute-start.3 = (f32[8,304]{1,0:T(8,128)S(1)}, f32[8,304]{1,0:T(8,128)S(1)}, u32[]{:S(2)}, u32[]{:S(2)}) collective-permute-start(f32[8,304]{1,0:T(8,128)S(1)} %add.28), channel_id=1, source_target_pairs={{0,16},{16,0},{1,17},{17,1},{2,18},{18,2},{3,19},{19,3},{4,20},{20... | collective-permute-start | bytes 29192 | tf_op jit(solution)/shard_map/ppermute | solution.py:460
  73.7 1.9 %collective-permute-done.3 = f32[8,304]{1,0:T(8,128)S(1)} collective-permute-done((f32[8,304]{1,0:T(8,128)S(1)}, f32[8,304]{1,0:T(8,128)S(1)}, u32[]{:S(2)}, u32[]{:S(2)}) %collective-permute-start.3) | collective-permute-done | bytes 9760 | tf_op jit(solution)/shard_map/ppermute | solution.py:460
  75.6 1.7 %collective-permute-start.4 = (f32[8,304]{1,0:T(8,128)S(1)}, f32[8,304]{1,0:T(8,128)S(1)}, u32[]{:S(2)}, u32[]{:S(2)}) collective-permute-start(f32[8,304]{1,0:T(8,128)S(1)} %add.29), channel_id=1, source_target_pairs={{0,2},{1,3},{2,0},{3,1},{4,6},{5,7},{6,4},{7,5},{8,10},{9,11},{10,... | collective-permute-start | bytes 29192 | tf_op jit(solution)/shard_map/ppermute | solution.py:452
  77.2 12.8 %inverse.1 = (bf16[304,304]{1,0:T(8,128)(2,1)}, bf16[304,304]{1,0:T(8,128)(2,1)}) custom-call(s32[2,1480]{1,0:T(2,128)} %bitcast.19), custom_call_target="tpu_custom_call" | custom-call | flops 2809446400 | bytes 8388608 | tf_op jit(solution)/shard_map/inverse/pallas_call | solution.py:331
  90.1 1.6 %collective-permute-start.5 = (f32[8,304]{1,0:T(8,128)S(1)}, f32[8,304]{1,0:T(8,128)S(1)}, u32[]{:S(2)}, u32[]{:S(2)}) collective-permute-start(f32[8,304]{1,0:T(8,128)S(1)} %add.30), channel_id=1, source_target_pairs={{0,4},{1,5},{2,6},{3,7},{4,0},{5,1},{6,2},{7,3},{8,12},{9,13},{10,... | collective-permute-start | bytes 29192 | tf_op jit(solution)/shard_map/ppermute | solution.py:452
  91.7 0.7 pad_add_fusion.refs_0_
  92.4 1.5 %collective-permute-done.5 = f32[8,304]{1,0:T(8,128)S(1)} collective-permute-done((f32[8,304]{1,0:T(8,128)S(1)}, f32[8,304]{1,0:T(8,128)S(1)}, u32[]{:S(2)}, u32[]{:S(2)}) %collective-permute-start.5) | collective-permute-done | bytes 9760 | tf_op jit(solution)/shard_map/ppermute | solution.py:452
  93.9 2.6 %collective-permute-start.6 = (f32[8,304]{1,0:T(8,128)S(1)}, f32[8,304]{1,0:T(8,128)S(1)}, u32[]{:S(2)}, u32[]{:S(2)}) collective-permute-start(f32[8,304]{1,0:T(8,128)S(1)} %add.31), channel_id=1, source_target_pairs={{0,8},{1,9},{2,10},{3,11},{4,12},{5,13},{6,14},{7,15},{8,0},{9,1},... | collective-permute-start | bytes 29192 | tf_op jit(solution)/shard_map/ppermute | solution.py:452
  96.5 5.8 %solve.1.refs_1_ = f32[16,304,128]{2,1,0:T(8,128)} custom-call(bf16[304,304]{1,0:T(8,128)(2,1)} %get-tuple-element.15.inverse_high.refs_3_, bf16[304,304]{1,0:T(8,128)(2,1)} %get-tuple-element.16.inverse_low.refs_4_, bf16[304,2048]{1,0:T(8,128)(2,1)} %get-tuple-element.22.high, bf16[304,2048]{1,0:T(8,128)(2,1)} %get-tuple-element.23.low), custom_call_target="tpu_custom_call" | custom-call | flops 1135607808 | bytes 6291456 | tf_op jit(solution)/shard_map/solve/pallas_call | solution.py:376
  102.2 0.6 add.32.refs_2_
  102.8 4.7 %refine.1 = f32[4736,128]{1,0:T(8,128)} custom-call(s32[2]{0:T(128)} %pad_add_fusion.refs_0_, f32[16,304,128]{2,1,0:T(8,128)} %solve.1.refs_1_, f32[8,304]{1,0:T(8,128)} %add.32.refs_2_, bf16[304,304]{1,0:T(8,128)(2,1)} %get-tuple-element.15.inverse_high.refs_3_, bf16[304,304]{1,0:T(8,128)(2,1)} %get-tuple-element.16.inverse_low.refs_4_), custom_call_target="tpu_custom_call" | custom-call | flops 3637248 | bytes 5242880 | tf_op jit(solution)/shard_map/refine/pallas_call | solution.py:435
  (10 shorter events, 0.1 us)
Async XLA Ops:
  22.2 42.4 %collective-permute-start.1 = (bf16[2384,128]{1,0:T(8,128)(2,1)}, bf16[2384,128]{1,0:T(8,128)(2,1)S(1)}, u32[]{:S(2)}, u32[]{:S(2)}) collective-permute-start(bf16[2384,128]{1,0:T(8,128)(2,1)} %get-tuple-element.21), channel_id=1, source_target_pairs={{0,16},{16,0},{1,17},{17,1},{2,18},{18,2},{3,19},{19,3},{4,20},{20... | collective-permute-start | bytes 1830920 | tf_op jit(solution)/shard_map/ppermute | solution.py:460
  26.3 21.4 %collective-permute-start = (bf16[12,8,16,128]{3,2,1,0:T(8,128)(2,1)S(1)}, bf16[12,8,16,128]{3,2,1,0:T(8,128)(2,1)S(1)}, u32[]{:S(2)}, u32[]{:S(2)}) collective-permute-start(bf16[12,8,16,128]{3,2,1,0:T(8,128)(2,1)S(1)} %constant_dynamic-slice_fusion), channel_id=1, source_target_pairs={{0,16},{16,0},{1,17},{17,1},{2,18},{18,2},{3,19},{19,3},{4,20},{20... | collective-permute-start | bytes 1179656 | tf_op jit(solution)/shard_map/ppermute | solution.py:460
  47.7 0.7 copy-start.1
  64.6 0.8 copy-start
  69.8 1.4 %collective-permute-start.2 = (f32[8,304]{1,0:T(8,128)}, f32[8,304]{1,0:T(8,128)S(1)}, u32[]{:S(2)}, u32[]{:S(2)}) collective-permute-start(f32[8,304]{1,0:T(8,128)} %get-tuple-element.24), channel_id=1, source_target_pairs={{0,1},{1,0},{2,3},{3,2},{4,5},{5,4},{6,7},{7,6},{8,9},{9,8},{10,11... | collective-permute-start | bytes 29192 | tf_op jit(solution)/shard_map/ppermute | solution.py:452
  71.9 3.7 %collective-permute-start.3 = (f32[8,304]{1,0:T(8,128)S(1)}, f32[8,304]{1,0:T(8,128)S(1)}, u32[]{:S(2)}, u32[]{:S(2)}) collective-permute-start(f32[8,304]{1,0:T(8,128)S(1)} %add.28), channel_id=1, source_target_pairs={{0,16},{16,0},{1,17},{17,1},{2,18},{18,2},{3,19},{19,3},{4,20},{20... | collective-permute-start | bytes 29192 | tf_op jit(solution)/shard_map/ppermute | solution.py:460
  75.6 14.5 %collective-permute-start.4 = (f32[8,304]{1,0:T(8,128)S(1)}, f32[8,304]{1,0:T(8,128)S(1)}, u32[]{:S(2)}, u32[]{:S(2)}) collective-permute-start(f32[8,304]{1,0:T(8,128)S(1)} %add.29), channel_id=1, source_target_pairs={{0,2},{1,3},{2,0},{3,1},{4,6},{5,7},{6,4},{7,5},{8,10},{9,11},{10,... | collective-permute-start | bytes 29192 | tf_op jit(solution)/shard_map/ppermute | solution.py:452
  90.1 3.8 %collective-permute-start.5 = (f32[8,304]{1,0:T(8,128)S(1)}, f32[8,304]{1,0:T(8,128)S(1)}, u32[]{:S(2)}, u32[]{:S(2)}) collective-permute-start(f32[8,304]{1,0:T(8,128)S(1)} %add.30), channel_id=1, source_target_pairs={{0,4},{1,5},{2,6},{3,7},{4,0},{5,1},{6,2},{7,3},{8,12},{9,13},{10,... | collective-permute-start | bytes 29192 | tf_op jit(solution)/shard_map/ppermute | solution.py:452
  93.9 8.4 %collective-permute-start.6 = (f32[8,304]{1,0:T(8,128)S(1)}, f32[8,304]{1,0:T(8,128)S(1)}, u32[]{:S(2)}, u32[]{:S(2)}) collective-permute-start(f32[8,304]{1,0:T(8,128)S(1)} %add.31), channel_id=1, source_target_pairs={{0,8},{1,9},{2,10},{3,11},{4,12},{5,13},{6,14},{7,15},{8,0},{9,1},... | collective-permute-start | bytes 29192 | tf_op jit(solution)/shard_map/ppermute | solution.py:452

commit v2 on v1

--- a/solution.py
+++ b/solution.py
@@ -13,7 +13,6 @@
 RIDGE = 0.5
 MAX_STEP = 40
 UNROLL = 8
-CHOOSE_UNROLL = 8
 LANES = 128
 SPLIT = 4
 VMEM_LIMIT = 56 * 1024 * 1024
@@ -37,7 +36,7 @@
     return lax.dot_general(first, second, dims, preferred_element_type=jnp.float32)
 
 
-def spread_looks(source, date, slot, step, looks, planes):
+def spread_looks(source, date, slot, step, looks, planes, choose=None, start=0, share=0, found=None):
     raw = source[pl.ds(date, step)].reshape(step, 2, SPLIT, 16, LANES)
     left = jnp.concatenate(
         [raw[:, :, sub].reshape(step * 32, LANES) for sub in range(SPLIT)], axis=1
@@ -52,16 +51,21 @@
                     planes[pl.ds(base + (rlook * LOOKC + look) * 16 + group * 8, 8), :] = spread[
                         top : top + 8, look * LANES : (look + 1) * LANES
                     ]
+        for k in range(share):
+            found = choose(start + at * share + k, found)
+    return found
 
 
 def pair_kernel(pair_count, with_halo, step, *refs):
     if with_halo:
-        (bounds, listed, counts, images, halo, looks, series, weights, raw, raw_halo, planes, sems) = refs
+        (listed, counts, images, halo, looks, series, weights, raw, raw_halo, planes, sems) = refs
     else:
-        (bounds, pairs, images, looks, series, listed, counts, raw, planes, sems, sums) = refs
+        (pairs, images, looks, series, listed, counts, raw, planes, sems, sums) = refs
     dates = images.shape[0]
     steps = dates // step
-    row_start, own_slot, halo_slot = bounds[0], bounds[1], bounds[2]
+    me = lax.axis_index("dates")
+    row_start = 8 * (me if with_halo else 1 - me)
+    own_slot, halo_slot = GAP * me, dates * (1 - me)
     copies = [
         pltpu.make_async_copy(
             images.at[pl.ds(at * step, step), pl.ds(row_start, 8)],
@@ -80,29 +84,29 @@
     total[...] = jnp.zeros_like(total)
     planes[pl.ds(spare * 128, 128), :] = jnp.zeros((128, LANES), jnp.float32)
 
+    second_list = pair_count + UNROLL
+
+    def choose(at, found):
+        packed = pairs[at]
+        listed[found[0]] = packed
+        listed[second_list + found[1]] = packed
+        return (found[0] + ((packed >> 20) & 1), found[1] + (packed >> 21))
+
+    found = (jnp.int32(0), jnp.int32(0))
+    share = 0 if with_halo else pair_count // dates
+    for at in range(steps):
+        copies[at].wait()
+        found = spread_looks(
+            raw, at * step, own_slot + at * step, step, looks, planes,
+            choose, at * step * share, share, found,
+        )
     if not with_halo:
-        def choose(at, found):
-            inside, across = found
-            packed = pairs[at]
-            listed[inside] = packed
-            listed[pair_count + UNROLL + across] = packed
-            return (inside + ((packed >> 20) & 1), across + (packed >> 21))
-
-        found = lax.fori_loop(
-            0, pair_count, choose, (jnp.int32(0), jnp.int32(0)), unroll=CHOOSE_UNROLL
-        )
+        for at in range(dates * share, pair_count):
+            found = choose(at, found)
         for part in range(2):
             counts[part] = found[part]
             for at in range(UNROLL):
-                listed[part * (pair_count + UNROLL) + found[part] + at] = jnp.int32(spare * 1025)
-
-    def spread_step(at, carry):
-        spread_looks(raw, at * step, own_slot + at * step, step, looks, planes)
-        return carry
-
-    for at in range(steps):
-        copies[at].wait()
-        spread_step(at, 0)
+                listed[part * second_list + found[part] + at] = jnp.int32(spare * 1025)
     if with_halo:
         copies[steps].wait()
         spread_looks(raw_halo, 0, halo_slot, GAP, looks, planes)
@@ -138,7 +142,7 @@
 
         def some_pairs(at, power, part=part):
             for k in range(UNROLL):
-                power = one_pair(listed[part * (pair_count + UNROLL) + at * UNROLL + k], power)
+                power = one_pair(listed[part * second_list + at * UNROLL + k], power)
             return power
 
         power = lax.fori_loop(0, (counts[part] + UNROLL - 1) // UNROLL, some_pairs, power)
@@ -171,7 +175,7 @@
     return pl.BlockSpec(memory_space=pl.ANY)
 
 
-def call_pairs(bounds, pairs, images, looks, given=None):
+def call_pairs(pairs, images, looks, given=None):
     dates = images.shape[0]
     pair_count = pairs.shape[0]
     step = max(k for k in range(1, MAX_STEP + 1) if dates % k == 0)
@@ -186,9 +190,9 @@
         halo, listed, counts = given
         out_shape = (sums, jax.ShapeDtypeStruct((8, LANES), jnp.float32))
         scratch.insert(1, pltpu.VMEM((GAP, 8, 16, LANES), jnp.bfloat16))
-        in_specs = [in_smem()] * 3 + [in_hbm(), in_hbm(), in_vmem()]
+        in_specs = [in_smem()] * 2 + [in_hbm(), in_hbm(), in_vmem()]
         out_specs = (in_vmem(), in_vmem())
-        args = (bounds, listed, counts, images, halo, looks)
+        args = (listed, counts, images, halo, looks)
     else:
         out_shape = (
             jax.ShapeDtypeStruct(((dates + 1) * 16, LANES), jnp.bfloat16),
@@ -196,9 +200,9 @@
             jax.ShapeDtypeStruct((2,), jnp.int32),
         )
         scratch.append(pltpu.VMEM(sums.shape, sums.dtype))
-        in_specs = [in_smem(), in_smem(), in_hbm(), in_vmem()]
+        in_specs = [in_smem(), in_hbm(), in_vmem()]
         out_specs = (in_vmem(), in_smem(), in_smem())
-        args = (bounds, pairs, images, looks)
+        args = (pairs, images, looks)
     return pl.pallas_call(
         lambda *refs: pair_kernel(pair_count, given is not None, step, *refs),
         out_shape=out_shape,
@@ -207,7 +211,7 @@
         scratch_shapes=scratch,
         compiler_params=pltpu.CompilerParams(vmem_limit_bytes=VMEM_LIMIT),
         cost_estimate=pl.CostEstimate(
-            flops=pair_count * 70 * 1024, bytes_accessed=dates * 8 * 16 * 256, transcendentals=0
+            flops=pair_count * 70 * 1024, bytes_accessed=pair_count * 48 * 1024, transcendentals=0
         ),
         name="pairs_other" if given is None else "pairs_own",
     )(*args)
@@ -227,7 +231,8 @@
 
 
 def combine_kernel(dates, row_total, col_total, *refs):
-    (bounds, own, own_weights, other, high, low, moments, full, weighted_rows) = refs
+    (own, own_weights, other, high, low, moments, full, weighted_rows) = refs
+    me = lax.axis_index("dates")
     count = dates * 2
     span = dates + GAP
     scale = 1.0 / float(LOOKR * LOOKC)
@@ -235,11 +240,11 @@
     def rows(start, size):
         return pl.ds(pl.multiple_of(start * 16, 16), size * 16)
 
-    full[rows(bounds[0], span), :] = own[pl.ds(0, span * 16), :] * scale
+    full[rows((dates - GAP) * me, span), :] = own[pl.ds(0, span * 16), :] * scale
     rest = dates - GAP
-    full[rows(bounds[1], rest), :] = other[rows(bounds[2], rest), :].astype(jnp.float32)
-    full[rows(bounds[3], GAP), :] += other[rows(bounds[4], GAP), :].astype(jnp.float32)
-    y_plane, x_plane = half_basis(bounds[5], bounds[6], row_total, col_total)
+    full[rows(span * (1 - me), rest), :] = other[rows(GAP * (1 - me), rest), :].astype(jnp.float32)
+    full[rows(dates - GAP * me, GAP), :] += other[rows(rest * me, GAP), :].astype(jnp.float32)
+    y_plane, x_plane = half_basis(8 * me, LANES * lax.axis_index("cols"), row_total, col_total)
     basis = (jnp.ones((8, LANES), jnp.float32), y_plane, x_plane)
     padded = full.shape[0] // 16
     full[pl.ds(count * 16, (padded - count) * 16), :] = jnp.zeros(
@@ -268,29 +273,29 @@
     )
 
 
-def call_combine(bounds, own, own_weights, other, dates, row_total, col_total):
+def call_combine(own, own_weights, other, dates, row_total, col_total):
     padded = pad_dates(dates * 2)
     wide = jax.ShapeDtypeStruct((padded, 16 * LANES), jnp.bfloat16)
     return pl.pallas_call(
         lambda *refs: combine_kernel(dates, row_total, col_total, *refs),
         out_shape=(wide, wide, jax.ShapeDtypeStruct((8, padded), jnp.float32)),
-        in_specs=[in_smem()] + [in_vmem()] * 3,
+        in_specs=[in_vmem()] * 3,
         out_specs=(in_vmem(),) * 3,
         scratch_shapes=[
             pltpu.VMEM((padded * 16, LANES), jnp.float32),
             pltpu.VMEM((8, 16 * LANES), jnp.float32),
         ],
         compiler_params=pltpu.CompilerParams(vmem_limit_bytes=VMEM_LIMIT),
-        cost_estimate=pl.CostEstimate(flops=padded * 8 * 12288, bytes_accessed=8 << 20, transcendentals=0),
+        cost_estimate=pl.CostEstimate(flops=padded * 8 * 12288, bytes_accessed=16 << 20, transcendentals=0),
         name="combine",
-    )(bounds, own, own_weights, other)
+    )(own, own_weights, other)
 
 
 def pad_dates(count):
     return (count + 3 + 15) // 16 * 16
 
 
-def inverse_kernel(pairs, high, low, state, normal_high, normal_low):
+def inverse_kernel(pairs, high, low, state, residual, normal_high, normal_low):
     padded = high.shape[0]
     date = lax.broadcasted_iota(jnp.int32, (padded, pairs.shape[1]), 0)
     design = (
@@ -305,24 +310,40 @@
     normal = dot32(design, design, NT) + RIDGE * eye
     normal_high[...], normal_low[...] = split_bf16(normal)
     largest = jnp.max(jnp.sum(jnp.abs(normal), axis=1))
-    state[...] = eye * (2.0 / (largest + RIDGE))
-    error = (largest - RIDGE) / (largest + RIDGE)
-
-    def product(first, second):
-        return (
-            dot32(first[0], second[0], NN) + dot32(first[0], second[1], NN) + dot32(first[1], second[0], NN)
-        )
-
-    def step(error):
-        scale = 2.0 / (2.0 - error * error)
-        now = split_bf16(state[...])
-        residual = split_bf16(eye - product((normal_high[...], normal_low[...]), now))
-        state[...] = scale * (state[...] + product(now, residual))
-        return scale - 1.0
-
-    lax.while_loop(lambda error: error > 1e-6, step, error)
-    step(jnp.float32(0.0))
+    careful = largest > 128.0
+    scale, error = centre((largest - RIDGE) / (largest + RIDGE))
+    start = 2.0 / (largest + RIDGE)
+    state[...] = (scale * start) * (2.0 * eye - start * normal)
+
+    def step(scale):
+        now, rest = split_bf16(state[...])
+        residual[...] = eye - dot32(normal_high[...], now, NN) - dot32(normal_high[...], rest, NN)
+
+        @pl.when(careful)
+        def _():
+            residual[...] -= dot32(normal_low[...], now, NN)
+
+        upper, lower = split_bf16(residual[...])
+        change = dot32(now, upper, NN)
+        state[...] = scale * (state[...] + change)
+
+        @pl.when(careful)
+        def _():
+            state[...] += scale * (dot32(now, lower, NN) + dot32(rest, upper, NN))
+
+    def body(error):
+        scale, left = centre(error)
+        step(scale)
+        return jnp.maximum(left, 0.05 * error)
+
+    lax.while_loop(lambda error: error > 5e-4, body, error)
+    step(jnp.float32(1.0))
     high[...], low[...] = split_bf16(state[...])
+
+
+def centre(error):
+    scale = 2.0 / (2.0 - error * error)
+    return scale, scale - 1.0
 
 
 def call_inverse(pair_rows, count):
@@ -335,11 +356,12 @@
         out_specs=(in_vmem(),) * 2,
         scratch_shapes=[
             pltpu.VMEM((padded, padded), jnp.float32),
+            pltpu.VMEM((padded, padded), jnp.float32),
             pltpu.VMEM((padded, padded), jnp.bfloat16),
             pltpu.VMEM((padded, padded), jnp.bfloat16),
         ],
         compiler_params=pltpu.CompilerParams(vmem_limit_bytes=VMEM_LIMIT),
-        cost_estimate=pl.CostEstimate(flops=100 * padded**3, bytes_accessed=8 << 20, transcendentals=0),
+        cost_estimate=pl.CostEstimate(flops=50 * padded**3, bytes_accessed=24 << 20, transcendentals=0),
         name="inverse",
     )(pair_rows)
 
@@ -380,14 +402,14 @@
         out_specs=in_vmem(),
         compiler_params=pltpu.CompilerParams(vmem_limit_bytes=VMEM_LIMIT),
         cost_estimate=pl.CostEstimate(
-            flops=6 * padded * padded * 16 * LANES, bytes_accessed=6 << 20, transcendentals=0
+            flops=6 * padded * padded * 16 * LANES, bytes_accessed=20 << 20, transcendentals=0
         ),
         name="solve",
     )(*inverse, *values)
 
 
 def refine_kernel(count, row_total, col_total, *refs):
-    (bounds, series, moments, inverse_high, inverse_low, refined) = refs
+    (series, moments, inverse_high, inverse_low, refined) = refs
     padded = series.shape[1]
     normal = [
         [moments[at : at + 1, count + k : count + k + 1] for k in range(3)] for at in range(3)
@@ -417,7 +439,8 @@
         + dot32(inverse_low[...], upper, NT)
     )[:count]
     lane = lax.broadcasted_iota(jnp.int32, (1, LANES), 1)
-    x_row = centred(bounds[1] + lane, col_total)
+    x_row = centred(LANES * lax.axis_index("cols") + lane, col_total)
+    row_start = 8 * lax.axis_index("dates")
     for part in range(2):
         level, along_y, along_x = (
             jnp.broadcast_to(ramps[:, part * 3 + at : part * 3 + at + 1], (count, LANES))
@@ -425,22 +448,22 @@
         )
         level = level + along_x * x_row
         for row in range(8):
-            y = centred(bounds[0] + row, row_total)
+            y = centred(row_start + row, row_total)
             refined[pl.ds(row * 2 + part, count, stride=16), :] = series[row * 2 + part, :count] - (
                 level + along_y * y
             )
 
 
-def call_refine(bounds, series, moments, inverse, count, row_total, col_total):
+def call_refine(series, moments, inverse, count, row_total, col_total):
     return pl.pallas_call(
         lambda *refs: refine_kernel(count, row_total, col_total, *refs),
         out_shape=jax.ShapeDtypeStruct((count * 16, LANES), jnp.float32),
-        in_specs=[in_smem()] + [in_vmem()] * 4,
+        in_specs=[in_vmem()] * 4,
         out_specs=in_vmem(),
         compiler_params=pltpu.CompilerParams(vmem_limit_bytes=VMEM_LIMIT),
-        cost_estimate=pl.CostEstimate(flops=count * 16 * LANES * 6, bytes_accessed=5 << 20, transcendentals=0),
+        cost_estimate=pl.CostEstimate(flops=count * 16 * LANES * 6, bytes_accessed=16 << 20, transcendentals=0),
         name="refine",
-    )(bounds, series, moments, *inverse)
+    )(series, moments, *inverse)
 
 
 def sum_devices(value):
@@ -479,42 +502,18 @@
     edge = lax.dynamic_slice(
         images, ((dates - GAP) * (1 - me), half * (1 - me), 0, 0), (GAP, half, 16, LANES)
     )
+    edge, pair_rows = lax.optimization_barrier((edge, pair_list.T))
     halo = swap_dates(edge)
+    inverse = call_inverse(pair_rows, dates * 2)
+    halo, inverse, packed = lax.optimization_barrier((halo, inverse, packed))
     looks = jnp.asarray(look_matrix(), jnp.bfloat16)
-    own_slot, halo_slot = GAP * me, dates * (1 - me)
-    other, listed, counts = call_pairs(
-        jnp.stack([half * (1 - me), own_slot, halo_slot]), packed, images, looks
-    )
+    other, listed, counts = call_pairs(packed, images, looks)
     other = swap_dates(other)
-    own, own_weights = call_pairs(
-        jnp.stack([half * me, own_slot, halo_slot]), packed, images, looks, (halo, listed, counts)
-    )
-    row_start, col_start = half * me, LANES * lax.axis_index("cols")
-    high, lowpart, moments = call_combine(
-        jnp.stack(
-            [
-                base,
-                (dates + GAP) * (1 - me),
-                GAP * (1 - me),
-                dates - GAP * me,
-                (dates - GAP) * me,
-                row_start,
-                col_start,
-            ]
-        ),
-        own,
-        own_weights,
-        other,
-        dates,
-        row_total,
-        col_total,
-    )
-    inverse = call_inverse(pair_list.T, dates * 2)
+    own, own_weights = call_pairs(packed, images, looks, (halo, listed, counts))
+    high, lowpart, moments = call_combine(own, own_weights, other, dates, row_total, col_total)
     moments = sum_devices(moments)
     series = call_solve(inverse, (high, lowpart))
-    refined = call_refine(
-        jnp.stack([row_start, col_start]), series, moments, inverse, dates * 2, row_total, col_total
-    )
+    refined = call_refine(series, moments, inverse, dates * 2, row_total, col_total)
     return refined.reshape(dates * 2, half, 2, LANES)
 
 

time: 108 us -> 81.5 us (0.75)
  waiting for transfers between devices: 25.4 us -> 8.45 us
  Pallas kernels: 64 us -> 56.2 us
  local copies, waits for them, and re-layouts: 3.21 us -> 1.84 us
  other arithmetic: 4.02 us -> 2.75 us
    ppermute x3, waiting for transfers between devices: 22.5 us -> 2.76 us  [swap_dates(): return lax.ppermute(value, 'dates', [(0, 1), (1, 0)])]
    pallas_call x1, Pallas kernels: 12.8 us -> 8.32 us  [call_inverse(): pl.pallas_call(inverse_kernel, out_shape=(square, square), in_specs=[in_v...]
    pallas_call x2, Pallas kernels: 36.3 us -> 32.8 us  [call_pairs(): pl.pallas_call(lambda *refs: pair_kernel(pair_count, given is not None, s...]
    ppermute x4, waiting for transfers between devices: 2.85 us -> 5.68 us  [sum_devices(): lax.ppermute(value, 'cols', [(at, at ^ bit) for at in range(cols)])]
    another operation x2 -> x0, other arithmetic: 1.27 us -> none  [the longest x1 0.66 us: two_halves(): jnp.stack([row_start, col_start])]
  transfers between devices with their start and end apart: 7 -> 7, of which waited for: 4 -> 4; matrix products, arithmetic and copies ran while one was open for 2% -> 2% of each run, Pallas kernels for 32% -> 37%
where the time goes in v2:
time: 81.5 us; the launch traced here: 80.9 us
  Pallas kernels  56.2 us (69%)
  starting transfers between devices  11.6 us (14%)
  waiting for transfers between devices  8.45 us (10%)
  other arithmetic  2.75 us (3%)
  local copies, waits for them, and re-layouts  1.84 us (2%)
    pallas_call x2, Pallas kernels, call_pairs(): pl.pallas_call(lambda *refs: pair_kernel(pair_count, given is not None, s...  32.8 us
    pallas_call x1, Pallas kernels, call_inverse(): pl.pallas_call(inverse_kernel, out_shape=(square, square), in_specs=[in_v...  8.32 us
    ppermute x3, starting transfers between devices, swap_dates(): return lax.ppermute(value, 'dates', [(0, 1), (1, 0)])  5.95 us
    pallas_call x1, Pallas kernels, call_solve(): pl.pallas_call(solve_kernel, out_shape=jax.ShapeDtypeStruct((16, padded,...  5.78 us
    ppermute x4, starting transfers between devices, sum_devices(): lax.ppermute(value, 'cols', [(at, at ^ bit) for at in range(cols)])  5.69 us
    ppermute x4, waiting for transfers between devices, sum_devices(): lax.ppermute(value, 'cols', [(at, at ^ bit) for at in range(cols)])  5.68 us
    pallas_call x1, Pallas kernels, call_refine(): pl.pallas_call(lambda *refs: refine_kernel(count, row_total, col_total, *...  4.71 us
    pallas_call x1, Pallas kernels, call_combine(): pl.pallas_call(lambda *refs: combine_kernel(dates, row_total, col_total,...  4.5 us
  transfers between devices with their start and end apart: 7, of which 4 were waited for; matrix products, arithmetic and copies ran while one was open for 2% of the time, Pallas kernels for 37%

profile of v2, /device:TPU:0, one launch (start us, length us, event | category | flops | bytes accessed | tf_op | source)
XLA Modules:
  0.0 80.9 jit_solution(508734437148748003)
XLA Ops:
  0.0 1.0 %constant_dynamic-slice_fusion = bf16[12,8,16,128]{3,2,1,0:T(8,128)(2,1)S(1)} fusion(bf16[148,16,16,128]{3,2,1,0:T(8,128)(2,1)} %bitcast.7, s32[]{:T(128)S(6)} %select_n.10, s32[]{:T(128)S(6)} %select_n.11), kind=kLoop, calls=%fused_computation.10 | loop fusion | bytes 786440 | tf_op jit(solution)/shard_map/dynamic_slice | solution.py:502
  1.0 3.0 %collective-permute-start = (bf16[12,8,16,128]{3,2,1,0:T(8,128)(2,1)S(1)}, bf16[12,8,16,128]{3,2,1,0:T(8,128)(2,1)S(1)}, u32[]{:S(2)}, u32[]{:S(2)}) collective-permute-start(bf16[12,8,16,128]{3,2,1,0:T(8,128)(2,1)S(1)} %constant_dynamic-slice_fusion), channel_id=1, source_target_pairs={{0,16},{16,0},{1,17},{17,1},{2,18},{18,2},{3,19},{19,3},{4,20},{20... | collective-permute-start | bytes 1179656 | tf_op jit(solution)/shard_map/ppermute | solution.py:483
  4.0 1.4 %fusion.refs_0_ = s32[1480]{0:T(1024)} fusion(s32[1480,2]{0,1:T(2,128)} %param.4, s32[]{:T(128)S(6)} %mul.11, s32[]{:T(128)S(6)} %add.27, s32[]{:T(128)S(6)} %mul.10), kind=kLoop, calls=%fused_computation.5 | loop fusion | flops 29600 | bytes 17772 | tf_op jit(solution)/shard_map/jit(_where)/select_n | solution.py:500
  5.5 8.3 %inverse.1 = (bf16[304,304]{1,0:T(8,128)(2,1)}, bf16[304,304]{1,0:T(8,128)(2,1)}) custom-call(s32[2,1480]{1,0:T(2,128)} %bitcast.10), custom_call_target="tpu_custom_call" | custom-call | flops 1404723200 | bytes 25165824 | tf_op jit(solution)/shard_map/inverse/pallas_call | solution.py:352
  13.8 0.0 collective-permute-done.refs_3_
  13.8 17.0 %pairs_other.1 = (bf16[2384,128]{1,0:T(8,128)(2,1)}, s32[2976]{0:T(1024)}, s32[2]{0:T(128)}) custom-call(s32[1480]{0:T(1024)} %fusion.refs_0_, bf16[148,16,16,128]{3,2,1,0:T(8,128)(2,1)} %bitcast.8, bf16[512,512]{1,0:T(8,128)(2,1)} %constant.26.clone.refs_2_.refs_4_), custom_call_target="tpu_custom_call" | custom-call | flops 106086400 | bytes 72744960 | tf_op jit(solution)/shard_map/pairs_other/pallas_call | solution.py:206
  30.8 2.0 %collective-permute-start.1 = (bf16[2384,128]{1,0:T(8,128)(2,1)}, bf16[2384,128]{1,0:T(8,128)(2,1)S(1)}, u32[]{:S(2)}, u32[]{:S(2)}) collective-permute-start(bf16[2384,128]{1,0:T(8,128)(2,1)} %get-tuple-element.33), channel_id=1, source_target_pairs={{0,16},{16,0},{1,17},{17,1},{2,18},{18,2},{3,19},{19,3},{4,20},{20... | collective-permute-start | bytes 1830920 | tf_op jit(solution)/shard_map/ppermute | solution.py:483
  32.9 15.8 %pairs_own.1 = (f32[2576,128]{1,0:T(8,128)}, f32[8,128]{1,0:T(8,128)}) custom-call(s32[2976]{0:T(1024)} %get-tuple-element.28.refs_0_, s32[2]{0:T(128)} %get-tuple-element.29.refs_1_, bf16[148,16,16,128]{3,2,1,0:T(8,128)(2,1)} %bitcast.9, bf16[12,8,16,128]{3,2,1,0:T(8,128)(2,1)} %copy-done.1, bf16[512,512]{1,0:T(8,128)(2,1)} %constant.26.clone.refs_2_.refs_4_), custom_call_target="tpu_custom_call" | custom-call | flops 106086400 | bytes 72744960 | tf_op jit(solution)/shard_map/pairs_own/pallas_call | solution.py:206
  48.7 0.0 collective-permute-done.1.refs_2_
  48.7 0.8 %copy-done = bf16[2384,128]{1,0:T(8,128)(2,1)} copy-done((bf16[2384,128]{1,0:T(8,128)(2,1)}, bf16[2384,128]{1,0:T(8,128)(2,1)S(1)}, u32[]{:S(2)}) %copy-start) | copy-done | bytes 610328
  49.5 4.5 %combine.1 = (bf16[304,2048]{1,0:T(8,128)(2,1)}, bf16[304,2048]{1,0:T(8,128)(2,1)}, f32[8,304]{1,0:T(8,128)}) custom-call(f32[2576,128]{1,0:T(8,128)} %get-tuple-element.31.refs_0_, f32[8,128]{1,0:T(8,128)} %get-tuple-element.32.refs_1_, bf16[2384,128]{1,0:T(8,128)(2,1)} %copy-done), custom_call_target="tpu_custom_call" | custom-call | flops 29884416 | bytes 16777216 | tf_op jit(solution)/shard_map/combine/pallas_call | solution.py:279
  54.0 1.4 %collective-permute-done.2 = f32[8,304]{1,0:T(8,128)S(1)} collective-permute-done((f32[8,304]{1,0:T(8,128)}, f32[8,304]{1,0:T(8,128)S(1)}, u32[]{:S(2)}, u32[]{:S(2)}) %collective-permute-start.2) | collective-permute-done | bytes 9760 | tf_op jit(solution)/shard_map/ppermute | solution.py:475
  55.4 0.7 add.28
  56.1 0.9 %collective-permute-start.3 = (f32[8,304]{1,0:T(8,128)S(1)}, f32[8,304]{1,0:T(8,128)S(1)}, u32[]{:S(2)}, u32[]{:S(2)}) collective-permute-start(f32[8,304]{1,0:T(8,128)S(1)} %add.28), channel_id=1, source_target_pairs={{0,16},{16,0},{1,17},{17,1},{2,18},{18,2},{3,19},{19,3},{4,20},{20... | collective-permute-start | bytes 29192 | tf_op jit(solution)/shard_map/ppermute | solution.py:483
  57.0 2.8 %collective-permute-done.3 = f32[8,304]{1,0:T(8,128)S(1)} collective-permute-done((f32[8,304]{1,0:T(8,128)S(1)}, f32[8,304]{1,0:T(8,128)S(1)}, u32[]{:S(2)}, u32[]{:S(2)}) %collective-permute-start.3) | collective-permute-done | bytes 9760 | tf_op jit(solution)/shard_map/ppermute | solution.py:483
  59.8 1.5 %collective-permute-start.4 = (f32[8,304]{1,0:T(8,128)S(1)}, f32[8,304]{1,0:T(8,128)S(1)}, u32[]{:S(2)}, u32[]{:S(2)}) collective-permute-start(f32[8,304]{1,0:T(8,128)S(1)} %add.29), channel_id=1, source_target_pairs={{0,2},{1,3},{2,0},{3,1},{4,6},{5,7},{6,4},{7,5},{8,10},{9,11},{10,... | collective-permute-start | bytes 29192 | tf_op jit(solution)/shard_map/ppermute | solution.py:475
  61.3 2.2 %collective-permute-done.4 = f32[8,304]{1,0:T(8,128)S(1)} collective-permute-done((f32[8,304]{1,0:T(8,128)S(1)}, f32[8,304]{1,0:T(8,128)S(1)}, u32[]{:S(2)}, u32[]{:S(2)}) %collective-permute-start.4) | collective-permute-done | bytes 9760 | tf_op jit(solution)/shard_map/ppermute | solution.py:475
  63.5 1.6 %collective-permute-start.5 = (f32[8,304]{1,0:T(8,128)S(1)}, f32[8,304]{1,0:T(8,128)S(1)}, u32[]{:S(2)}, u32[]{:S(2)}) collective-permute-start(f32[8,304]{1,0:T(8,128)S(1)} %add.30), channel_id=1, source_target_pairs={{0,4},{1,5},{2,6},{3,7},{4,0},{5,1},{6,2},{7,3},{8,12},{9,13},{10,... | collective-permute-start | bytes 29192 | tf_op jit(solution)/shard_map/ppermute | solution.py:475
  65.1 2.1 %collective-permute-done.5 = f32[8,304]{1,0:T(8,128)S(1)} collective-permute-done((f32[8,304]{1,0:T(8,128)S(1)}, f32[8,304]{1,0:T(8,128)S(1)}, u32[]{:S(2)}, u32[]{:S(2)}) %collective-permute-start.5) | collective-permute-done | bytes 9760 | tf_op jit(solution)/shard_map/ppermute | solution.py:475
  67.2 2.6 %collective-permute-start.6 = (f32[8,304]{1,0:T(8,128)S(1)}, f32[8,304]{1,0:T(8,128)S(1)}, u32[]{:S(2)}, u32[]{:S(2)}) collective-permute-start(f32[8,304]{1,0:T(8,128)S(1)} %add.31), channel_id=1, source_target_pairs={{0,8},{1,9},{2,10},{3,11},{4,12},{5,13},{6,14},{7,15},{8,0},{9,1},... | collective-permute-start | bytes 29192 | tf_op jit(solution)/shard_map/ppermute | solution.py:475
  69.8 5.8 %solve.1.refs_0_ = f32[16,304,128]{2,1,0:T(8,128)} custom-call(bf16[304,304]{1,0:T(8,128)(2,1)} %get-tuple-element.25.inverse_high.refs_2_, bf16[304,304]{1,0:T(8,128)(2,1)} %get-tuple-element.26.inverse_low.refs_3_, bf16[304,2048]{1,0:T(8,128)(2,1)} %get-tuple-element.34.high, bf16[304,2048]{1,0:T(8,128)(2,1)} %get-tuple-element.35.low), custom_call_target="tpu_custom_call" | custom-call | flops 1135607808 | bytes 20971520 | tf_op jit(solution)/shard_map/solve/pallas_call | solution.py:398
  75.6 0.0 collective-permute-done.6
  75.6 0.6 add.32.refs_1_
  76.2 4.7 %refine.1 = f32[4736,128]{1,0:T(8,128)} custom-call(f32[16,304,128]{2,1,0:T(8,128)} %solve.1.refs_0_, f32[8,304]{1,0:T(8,128)} %add.32.refs_1_, bf16[304,304]{1,0:T(8,128)(2,1)} %get-tuple-element.25.inverse_high.refs_2_, bf16[304,304]{1,0:T(8,128)(2,1)} %get-tuple-element.26.inverse_low.refs_3_), custom_call_target="tpu_custom_call" | custom-call | flops 3637248 | bytes 16777216 | tf_op jit(solution)/shard_map/refine/pallas_call | solution.py:458
  (7 shorter events, 0.0 us)
Async XLA Ops:
  1.0 12.8 %collective-permute-start = (bf16[12,8,16,128]{3,2,1,0:T(8,128)(2,1)S(1)}, bf16[12,8,16,128]{3,2,1,0:T(8,128)(2,1)S(1)}, u32[]{:S(2)}, u32[]{:S(2)}) collective-permute-start(bf16[12,8,16,128]{3,2,1,0:T(8,128)(2,1)S(1)} %constant_dynamic-slice_fusion), channel_id=1, source_target_pairs={{0,16},{16,0},{1,17},{17,1},{2,18},{18,2},{3,19},{19,3},{4,20},{20... | collective-permute-start | bytes 1179656 | tf_op jit(solution)/shard_map/ppermute | solution.py:483
  13.8 17.0 %copy-start.1 = (bf16[12,8,16,128]{3,2,1,0:T(8,128)(2,1)}, bf16[12,8,16,128]{3,2,1,0:T(8,128)(2,1)S(1)}, u32[]{:S(2)}) copy-start(bf16[12,8,16,128]{3,2,1,0:T(8,128)(2,1)S(1)} %collective-permute-done.refs_3_) | copy-start | bytes 1179652
  30.8 17.8 %collective-permute-start.1 = (bf16[2384,128]{1,0:T(8,128)(2,1)}, bf16[2384,128]{1,0:T(8,128)(2,1)S(1)}, u32[]{:S(2)}, u32[]{:S(2)}) collective-permute-start(bf16[2384,128]{1,0:T(8,128)(2,1)} %get-tuple-element.33), channel_id=1, source_target_pairs={{0,16},{16,0},{1,17},{17,1},{2,18},{18,2},{3,19},{19,3},{4,20},{20... | collective-permute-start | bytes 1830920 | tf_op jit(solution)/shard_map/ppermute | solution.py:483
  48.7 0.8 %copy-start = (bf16[2384,128]{1,0:T(8,128)(2,1)}, bf16[2384,128]{1,0:T(8,128)(2,1)S(1)}, u32[]{:S(2)}) copy-start(bf16[2384,128]{1,0:T(8,128)(2,1)S(1)} %collective-permute-done.1.refs_2_) | copy-start | bytes 1830916
  54.0 1.4 %collective-permute-start.2 = (f32[8,304]{1,0:T(8,128)}, f32[8,304]{1,0:T(8,128)S(1)}, u32[]{:S(2)}, u32[]{:S(2)}) collective-permute-start(f32[8,304]{1,0:T(8,128)} %get-tuple-element.36), channel_id=1, source_target_pairs={{0,1},{1,0},{2,3},{3,2},{4,5},{5,4},{6,7},{7,6},{8,9},{9,8},{10,11... | collective-permute-start | bytes 29192 | tf_op jit(solution)/shard_map/ppermute | solution.py:475
  56.1 3.7 %collective-permute-start.3 = (f32[8,304]{1,0:T(8,128)S(1)}, f32[8,304]{1,0:T(8,128)S(1)}, u32[]{:S(2)}, u32[]{:S(2)}) collective-permute-start(f32[8,304]{1,0:T(8,128)S(1)} %add.28), channel_id=1, source_target_pairs={{0,16},{16,0},{1,17},{17,1},{2,18},{18,2},{3,19},{19,3},{4,20},{20... | collective-permute-start | bytes 29192 | tf_op jit(solution)/shard_map/ppermute | solution.py:483
  59.8 3.7 %collective-permute-start.4 = (f32[8,304]{1,0:T(8,128)S(1)}, f32[8,304]{1,0:T(8,128)S(1)}, u32[]{:S(2)}, u32[]{:S(2)}) collective-permute-start(f32[8,304]{1,0:T(8,128)S(1)} %add.29), channel_id=1, source_target_pairs={{0,2},{1,3},{2,0},{3,1},{4,6},{5,7},{6,4},{7,5},{8,10},{9,11},{10,... | collective-permute-start | bytes 29192 | tf_op jit(solution)/shard_map/ppermute | solution.py:475
  63.5 3.7 %collective-permute-start.5 = (f32[8,304]{1,0:T(8,128)S(1)}, f32[8,304]{1,0:T(8,128)S(1)}, u32[]{:S(2)}, u32[]{:S(2)}) collective-permute-start(f32[8,304]{1,0:T(8,128)S(1)} %add.30), channel_id=1, source_target_pairs={{0,4},{1,5},{2,6},{3,7},{4,0},{5,1},{6,2},{7,3},{8,12},{9,13},{10,... | collective-permute-start | bytes 29192 | tf_op jit(solution)/shard_map/ppermute | solution.py:475
  67.2 8.4 %collective-permute-start.6 = (f32[8,304]{1,0:T(8,128)S(1)}, f32[8,304]{1,0:T(8,128)S(1)}, u32[]{:S(2)}, u32[]{:S(2)}) collective-permute-start(f32[8,304]{1,0:T(8,128)S(1)} %add.31), channel_id=1, source_target_pairs={{0,8},{1,9},{2,10},{3,11},{4,12},{5,13},{6,14},{7,15},{8,0},{9,1},... | collective-permute-start | bytes 29192 | tf_op jit(solution)/shard_map/ppermute | solution.py:475

commit v3 on v2

--- a/solution.py
+++ b/solution.py
@@ -15,7 +15,8 @@
 UNROLL = 8
 LANES = 128
 SPLIT = 4
-VMEM_LIMIT = 56 * 1024 * 1024
+PAIR_VMEM = 28 * 1024 * 1024
+SMALL_VMEM = 12 * 1024 * 1024
 NN = (((1,), (0,)), ((), ()))
 NT = (((1,), (1,)), ((), ()))
 
@@ -209,7 +210,7 @@
         in_specs=in_specs,
         out_specs=out_specs,
         scratch_shapes=scratch,
-        compiler_params=pltpu.CompilerParams(vmem_limit_bytes=VMEM_LIMIT),
+        compiler_params=pltpu.CompilerParams(vmem_limit_bytes=PAIR_VMEM),
         cost_estimate=pl.CostEstimate(
             flops=pair_count * 70 * 1024, bytes_accessed=pair_count * 48 * 1024, transcendentals=0
         ),
@@ -285,7 +286,7 @@
             pltpu.VMEM((padded * 16, LANES), jnp.float32),
             pltpu.VMEM((8, 16 * LANES), jnp.float32),
         ],
-        compiler_params=pltpu.CompilerParams(vmem_limit_bytes=VMEM_LIMIT),
+        compiler_params=pltpu.CompilerParams(vmem_limit_bytes=SMALL_VMEM),
         cost_estimate=pl.CostEstimate(flops=padded * 8 * 12288, bytes_accessed=16 << 20, transcendentals=0),
         name="combine",
     )(own, own_weights, other)
@@ -360,7 +361,7 @@
             pltpu.VMEM((padded, padded), jnp.bfloat16),
             pltpu.VMEM((padded, padded), jnp.bfloat16),
         ],
-        compiler_params=pltpu.CompilerParams(vmem_limit_bytes=VMEM_LIMIT),
+        compiler_params=pltpu.CompilerParams(vmem_limit_bytes=SMALL_VMEM),
         cost_estimate=pl.CostEstimate(flops=50 * padded**3, bytes_accessed=24 << 20, transcendentals=0),
         name="inverse",
     )(pair_rows)
@@ -400,7 +401,7 @@
         out_shape=jax.ShapeDtypeStruct((16, padded, LANES), jnp.float32),
         in_specs=[in_vmem()] * 4,
         out_specs=in_vmem(),
-        compiler_params=pltpu.CompilerParams(vmem_limit_bytes=VMEM_LIMIT),
+        compiler_params=pltpu.CompilerParams(vmem_limit_bytes=SMALL_VMEM),
         cost_estimate=pl.CostEstimate(
             flops=6 * padded * padded * 16 * LANES, bytes_accessed=20 << 20, transcendentals=0
         ),
@@ -460,7 +461,7 @@
         out_shape=jax.ShapeDtypeStruct((count * 16, LANES), jnp.float32),
         in_specs=[in_vmem()] * 4,
         out_specs=in_vmem(),
-        compiler_params=pltpu.CompilerParams(vmem_limit_bytes=VMEM_LIMIT),
+        compiler_params=pltpu.CompilerParams(vmem_limit_bytes=SMALL_VMEM),
         cost_estimate=pl.CostEstimate(flops=count * 16 * LANES * 6, bytes_accessed=16 << 20, transcendentals=0),
         name="refine",
     )(series, moments, *inverse)

time: 81.5 us -> 72 us (0.88)
  Pallas kernels: 56.2 us -> 44.7 us
  local copies, waits for them, and re-layouts: 1.84 us -> 5.48 us
  other arithmetic: 2.75 us -> 0.86 us
  waiting for transfers between devices: 8.45 us -> 9.55 us
    unnamed x4 -> x6, local copies, waits for them, and re-layouts: 0.82 us -> 4.46 us
    pallas_call x1, Pallas kernels: 5.78 us -> 2.45 us  [call_solve(): pl.pallas_call(solve_kernel, out_shape=jax.ShapeDtypeStruct((16, padded,...]
    pallas_call x2, Pallas kernels: 32.8 us -> 30.3 us  [call_pairs(): pl.pallas_call(lambda *refs: pair_kernel(pair_count, given is not None, s...]
    pallas_call x1, Pallas kernels: 4.5 us -> 2.06 us  [call_combine(): pl.pallas_call(lambda *refs: combine_kernel(dates, row_total, col_total,...]
    pallas_call x1, Pallas kernels: 4.71 us -> 2.94 us  [call_refine(): pl.pallas_call(lambda *refs: refine_kernel(count, row_total, col_total, *...]
    pallas_call x1, Pallas kernels: 8.32 us -> 6.88 us  [call_inverse(): pl.pallas_call(inverse_kernel, out_shape=(square, square), in_specs=[in_v...]
    add x4, other arithmetic: 1.32 us -> 0.02 us  [sum_devices(): value + lax.ppermute(value, 'cols', [(at, at ^ bit) for at in range(cols)])]
    ppermute x3, waiting for transfers between devices: 2.76 us -> 4.04 us  [swap_dates(): return lax.ppermute(value, 'dates', [(0, 1), (1, 0)])]
  transfers between devices with their start and end apart: 7 -> 7, of which waited for: 4 -> 5; matrix products, arithmetic and copies ran while one was open for 2% -> 1% of each run, Pallas kernels for 37% -> 33%
where the time goes in v3:
time: 72 us; the launch traced here: 71.6 us
  Pallas kernels  44.7 us (62%)
  starting transfers between devices  11 us (15%)
  waiting for transfers between devices  9.55 us (13%)
  local copies, waits for them, and re-layouts  5.48 us (8%)
  other arithmetic  0.86 us (1%)
    pallas_call x2, Pallas kernels, call_pairs(): pl.pallas_call(lambda *refs: pair_kernel(pair_count, given is not None, s...  30.3 us
    pallas_call x1, Pallas kernels, call_inverse(): pl.pallas_call(inverse_kernel, out_shape=(square, square), in_specs=[in_v...  6.88 us
    ppermute x4, starting transfers between devices, sum_devices(): lax.ppermute(value, 'cols', [(at, at ^ bit) for at in range(cols)])  5.71 us
    ppermute x4, waiting for transfers between devices, sum_devices(): lax.ppermute(value, 'cols', [(at, at ^ bit) for at in range(cols)])  5.51 us
    ppermute x3, starting transfers between devices, swap_dates(): return lax.ppermute(value, 'dates', [(0, 1), (1, 0)])  5.25 us
    unnamed x6, local copies, waits for them, and re-layouts  4.46 us
    ppermute x3, waiting for transfers between devices, swap_dates(): return lax.ppermute(value, 'dates', [(0, 1), (1, 0)])  4.04 us
    pallas_call x1, Pallas kernels, call_refine(): pl.pallas_call(lambda *refs: refine_kernel(count, row_total, col_total, *...  2.94 us
  transfers between devices with their start and end apart: 7, of which 5 were waited for; matrix products, arithmetic and copies ran while one was open for 1% of the time, Pallas kernels for 33%

profile of v3, /device:TPU:0, one launch (start us, length us, event | category | flops | bytes accessed | tf_op | source)
XLA Modules:
  0.0 71.6 jit_solution(14214448434328988607)
XLA Ops:
  0.0 1.0 %constant_dynamic-slice_fusion = bf16[12,8,16,128]{3,2,1,0:T(8,128)(2,1)S(1)} fusion(bf16[148,16,16,128]{3,2,1,0:T(8,128)(2,1)} %bitcast.7, s32[]{:T(128)S(6)} %select_n.10, s32[]{:T(128)S(6)} %select_n.11), kind=kLoop, calls=%fused_computation.10 | loop fusion | bytes 786440 | tf_op jit(solution)/shard_map/dynamic_slice | solution.py:503
  1.0 3.0 %collective-permute-start = (bf16[12,8,16,128]{3,2,1,0:T(8,128)(2,1)S(1)}, bf16[12,8,16,128]{3,2,1,0:T(8,128)(2,1)S(1)}, u32[]{:S(2)}, u32[]{:S(2)}) collective-permute-start(bf16[12,8,16,128]{3,2,1,0:T(8,128)(2,1)S(1)} %constant_dynamic-slice_fusion), channel_id=1, source_target_pairs={{0,16},{16,0},{1,17},{17,1},{2,18},{18,2},{3,19},{19,3},{4,20},{20... | collective-permute-start | bytes 1179656 | tf_op jit(solution)/shard_map/ppermute | solution.py:484
  4.0 0.8 %fusion.refs_0_ = s32[1480]{0:T(1024)S(1)} fusion(s32[1480,2]{0,1:T(2,128)} %param.4, s32[]{:T(128)S(6)} %mul.11, s32[]{:T(128)S(6)} %add.27, s32[]{:T(128)S(6)} %mul.10), kind=kLoop, calls=%fused_computation.5 | loop fusion | flops 29600 | bytes 17772 | tf_op jit(solution)/shard_map/jit(_where)/select_n | solution.py:501
  4.9 0.0 copy-start.2
  4.9 0.7 copy-done.2
  5.6 6.9 %inverse.1 = (bf16[304,304]{1,0:T(8,128)(2,1)S(1)}, bf16[304,304]{1,0:T(8,128)(2,1)S(1)}) custom-call(s32[2,1480]{1,0:T(2,128)S(1)} %bitcast.10), custom_call_target="tpu_custom_call" | custom-call | flops 1404723200 | bytes 25165824 | tf_op jit(solution)/shard_map/inverse/pallas_call | solution.py:353
  12.5 0.7 collective-permute-done.refs_3_
  13.2 3.8 %copy-done = bf16[148,32,2,512]{3,2,1,0:T(2,128)(2,1)S(1)} copy-done((bf16[148,32,2,512]{3,2,1,0:T(2,128)(2,1)S(1)}, bf16[148,32,2,512]{3,2,1,0:T(2,128)(2,1)}, u32[]{:S(2)}) %copy-start) | copy-done | bytes 9699352
  16.9 16.0 %pairs_other.1 = (bf16[2384,128]{1,0:T(8,128)(2,1)S(1)}, s32[2976]{0:T(1024)S(1)}, s32[2]{0:T(128)S(1)}) custom-call(s32[1480]{0:T(1024)S(1)} %fusion.refs_0_, bf16[148,16,16,128]{3,2,1,0:T(8,128)(2,1)S(1)} %bitcast.8, bf16[512,512]{1,0:T(8,128)(2,1)S(1)} %copy-done.1), custom_call_target="tpu_custom_call" | custom-call | flops 106086400 | bytes 72744960 | tf_op jit(solution)/shard_map/pairs_other/pallas_call | solution.py:207
  33.0 1.9 %collective-permute-start.1 = (bf16[2384,128]{1,0:T(8,128)(2,1)S(1)}, bf16[2384,128]{1,0:T(8,128)(2,1)S(1)}, u32[]{:S(2)}, u32[]{:S(2)}) collective-permute-start(bf16[2384,128]{1,0:T(8,128)(2,1)S(1)} %get-tuple-element.33), channel_id=1, source_target_pairs={{0,16},{16,0},{1,17},{17,1},{2,18},{18,2},{3,19},{19,3},{4,20},{20... | collective-permute-start | bytes 1830920 | tf_op jit(solution)/shard_map/ppermute | solution.py:484
  34.9 14.3 %pairs_own.1 = (f32[2576,128]{1,0:T(8,128)S(1)}, f32[8,128]{1,0:T(8,128)S(1)}) custom-call(s32[2976]{0:T(1024)S(1)} %get-tuple-element.28.refs_0_, s32[2]{0:T(128)S(1)} %get-tuple-element.29.refs_1_, bf16[148,16,16,128]{3,2,1,0:T(8,128)(2,1)S(1)} %bitcast.9, bf16[12,8,16,128]{3,2,1,0:T(8,128)(2,1)S(1)} %collective-permute-done.refs_3_, ...), custom_call_target="tpu_custom_call" | custom-call | flops 106086400 | bytes 72744960 | tf_op jit(solution)/shard_map/pairs_own/pallas_call | solution.py:207
  49.2 0.0 collective-permute-done.1.refs_2_
  49.2 2.1 %combine.1 = (bf16[304,2048]{1,0:T(8,128)(2,1)S(1)}, bf16[304,2048]{1,0:T(8,128)(2,1)S(1)}, f32[8,304]{1,0:T(8,128)S(1)}) custom-call(f32[2576,128]{1,0:T(8,128)S(1)} %get-tuple-element.31.refs_0_, f32[8,128]{1,0:T(8,128)S(1)} %get-tuple-element.32.refs_1_, bf16[2384,128]{1,0:T(8,128)(2,1)S(1)} %collective-permute-done.1.refs_2_), custom_call_target="tpu_custom_call" | custom-call | flops 29884416 | bytes 16777216 | tf_op jit(solution)/shard_map/combine/pallas_call | solution.py:280
  51.2 0.0 collective-permute-start.2
  51.2 1.2 %collective-permute-done.2 = f32[8,304]{1,0:T(8,128)S(1)} collective-permute-done((f32[8,304]{1,0:T(8,128)S(1)}, f32[8,304]{1,0:T(8,128)S(1)}, u32[]{:S(2)}, u32[]{:S(2)}) %collective-permute-start.2) | collective-permute-done | bytes 9760 | tf_op jit(solution)/shard_map/ppermute | solution.py:476
  52.5 0.3 collective-permute-start.3
  52.8 3.4 %collective-permute-done.3 = f32[8,304]{1,0:T(8,128)S(1)} collective-permute-done((f32[8,304]{1,0:T(8,128)S(1)}, f32[8,304]{1,0:T(8,128)S(1)}, u32[]{:S(2)}, u32[]{:S(2)}) %collective-permute-start.3) | collective-permute-done | bytes 9760 | tf_op jit(solution)/shard_map/ppermute | solution.py:484
  56.2 1.5 %collective-permute-start.4 = (f32[8,304]{1,0:T(8,128)S(1)}, f32[8,304]{1,0:T(8,128)S(1)}, u32[]{:S(2)}, u32[]{:S(2)}) collective-permute-start(f32[8,304]{1,0:T(8,128)S(1)} %add.29), channel_id=1, source_target_pairs={{0,2},{1,3},{2,0},{3,1},{4,6},{5,7},{6,4},{7,5},{8,10},{9,11},{10,... | collective-permute-start | bytes 29192 | tf_op jit(solution)/shard_map/ppermute | solution.py:476
  57.7 2.2 %collective-permute-done.4 = f32[8,304]{1,0:T(8,128)S(1)} collective-permute-done((f32[8,304]{1,0:T(8,128)S(1)}, f32[8,304]{1,0:T(8,128)S(1)}, u32[]{:S(2)}, u32[]{:S(2)}) %collective-permute-start.4) | collective-permute-done | bytes 9760 | tf_op jit(solution)/shard_map/ppermute | solution.py:476
  59.9 1.6 %collective-permute-start.5 = (f32[8,304]{1,0:T(8,128)S(1)}, f32[8,304]{1,0:T(8,128)S(1)}, u32[]{:S(2)}, u32[]{:S(2)}) collective-permute-start(f32[8,304]{1,0:T(8,128)S(1)} %add.30), channel_id=1, source_target_pairs={{0,4},{1,5},{2,6},{3,7},{4,0},{5,1},{6,2},{7,3},{8,12},{9,13},{10,... | collective-permute-start | bytes 29192 | tf_op jit(solution)/shard_map/ppermute | solution.py:476
  61.4 2.1 %collective-permute-done.5 = f32[8,304]{1,0:T(8,128)S(1)} collective-permute-done((f32[8,304]{1,0:T(8,128)S(1)}, f32[8,304]{1,0:T(8,128)S(1)}, u32[]{:S(2)}, u32[]{:S(2)}) %collective-permute-start.5) | collective-permute-done | bytes 9760 | tf_op jit(solution)/shard_map/ppermute | solution.py:476
  63.6 2.6 %collective-permute-start.6 = (f32[8,304]{1,0:T(8,128)S(1)}, f32[8,304]{1,0:T(8,128)S(1)}, u32[]{:S(2)}, u32[]{:S(2)}) collective-permute-start(f32[8,304]{1,0:T(8,128)S(1)} %add.31), channel_id=1, source_target_pairs={{0,8},{1,9},{2,10},{3,11},{4,12},{5,13},{6,14},{7,15},{8,0},{9,1},... | collective-permute-start | bytes 29192 | tf_op jit(solution)/shard_map/ppermute | solution.py:476
  66.2 2.5 %solve.1.refs_0_ = f32[16,304,128]{2,1,0:T(8,128)S(1)} custom-call(bf16[304,304]{1,0:T(8,128)(2,1)S(1)} %get-tuple-element.25.inverse_high.refs_2_, bf16[304,304]{1,0:T(8,128)(2,1)S(1)} %get-tuple-element.26.inverse_low.refs_3_, bf16[304,2048]{1,0:T(8,128)(2,1)S(1)} %get-tuple-element.34.high, bf16[304,2048]{1,0:T(8,128)(2,1)S(1)} %get-tuple-element.35.low), custom_call_target="tpu_custom_call" | custom-call | flops 1135607808 | bytes 20971520 | tf_op jit(solution)/shard_map/solve/pallas_call | solution.py:399
  68.6 2.9 %refine.1 = f32[4736,128]{1,0:T(8,128)} custom-call(f32[16,304,128]{2,1,0:T(8,128)S(1)} %solve.1.refs_0_, f32[8,304]{1,0:T(8,128)S(1)} %add.32.refs_1_, bf16[304,304]{1,0:T(8,128)(2,1)S(1)} %get-tuple-element.25.inverse_high.refs_2_, bf16[304,304]{1,0:T(8,128)(2,1)S(1)} %get-tuple-element.26.inverse_low.refs_3_), custom_call_target="tpu_custom_call" | custom-call | flops 3637248 | bytes 16777216 | tf_op jit(solution)/shard_map/refine/pallas_call | solution.py:459
  (9 shorter events, 0.0 us)
Async XLA Ops:
  1.0 12.1 %collective-permute-start = (bf16[12,8,16,128]{3,2,1,0:T(8,128)(2,1)S(1)}, bf16[12,8,16,128]{3,2,1,0:T(8,128)(2,1)S(1)}, u32[]{:S(2)}, u32[]{:S(2)}) collective-permute-start(bf16[12,8,16,128]{3,2,1,0:T(8,128)(2,1)S(1)} %constant_dynamic-slice_fusion), channel_id=1, source_target_pairs={{0,16},{16,0},{1,17},{17,1},{2,18},{18,2},{3,19},{19,3},{4,20},{20... | collective-permute-start | bytes 1179656 | tf_op jit(solution)/shard_map/ppermute | solution.py:484
  4.9 0.7 copy-start.2
  5.6 7.6 %copy-start.1 = (bf16[512,512]{1,0:T(8,128)(2,1)S(1)}, bf16[512,512]{1,0:T(8,128)(2,1)}, u32[]{:S(2)}) copy-start(bf16[512,512]{1,0:T(8,128)(2,1)} %constant.26.clone.refs_2_.refs_4_) | copy-start | bytes 1572868
  13.1 3.8 %copy-start = (bf16[148,32,2,512]{3,2,1,0:T(2,128)(2,1)S(1)}, bf16[148,32,2,512]{3,2,1,0:T(2,128)(2,1)}, u32[]{:S(2)}) copy-start(bf16[148,32,2,512]{3,2,1,0:T(2,128)(2,1)} %param.3) | copy-start | bytes 29097988
  33.0 16.2 %collective-permute-start.1 = (bf16[2384,128]{1,0:T(8,128)(2,1)S(1)}, bf16[2384,128]{1,0:T(8,128)(2,1)S(1)}, u32[]{:S(2)}, u32[]{:S(2)}) collective-permute-start(bf16[2384,128]{1,0:T(8,128)(2,1)S(1)} %get-tuple-element.33), channel_id=1, source_target_pairs={{0,16},{16,0},{1,17},{17,1},{2,18},{18,2},{3,19},{19,3},{4,20},{20... | collective-permute-start | bytes 1830920 | tf_op jit(solution)/shard_map/ppermute | solution.py:484
  51.2 1.2 %collective-permute-start.2 = (f32[8,304]{1,0:T(8,128)S(1)}, f32[8,304]{1,0:T(8,128)S(1)}, u32[]{:S(2)}, u32[]{:S(2)}) collective-permute-start(f32[8,304]{1,0:T(8,128)S(1)} %get-tuple-element.36), channel_id=1, source_target_pairs={{0,1},{1,0},{2,3},{3,2},{4,5},{5,4},{6,7},{7,6},{8,9},{9,8},{10,11... | collective-permute-start | bytes 29192 | tf_op jit(solution)/shard_map/ppermute | solution.py:476
  52.5 3.7 %collective-permute-start.3 = (f32[8,304]{1,0:T(8,128)S(1)}, f32[8,304]{1,0:T(8,128)S(1)}, u32[]{:S(2)}, u32[]{:S(2)}) collective-permute-start(f32[8,304]{1,0:T(8,128)S(1)} %add.28), channel_id=1, source_target_pairs={{0,16},{16,0},{1,17},{17,1},{2,18},{18,2},{3,19},{19,3},{4,20},{20... | collective-permute-start | bytes 29192 | tf_op jit(solution)/shard_map/ppermute | solution.py:484
  56.2 3.7 %collective-permute-start.4 = (f32[8,304]{1,0:T(8,128)S(1)}, f32[8,304]{1,0:T(8,128)S(1)}, u32[]{:S(2)}, u32[]{:S(2)}) collective-permute-start(f32[8,304]{1,0:T(8,128)S(1)} %add.29), channel_id=1, source_target_pairs={{0,2},{1,3},{2,0},{3,1},{4,6},{5,7},{6,4},{7,5},{8,10},{9,11},{10,... | collective-permute-start | bytes 29192 | tf_op jit(solution)/shard_map/ppermute | solution.py:476
  59.9 3.7 %collective-permute-start.5 = (f32[8,304]{1,0:T(8,128)S(1)}, f32[8,304]{1,0:T(8,128)S(1)}, u32[]{:S(2)}, u32[]{:S(2)}) collective-permute-start(f32[8,304]{1,0:T(8,128)S(1)} %add.30), channel_id=1, source_target_pairs={{0,4},{1,5},{2,6},{3,7},{4,0},{5,1},{6,2},{7,3},{8,12},{9,13},{10,... | collective-permute-start | bytes 29192 | tf_op jit(solution)/shard_map/ppermute | solution.py:476
  63.6 5.1 %collective-permute-start.6 = (f32[8,304]{1,0:T(8,128)S(1)}, f32[8,304]{1,0:T(8,128)S(1)}, u32[]{:S(2)}, u32[]{:S(2)}) collective-permute-start(f32[8,304]{1,0:T(8,128)S(1)} %add.31), channel_id=1, source_target_pairs={{0,8},{1,9},{2,10},{3,11},{4,12},{5,13},{6,14},{7,15},{8,0},{9,1},... | collective-permute-start | bytes 29192 | tf_op jit(solution)/shard_map/ppermute | solution.py:476

commit v4 on v3

--- a/solution.py
+++ b/solution.py
@@ -15,7 +15,9 @@
 UNROLL = 8
 LANES = 128
 SPLIT = 4
-PAIR_VMEM = 28 * 1024 * 1024
+SOME_STEPS = 3
+PAIR_VMEM = 52 * 1024 * 1024
+OWN_VMEM = 32 * 1024 * 1024
 SMALL_VMEM = 12 * 1024 * 1024
 NN = (((1,), (0,)), ((), ()))
 NT = (((1,), (1,)), ((), ()))
@@ -37,8 +39,8 @@
     return lax.dot_general(first, second, dims, preferred_element_type=jnp.float32)
 
 
-def spread_looks(source, date, slot, step, looks, planes, choose=None, start=0, share=0, found=None):
-    raw = source[pl.ds(date, step)].reshape(step, 2, SPLIT, 16, LANES)
+def spread_looks(source, row, date, slot, step, looks, planes, choose=None, start=0, share=0, found=None):
+    raw = source[pl.ds(date, step), pl.ds(row, 8)].reshape(step, 2, SPLIT, 16, LANES)
     left = jnp.concatenate(
         [raw[:, :, sub].reshape(step * 32, LANES) for sub in range(SPLIT)], axis=1
     )
@@ -59,7 +61,7 @@
 
 def pair_kernel(pair_count, with_halo, step, *refs):
     if with_halo:
-        (listed, counts, images, halo, looks, series, weights, raw, raw_halo, planes, sems) = refs
+        (listed, counts, images, halo, looks, series, weights, planes) = refs
     else:
         (pairs, images, looks, series, listed, counts, raw, planes, sems, sums) = refs
     dates = images.shape[0]
@@ -67,16 +69,13 @@
     me = lax.axis_index("dates")
     row_start = 8 * (me if with_halo else 1 - me)
     own_slot, halo_slot = GAP * me, dates * (1 - me)
-    copies = [
-        pltpu.make_async_copy(
-            images.at[pl.ds(at * step, step), pl.ds(row_start, 8)],
-            raw.at[pl.ds(at * step, step)],
-            sems.at[at],
-        )
-        for at in range(steps)
-    ]
-    if with_halo:
-        copies.append(pltpu.make_async_copy(halo, raw_halo, sems.at[steps]))
+    copies = []
+    if not with_halo:
+        for at in range(steps):
+            part = pl.ds(at * step, step)
+            copies.append(
+                pltpu.make_async_copy(images.at[part, pl.ds(row_start, 8)], raw.at[part], sems.at[at])
+            )
     for copy in copies:
         copy.start()
 
@@ -96,9 +95,13 @@
     found = (jnp.int32(0), jnp.int32(0))
     share = 0 if with_halo else pair_count // dates
     for at in range(steps):
-        copies[at].wait()
+        if with_halo:
+            source, row = images, row_start
+        else:
+            copies[at].wait()
+            source, row = raw, 0
         found = spread_looks(
-            raw, at * step, own_slot + at * step, step, looks, planes,
+            source, row, at * step, own_slot + at * step, step, looks, planes,
             choose, at * step * share, share, found,
         )
     if not with_halo:
@@ -109,8 +112,7 @@
             for at in range(UNROLL):
                 listed[part * second_list + found[part] + at] = jnp.int32(spare * 1025)
     if with_halo:
-        copies[steps].wait()
-        spread_looks(raw_halo, 0, halo_slot, GAP, looks, planes)
+        spread_looks(halo, 0, 0, halo_slot, GAP, looks, planes)
 
     def one_pair(packed, power):
         first = packed & 1023
@@ -181,17 +183,12 @@
     pair_count = pairs.shape[0]
     step = max(k for k in range(1, MAX_STEP + 1) if dates % k == 0)
     slots = dates + GAP + 1
-    scratch = [
-        pltpu.VMEM((dates, 8, 16, LANES), jnp.bfloat16),
-        pltpu.VMEM((slots * 128, LANES), jnp.float32),
-        pltpu.SemaphoreType.DMA((dates // step + 1,)),
-    ]
+    scratch = [pltpu.VMEM((slots * 128, LANES), jnp.float32)]
     sums = jax.ShapeDtypeStruct((slots * 16, LANES), jnp.float32)
     if given is not None:
         halo, listed, counts = given
         out_shape = (sums, jax.ShapeDtypeStruct((8, LANES), jnp.float32))
-        scratch.insert(1, pltpu.VMEM((GAP, 8, 16, LANES), jnp.bfloat16))
-        in_specs = [in_smem()] * 2 + [in_hbm(), in_hbm(), in_vmem()]
+        in_specs = [in_smem()] * 2 + [in_vmem()] * 3
         out_specs = (in_vmem(), in_vmem())
         args = (listed, counts, images, halo, looks)
     else:
@@ -200,7 +197,8 @@
             jax.ShapeDtypeStruct((2 * (pair_count + UNROLL),), jnp.int32),
             jax.ShapeDtypeStruct((2,), jnp.int32),
         )
-        scratch.append(pltpu.VMEM(sums.shape, sums.dtype))
+        scratch = [pltpu.VMEM((dates, 8, 16, LANES), jnp.bfloat16)] + scratch
+        scratch += [pltpu.SemaphoreType.DMA((dates // step,)), pltpu.VMEM(sums.shape, sums.dtype)]
         in_specs = [in_smem(), in_hbm(), in_vmem()]
         out_specs = (in_vmem(), in_smem(), in_smem())
         args = (pairs, images, looks)
@@ -210,7 +208,7 @@
         in_specs=in_specs,
         out_specs=out_specs,
         scratch_shapes=scratch,
-        compiler_params=pltpu.CompilerParams(vmem_limit_bytes=PAIR_VMEM),
+        compiler_params=pltpu.CompilerParams(vmem_limit_bytes=PAIR_VMEM if given is None else OWN_VMEM),
         cost_estimate=pl.CostEstimate(
             flops=pair_count * 70 * 1024, bytes_accessed=pair_count * 48 * 1024, transcendentals=0
         ),
@@ -296,28 +294,31 @@
     return (count + 3 + 15) // 16 * 16
 
 
-def inverse_kernel(pairs, high, low, state, residual, normal_high, normal_low):
-    padded = high.shape[0]
+def start_inverse_kernel(pairs, state, normal_high, normal_low, progress):
+    padded = state.shape[0]
     date = lax.broadcasted_iota(jnp.int32, (padded, pairs.shape[1]), 0)
     design = (
         jnp.where(date == pairs[0:1, :], 1.0, 0.0) - jnp.where(date == pairs[1:2, :], 1.0, 0.0)
     ).astype(jnp.bfloat16)
-    eye = jnp.where(
-        lax.broadcasted_iota(jnp.int32, (padded, padded), 0)
-        == lax.broadcasted_iota(jnp.int32, (padded, padded), 1),
-        1.0,
-        0.0,
-    )
+    eye = unit(padded)
     normal = dot32(design, design, NT) + RIDGE * eye
     normal_high[...], normal_low[...] = split_bf16(normal)
     largest = jnp.max(jnp.sum(jnp.abs(normal), axis=1))
-    careful = largest > 128.0
     scale, error = centre((largest - RIDGE) / (largest + RIDGE))
-    start = 2.0 / (largest + RIDGE)
-    state[...] = (scale * start) * (2.0 * eye - start * normal)
+    first = 2.0 / (largest + RIDGE)
+    state[...] = (scale * first) * (2.0 * eye - first * normal)
+    progress[0] = error
+    progress[1] = largest
+
+
+def go_on_inverse_kernel(last, state, normal_high, normal_low, progress, *refs):
+    residual, now_state = refs[-2:]
+    eye = unit(state.shape[0])
+    careful = progress[1] > 128.0
+    now_state[...] = state[...]
 
     def step(scale):
-        now, rest = split_bf16(state[...])
+        now, rest = split_bf16(now_state[...])
         residual[...] = eye - dot32(normal_high[...], now, NN) - dot32(normal_high[...], rest, NN)
 
         @pl.when(careful)
@@ -326,20 +327,34 @@
 
         upper, lower = split_bf16(residual[...])
         change = dot32(now, upper, NN)
-        state[...] = scale * (state[...] + change)
+        now_state[...] = scale * (now_state[...] + change)
 
         @pl.when(careful)
         def _():
-            state[...] += scale * (dot32(now, lower, NN) + dot32(rest, upper, NN))
-
-    def body(error):
+            now_state[...] += scale * (dot32(now, lower, NN) + dot32(rest, upper, NN))
+
+    def unfinished(carry):
+        return (carry[0] > 5e-4) & (last | (carry[1] < SOME_STEPS))
+
+    def body(carry):
+        error, count = carry
         scale, left = centre(error)
         step(scale)
-        return jnp.maximum(left, 0.05 * error)
-
-    lax.while_loop(lambda error: error > 5e-4, body, error)
-    step(jnp.float32(1.0))
-    high[...], low[...] = split_bf16(state[...])
+        return jnp.maximum(left, 0.05 * error), count + 1
+
+    error, _ = lax.while_loop(unfinished, body, (progress[0], jnp.int32(0)))
+    if last:
+        step(jnp.float32(1.0))
+        refs[0][...], refs[1][...] = split_bf16(now_state[...])
+    else:
+        refs[0][...] = now_state[...]
+        refs[1][0] = error
+        refs[1][1] = progress[1]
+
+
+def unit(size):
+    row = lax.broadcasted_iota(jnp.int32, (size, size), 0)
+    return jnp.where(row == lax.broadcasted_iota(jnp.int32, (size, size), 1), 1.0, 0.0)
 
 
 def centre(error):
@@ -347,24 +362,45 @@
     return scale, scale - 1.0
 
 
-def call_inverse(pair_rows, count):
+def inverse_call(kernel, out_shape, out_specs, scratch, name, args):
+    return pl.pallas_call(
+        kernel,
+        out_shape=out_shape,
+        in_specs=[in_vmem()] * min(len(args), 3) + [in_smem()] * (len(args) - 3),
+        out_specs=out_specs,
+        scratch_shapes=scratch,
+        compiler_params=pltpu.CompilerParams(vmem_limit_bytes=SMALL_VMEM),
+        cost_estimate=pl.CostEstimate(flops=1 << 30, bytes_accessed=8 << 20, transcendentals=0),
+        name=name,
+    )(*args)
+
+
+def start_inverse(pair_rows, count):
     padded = pad_dates(count)
-    square = jax.ShapeDtypeStruct((padded, padded), jnp.bfloat16)
-    return pl.pallas_call(
-        inverse_kernel,
-        out_shape=(square, square),
-        in_specs=[in_vmem()],
-        out_specs=(in_vmem(),) * 2,
-        scratch_shapes=[
-            pltpu.VMEM((padded, padded), jnp.float32),
-            pltpu.VMEM((padded, padded), jnp.float32),
-            pltpu.VMEM((padded, padded), jnp.bfloat16),
-            pltpu.VMEM((padded, padded), jnp.bfloat16),
-        ],
-        compiler_params=pltpu.CompilerParams(vmem_limit_bytes=SMALL_VMEM),
-        cost_estimate=pl.CostEstimate(flops=50 * padded**3, bytes_accessed=24 << 20, transcendentals=0),
-        name="inverse",
-    )(pair_rows)
+    full = jax.ShapeDtypeStruct((padded, padded), jnp.float32)
+    half = jax.ShapeDtypeStruct((padded, padded), jnp.bfloat16)
+    progress = jax.ShapeDtypeStruct((2,), jnp.float32)
+    return inverse_call(
+        start_inverse_kernel,
+        (full, half, half, progress),
+        (in_vmem(), in_vmem(), in_vmem(), in_smem()),
+        [],
+        "start_inverse",
+        (pair_rows,),
+    )
+
+
+def go_on_inverse(state, normal_high, normal_low, progress, last):
+    out_shape = (normal_high, normal_high) if last else (state, progress)
+    full = pltpu.VMEM(state.shape, jnp.float32)
+    return inverse_call(
+        lambda *refs: go_on_inverse_kernel(last, *refs),
+        tuple(jax.ShapeDtypeStruct(like.shape, like.dtype) for like in out_shape),
+        (in_vmem(), in_vmem() if last else in_smem()),
+        [full, full],
+        "end_inverse" if last else "go_on_inverse",
+        (state, normal_high, normal_low, progress),
+    )
 
 
 def solve_kernel(inverse_high, inverse_low, high, low, series):
@@ -467,17 +503,25 @@
     )(series, moments, *inverse)
 
 
-def sum_devices(value):
+def sum_beside(value, work):
     cols = lax.axis_size("cols")
+    pairings = [("dates", [(0, 1), (1, 0)])]
+    bit = cols // 2
+    while bit and not cols & (cols - 1):
+        pairings.append(("cols", [(at, at ^ bit) for at in range(cols)]))
+        bit //= 2
+    state = ()
+    for at in range(max(len(pairings), len(work))):
+        value, state = lax.optimization_barrier((value, state))
+        if at < len(pairings):
+            other = lax.ppermute(value, *pairings[at])
+        if at < len(work):
+            state = work[at](state)
+        if at < len(pairings):
+            value = value + other
     if cols & (cols - 1):
-        return lax.psum(value, ("dates", "cols"))
-    bit = 1
-    while bit < cols:
-        value = value + lax.ppermute(value, "cols", [(at, at ^ bit) for at in range(cols)])
-        bit *= 2
-        if bit == 2:
-            value = value + swap_dates(value)
-    return value
+        value = lax.psum(value, "cols")
+    return value, state
 
 
 def swap_dates(value):
@@ -503,17 +547,29 @@
     edge = lax.dynamic_slice(
         images, ((dates - GAP) * (1 - me), half * (1 - me), 0, 0), (GAP, half, 16, LANES)
     )
-    edge, pair_rows = lax.optimization_barrier((edge, pair_list.T))
+    edge, packed = lax.optimization_barrier((edge, packed))
     halo = swap_dates(edge)
-    inverse = call_inverse(pair_rows, dates * 2)
-    halo, inverse, packed = lax.optimization_barrier((halo, inverse, packed))
     looks = jnp.asarray(look_matrix(), jnp.bfloat16)
     other, listed, counts = call_pairs(packed, images, looks)
+    other, halo = lax.optimization_barrier((other, halo))
     other = swap_dates(other)
     own, own_weights = call_pairs(packed, images, looks, (halo, listed, counts))
     high, lowpart, moments = call_combine(own, own_weights, other, dates, row_total, col_total)
-    moments = sum_devices(moments)
-    series = call_solve(inverse, (high, lowpart))
+
+    def first(state):
+        return start_inverse(pair_list.T, dates * 2)
+
+    def second(state):
+        values, progress = go_on_inverse(*state, last=False)
+        return (values,) + state[1:3] + (progress,)
+
+    def third(state):
+        return go_on_inverse(*state, last=True)
+
+    def fourth(state):
+        return state, call_solve(state, (high, lowpart))
+
+    moments, (inverse, series) = sum_beside(moments, [first, second, third, fourth])
     refined = call_refine(series, moments, inverse, dates * 2, row_total, col_total)
     return refined.reshape(dates * 2, half, 2, LANES)
 

time: 72 us -> 64 us (0.89)
  waiting for transfers between devices: 9.55 us -> 4.72 us
  local copies, waits for them, and re-layouts: 5.48 us -> 2.08 us
    unnamed x6, local copies, waits for them, and re-layouts: 4.46 us -> 1.05 us
    ppermute x4 -> x5, waiting for transfers between devices: 5.51 us -> 2.46 us  [sum_beside(): other = lax.ppermute(value, *pairings[at])]
    ppermute x3 -> x2, waiting for transfers between devices: 4.04 us -> 2.25 us  [swap_dates(): return lax.ppermute(value, 'dates', [(0, 1), (1, 0)])]
    pallas_call x1 -> x3, Pallas kernels: 6.88 us -> 8.65 us  [inverse_call(): pl.pallas_call(kernel, out_shape=out_shape, in_specs=[in_vmem()] * min(le...]
    ppermute x3 -> x2, starting transfers between devices: 5.25 us -> 3.57 us  [swap_dates(): return lax.ppermute(value, 'dates', [(0, 1), (1, 0)])]
    pallas_call x2, Pallas kernels: 30.3 us -> 29.2 us  [call_pairs(): pl.pallas_call(lambda *refs: pair_kernel(pair_count, given is not None, s...]
    ppermute x4 -> x5, starting transfers between devices: 5.71 us -> 6.72 us  [sum_beside(): other = lax.ppermute(value, *pairings[at])]
  transfers between devices with their start and end apart: 7 -> 7, of which waited for: 5 -> 3; matrix products, arithmetic and copies ran while one was open for 1% -> 0% of each run, Pallas kernels for 33% -> 64%
where the time goes in v4:
time: 64 us; the launch traced here: 63.4 us
  Pallas kernels  45.3 us (71%)
  starting transfers between devices  10.3 us (16%)
  waiting for transfers between devices  4.72 us (7%)
  local copies, waits for them, and re-layouts  2.08 us (3%)
  other arithmetic  0.86 us (1%)
    pallas_call x2, Pallas kernels, call_pairs(): pl.pallas_call(lambda *refs: pair_kernel(pair_count, given is not None, s...  29.2 us
    pallas_call x3, Pallas kernels, inverse_call(): pl.pallas_call(kernel, out_shape=out_shape, in_specs=[in_vmem()] * min(le...  8.65 us
    ppermute x5, starting transfers between devices, sum_beside(): other = lax.ppermute(value, *pairings[at])  6.72 us
    ppermute x2, starting transfers between devices, swap_dates(): return lax.ppermute(value, 'dates', [(0, 1), (1, 0)])  3.57 us
    pallas_call x1, Pallas kernels, call_refine(): pl.pallas_call(lambda *refs: refine_kernel(count, row_total, col_total, *...  2.94 us
    ppermute x5, waiting for transfers between devices, sum_beside(): other = lax.ppermute(value, *pairings[at])  2.46 us
    pallas_call x1, Pallas kernels, call_solve(): pl.pallas_call(solve_kernel, out_shape=jax.ShapeDtypeStruct((16, padded,...  2.43 us
    ppermute x2, waiting for transfers between devices, swap_dates(): return lax.ppermute(value, 'dates', [(0, 1), (1, 0)])  2.25 us
  transfers between devices with their start and end apart: 7, of which 3 were waited for; matrix products, arithmetic and copies ran while one was open for 0% of the time, Pallas kernels for 64%

profile of v4, /device:TPU:0, one launch (start us, length us, event | category | flops | bytes accessed | tf_op | source)
XLA Modules:
  0.0 63.4 jit_solution(9022595030646156554)
XLA Ops:
  0.0 0.8 %fusion.refs_0_ = s32[1480]{0:T(1024)S(1)} fusion(s32[1480,2]{0,1:T(2,128)} %param.4, s32[]{:T(128)S(6)} %mul.11, s32[]{:T(128)S(6)} %add.27, s32[]{:T(128)S(6)} %mul.10), kind=kLoop, calls=%fused_computation.5 | loop fusion | flops 29600 | bytes 17772 | tf_op jit(solution)/shard_map/jit(_where)/select_n | solution.py:545
  0.8 1.0 %constant_dynamic-slice_fusion = bf16[12,8,16,128]{3,2,1,0:T(8,128)(2,1)S(1)} fusion(bf16[148,16,16,128]{3,2,1,0:T(8,128)(2,1)} %bitcast.7, s32[]{:T(128)S(6)} %select_n.10, s32[]{:T(128)S(6)} %select_n.11), kind=kLoop, calls=%fused_computation.10 | loop fusion | bytes 786440 | tf_op jit(solution)/shard_map/dynamic_slice | solution.py:547
  1.9 3.0 %collective-permute-start = (bf16[12,8,16,128]{3,2,1,0:T(8,128)(2,1)S(1)}, bf16[12,8,16,128]{3,2,1,0:T(8,128)(2,1)S(1)}, u32[]{:S(2)}, u32[]{:S(2)}) collective-permute-start(bf16[12,8,16,128]{3,2,1,0:T(8,128)(2,1)S(1)} %constant_dynamic-slice_fusion), channel_id=1, source_target_pairs={{0,16},{16,0},{1,17},{17,1},{2,18},{18,2},{3,19},{19,3},{4,20},{20... | collective-permute-start | bytes 1179656 | tf_op jit(solution)/shard_map/ppermute | solution.py:528
  4.9 1.0 %copy-done.1 = bf16[512,512]{1,0:T(8,128)(2,1)S(1)} copy-done((bf16[512,512]{1,0:T(8,128)(2,1)S(1)}, bf16[512,512]{1,0:T(8,128)(2,1)}, u32[]{:S(2)}) %copy-start.1) | copy-done | bytes 524312
  5.9 16.8 %pairs_other.1 = (bf16[2384,128]{1,0:T(8,128)(2,1)S(1)}, s32[2976]{0:T(1024)S(1)}, s32[2]{0:T(128)S(1)}) custom-call(s32[1480]{0:T(1024)S(1)} %fusion.refs_0_, bf16[148,16,16,128]{3,2,1,0:T(8,128)(2,1)} %bitcast.8, bf16[512,512]{1,0:T(8,128)(2,1)S(1)} %copy-done.1), custom_call_target="tpu_custom_call" | custom-call | flops 106086400 | bytes 72744960 | tf_op jit(solution)/shard_map/pairs_other/pallas_call | solution.py:205
  22.7 0.0 collective-permute-done.refs_3_
  22.7 0.6 collective-permute-start.1
  23.3 12.5 %pairs_own.1 = (f32[2576,128]{1,0:T(8,128)S(1)}, f32[8,128]{1,0:T(8,128)S(1)}) custom-call(s32[2976]{0:T(1024)S(1)} %get-tuple-element.43.refs_0_, s32[2]{0:T(128)S(1)} %get-tuple-element.44.refs_1_, bf16[148,16,16,128]{3,2,1,0:T(8,128)(2,1)S(1)} %bitcast.9, bf16[12,8,16,128]{3,2,1,0:T(8,128)(2,1)S(1)} %collective-permute-done.refs_3_, ...), custom_call_target="tpu_custom_call" | custom-call | flops 106086400 | bytes 72744960 | tf_op jit(solution)/shard_map/pairs_own/pallas_call | solution.py:205
  35.7 2.3 %collective-permute-done.1.refs_2_ = bf16[2384,128]{1,0:T(8,128)(2,1)S(1)} collective-permute-done((bf16[2384,128]{1,0:T(8,128)(2,1)S(1)}, bf16[2384,128]{1,0:T(8,128)(2,1)S(1)}, u32[]{:S(2)}, u32[]{:S(2)}) %collective-permute-start.1) | collective-permute-done | bytes 610336 | tf_op jit(solution)/shard_map/ppermute | solution.py:528
  38.0 2.1 %combine.1 = (bf16[304,2048]{1,0:T(8,128)(2,1)S(1)}, bf16[304,2048]{1,0:T(8,128)(2,1)S(1)}, f32[8,304]{1,0:T(8,128)S(1)}) custom-call(f32[2576,128]{1,0:T(8,128)S(1)} %get-tuple-element.48.refs_0_, f32[8,128]{1,0:T(8,128)S(1)} %get-tuple-element.49.refs_1_, bf16[2384,128]{1,0:T(8,128)(2,1)S(1)} %collective-permute-done.1.refs_2_), custom_call_target="tpu_custom_call" | custom-call | flops 29884416 | bytes 16777216 | tf_op jit(solution)/shard_map/combine/pallas_call | solution.py:278
  40.1 0.8 %collective-permute-start.2 = (f32[8,304]{1,0:T(8,128)S(1)}, f32[8,304]{1,0:T(8,128)S(1)}, u32[]{:S(2)}, u32[]{:S(2)}) collective-permute-start(f32[8,304]{1,0:T(8,128)S(1)} %get-tuple-element.51), channel_id=1, source_target_pairs={{0,16},{16,0},{1,17},{17,1},{2,18},{18,2},{3,19},{19,3},{4,20},{20... | collective-permute-start | bytes 29192 | tf_op jit(solution)/shard_map/ppermute | solution.py:517
  40.9 1.6 %start_inverse.1 = (f32[304,304]{1,0:T(8,128)S(1)}, bf16[304,304]{1,0:T(8,128)(2,1)S(1)}, bf16[304,304]{1,0:T(8,128)(2,1)S(1)}, f32[2]{0:T(128)S(1)}) custom-call(s32[2,1480]{1,0:T(2,128)S(1)} %bitcast.10), custom_call_target="tpu_custom_call" | custom-call | flops 1073741824 | bytes 8388608 | tf_op jit(solution)/shard_map/start_inverse/pallas_call | solution.py:366
  42.5 1.3 %collective-permute-done.2 = f32[8,304]{1,0:T(8,128)S(1)} collective-permute-done((f32[8,304]{1,0:T(8,128)S(1)}, f32[8,304]{1,0:T(8,128)S(1)}, u32[]{:S(2)}, u32[]{:S(2)}) %collective-permute-start.2) | collective-permute-done | bytes 9760 | tf_op jit(solution)/shard_map/ppermute | solution.py:517
  43.8 2.6 %collective-permute-start.3 = (f32[8,304]{1,0:T(8,128)S(1)}, f32[8,304]{1,0:T(8,128)S(1)}, u32[]{:S(2)}, u32[]{:S(2)}) collective-permute-start(f32[8,304]{1,0:T(8,128)S(1)} %add.28), channel_id=1, source_target_pairs={{0,8},{1,9},{2,10},{3,11},{4,12},{5,13},{6,14},{7,15},{8,0},{9,1},... | collective-permute-start | bytes 29192 | tf_op jit(solution)/shard_map/ppermute | solution.py:517
  46.4 3.9 %go_on_inverse.1 = (f32[304,304]{1,0:T(8,128)S(1)}, f32[2]{0:T(128)S(1)}) custom-call(f32[304,304]{1,0:T(8,128)S(1)} %get-tuple-element.57.refs_0_, bf16[304,304]{1,0:T(8,128)(2,1)S(1)} %get-tuple-element.65.refs_1_, bf16[304,304]{1,0:T(8,128)(2,1)S(1)} %get-tuple-element.66.refs_2_, f32[2]{0:T(128)S(1)} %get-tuple-element.60.refs_3_), custom_call_target="tpu_custom_call" | custom-call | flops 1073741824 | bytes 8388608 | tf_op jit(solution)/shard_map/go_on_inverse/pallas_call | solution.py:366
  50.3 0.0 collective-permute-done.3
  50.3 1.6 %collective-permute-start.4 = (f32[8,304]{1,0:T(8,128)S(1)}, f32[8,304]{1,0:T(8,128)S(1)}, u32[]{:S(2)}, u32[]{:S(2)}) collective-permute-start(f32[8,304]{1,0:T(8,128)S(1)} %add.29), channel_id=1, source_target_pairs={{0,4},{1,5},{2,6},{3,7},{4,0},{5,1},{6,2},{7,3},{8,12},{9,13},{10,... | collective-permute-start | bytes 29192 | tf_op jit(solution)/shard_map/ppermute | solution.py:517
  51.9 3.2 %end_inverse.1 = (bf16[304,304]{1,0:T(8,128)(2,1)S(1)}, bf16[304,304]{1,0:T(8,128)(2,1)S(1)}) custom-call(f32[304,304]{1,0:T(8,128)S(1)} %get-tuple-element.64.refs_0_, bf16[304,304]{1,0:T(8,128)(2,1)S(1)} %get-tuple-element.65.refs_1_, bf16[304,304]{1,0:T(8,128)(2,1)S(1)} %get-tuple-element.66.refs_2_, f32[2]{0:T(128)S(1)} %get-tuple-element.67.refs_3_), custom_call_target="tpu_custom_call" | custom-call | flops 1073741824 | bytes 8388608 | tf_op jit(solution)/shard_map/end_inverse/pallas_call | solution.py:366
  55.1 0.0 collective-permute-done.4
  55.1 1.6 %collective-permute-start.5 = (f32[8,304]{1,0:T(8,128)S(1)}, f32[8,304]{1,0:T(8,128)S(1)}, u32[]{:S(2)}, u32[]{:S(2)}) collective-permute-start(f32[8,304]{1,0:T(8,128)S(1)} %add.30), channel_id=1, source_target_pairs={{0,2},{1,3},{2,0},{3,1},{4,6},{5,7},{6,4},{7,5},{8,10},{9,11},{10,... | collective-permute-start | bytes 29192 | tf_op jit(solution)/shard_map/ppermute | solution.py:517
  56.7 2.4 %solve.1.refs_0_ = f32[16,304,128]{2,1,0:T(8,128)S(1)} custom-call(bf16[304,304]{1,0:T(8,128)(2,1)S(1)} %get-tuple-element.77.inverse_high.refs_2_, bf16[304,304]{1,0:T(8,128)(2,1)S(1)} %get-tuple-element.78.inverse_low.refs_3_, bf16[304,2048]{1,0:T(8,128)(2,1)S(1)} %get-tuple-element.73.high, bf16[304,2048]{1,0:T(8,128)(2,1)S(1)} %get-tuple-element.74.low), custom_call_target="tpu_custom_call" | custom-call | flops 1135607808 | bytes 20971520 | tf_op jit(solution)/shard_map/solve/pallas_call | solution.py:435
  59.2 0.1 collective-permute-start.6
  59.3 1.2 %collective-permute-done.6 = f32[8,304]{1,0:T(8,128)S(1)} collective-permute-done((f32[8,304]{1,0:T(8,128)S(1)}, f32[8,304]{1,0:T(8,128)S(1)}, u32[]{:S(2)}, u32[]{:S(2)}) %collective-permute-start.6) | collective-permute-done | bytes 9760 | tf_op jit(solution)/shard_map/ppermute | solution.py:517
  60.4 2.9 %refine.1 = f32[4736,128]{1,0:T(8,128)} custom-call(f32[16,304,128]{2,1,0:T(8,128)S(1)} %solve.1.refs_0_, f32[8,304]{1,0:T(8,128)S(1)} %add.32.refs_1_, bf16[304,304]{1,0:T(8,128)(2,1)S(1)} %get-tuple-element.77.inverse_high.refs_2_, bf16[304,304]{1,0:T(8,128)(2,1)S(1)} %get-tuple-element.78.inverse_low.refs_3_), custom_call_target="tpu_custom_call" | custom-call | flops 3637248 | bytes 16777216 | tf_op jit(solution)/shard_map/refine/pallas_call | solution.py:495
  (11 shorter events, 0.0 us)
Async XLA Ops:
  1.9 20.8 %collective-permute-start = (bf16[12,8,16,128]{3,2,1,0:T(8,128)(2,1)S(1)}, bf16[12,8,16,128]{3,2,1,0:T(8,128)(2,1)S(1)}, u32[]{:S(2)}, u32[]{:S(2)}) collective-permute-start(bf16[12,8,16,128]{3,2,1,0:T(8,128)(2,1)S(1)} %constant_dynamic-slice_fusion), channel_id=1, source_target_pairs={{0,16},{16,0},{1,17},{17,1},{2,18},{18,2},{3,19},{19,3},{4,20},{20... | collective-permute-start | bytes 1179656 | tf_op jit(solution)/shard_map/ppermute | solution.py:528
  4.9 1.0 %copy-start.1 = (bf16[512,512]{1,0:T(8,128)(2,1)S(1)}, bf16[512,512]{1,0:T(8,128)(2,1)}, u32[]{:S(2)}) copy-start(bf16[512,512]{1,0:T(8,128)(2,1)} %constant.26.clone.refs_2_.refs_4_) | copy-start | bytes 1572868
  5.9 17.4 %copy-start = (bf16[148,32,2,512]{3,2,1,0:T(2,128)(2,1)S(1)}, bf16[148,32,2,512]{3,2,1,0:T(2,128)(2,1)}, u32[]{:S(2)}) copy-start(bf16[148,32,2,512]{3,2,1,0:T(2,128)(2,1)} %param.3) | copy-start | bytes 29097988
  22.7 15.3 %collective-permute-start.1 = (bf16[2384,128]{1,0:T(8,128)(2,1)S(1)}, bf16[2384,128]{1,0:T(8,128)(2,1)S(1)}, u32[]{:S(2)}, u32[]{:S(2)}) collective-permute-start(bf16[2384,128]{1,0:T(8,128)(2,1)S(1)} %get-tuple-element.50), channel_id=1, source_target_pairs={{0,16},{16,0},{1,17},{17,1},{2,18},{18,2},{3,19},{19,3},{4,20},{20... | collective-permute-start | bytes 1830920 | tf_op jit(solution)/shard_map/ppermute | solution.py:528
  23.3 17.6 %copy-start.2 = (s32[1480,2]{0,1:T(2,128)S(1)}, s32[1480,2]{0,1:T(2,128)}, u32[]{:S(2)}) copy-start(s32[1480,2]{0,1:T(2,128)} %param.4) | copy-start | bytes 35524
  40.1 3.7 %collective-permute-start.2 = (f32[8,304]{1,0:T(8,128)S(1)}, f32[8,304]{1,0:T(8,128)S(1)}, u32[]{:S(2)}, u32[]{:S(2)}) collective-permute-start(f32[8,304]{1,0:T(8,128)S(1)} %get-tuple-element.51), channel_id=1, source_target_pairs={{0,16},{16,0},{1,17},{17,1},{2,18},{18,2},{3,19},{19,3},{4,20},{20... | collective-permute-start | bytes 29192 | tf_op jit(solution)/shard_map/ppermute | solution.py:517
  43.8 6.5 %collective-permute-start.3 = (f32[8,304]{1,0:T(8,128)S(1)}, f32[8,304]{1,0:T(8,128)S(1)}, u32[]{:S(2)}, u32[]{:S(2)}) collective-permute-start(f32[8,304]{1,0:T(8,128)S(1)} %add.28), channel_id=1, source_target_pairs={{0,8},{1,9},{2,10},{3,11},{4,12},{5,13},{6,14},{7,15},{8,0},{9,1},... | collective-permute-start | bytes 29192 | tf_op jit(solution)/shard_map/ppermute | solution.py:517
  50.3 4.8 %collective-permute-start.4 = (f32[8,304]{1,0:T(8,128)S(1)}, f32[8,304]{1,0:T(8,128)S(1)}, u32[]{:S(2)}, u32[]{:S(2)}) collective-permute-start(f32[8,304]{1,0:T(8,128)S(1)} %add.29), channel_id=1, source_target_pairs={{0,4},{1,5},{2,6},{3,7},{4,0},{5,1},{6,2},{7,3},{8,12},{9,13},{10,... | collective-permute-start | bytes 29192 | tf_op jit(solution)/shard_map/ppermute | solution.py:517
  55.1 4.0 %collective-permute-start.5 = (f32[8,304]{1,0:T(8,128)S(1)}, f32[8,304]{1,0:T(8,128)S(1)}, u32[]{:S(2)}, u32[]{:S(2)}) collective-permute-start(f32[8,304]{1,0:T(8,128)S(1)} %add.30), channel_id=1, source_target_pairs={{0,2},{1,3},{2,0},{3,1},{4,6},{5,7},{6,4},{7,5},{8,10},{9,11},{10,... | collective-permute-start | bytes 29192 | tf_op jit(solution)/shard_map/ppermute | solution.py:517
  59.2 1.2 %collective-permute-start.6 = (f32[8,304]{1,0:T(8,128)S(1)}, f32[8,304]{1,0:T(8,128)S(1)}, u32[]{:S(2)}, u32[]{:S(2)}) collective-permute-start(f32[8,304]{1,0:T(8,128)S(1)} %add.31), channel_id=1, source_target_pairs={{0,1},{1,0},{2,3},{3,2},{4,5},{5,4},{6,7},{7,6},{8,9},{9,8},{10,11... | collective-permute-start | bytes 29192 | tf_op jit(solution)/shard_map/ppermute | solution.py:517

commit v5 on v4

--- a/solution.py
+++ b/solution.py
@@ -1,6 +1,5 @@
 import jax
 import jax.numpy as jnp
-import numpy as np
 from jax import lax
 from jax.experimental import pallas as pl
 from jax.experimental.pallas import tpu as pltpu
@@ -12,10 +11,10 @@
 GAP = 12
 RIDGE = 0.5
 MAX_STEP = 40
-UNROLL = 8
+UNROLL = 16
 LANES = 128
 SPLIT = 4
-SOME_STEPS = 3
+SOME_STEPS = 2
 PAIR_VMEM = 52 * 1024 * 1024
 OWN_VMEM = 32 * 1024 * 1024
 SMALL_VMEM = 12 * 1024 * 1024
@@ -23,11 +22,12 @@
 NT = (((1,), (1,)), ((), ()))
 
 
-def look_matrix():
-    row = np.arange(SPLIT * LANES)
+def fill_looks(looks):
+    row = lax.broadcasted_iota(jnp.int32, (looks.shape[0], 1), 0)
     lane, sub = row % LANES, row // LANES
     target = (lane % LOOKC) * LANES + sub * (LANES // SPLIT) + lane // LOOKC
-    return (target[:, None] == row[None, :]).astype(np.float32)
+    here = target == lax.broadcasted_iota(jnp.int32, looks.shape, 1)
+    looks[...] = jnp.where(here, 1.0, 0.0).astype(jnp.bfloat16)
 
 
 def split_bf16(value):
@@ -61,9 +61,9 @@
 
 def pair_kernel(pair_count, with_halo, step, *refs):
     if with_halo:
-        (listed, counts, images, halo, looks, series, weights, planes) = refs
+        (listed, counts, images, halo, series, weights, planes, looks) = refs
     else:
-        (pairs, images, looks, series, listed, counts, raw, planes, sems, sums) = refs
+        (pairs, images, series, listed, counts, raw, planes, looks, sems, sums) = refs
     dates = images.shape[0]
     steps = dates // step
     me = lax.axis_index("dates")
@@ -81,6 +81,7 @@
 
     total = series if with_halo else sums
     spare = dates + GAP
+    fill_looks(looks)
     total[...] = jnp.zeros_like(total)
     planes[pl.ds(spare * 128, 128), :] = jnp.zeros((128, LANES), jnp.float32)
 
@@ -178,19 +179,22 @@
     return pl.BlockSpec(memory_space=pl.ANY)
 
 
-def call_pairs(pairs, images, looks, given=None):
+def call_pairs(pairs, images, given=None):
     dates = images.shape[0]
     pair_count = pairs.shape[0]
     step = max(k for k in range(1, MAX_STEP + 1) if dates % k == 0)
     slots = dates + GAP + 1
-    scratch = [pltpu.VMEM((slots * 128, LANES), jnp.float32)]
+    scratch = [
+        pltpu.VMEM((slots * 128, LANES), jnp.float32),
+        pltpu.VMEM((SPLIT * LANES, LOOKC * LANES), jnp.bfloat16),
+    ]
     sums = jax.ShapeDtypeStruct((slots * 16, LANES), jnp.float32)
     if given is not None:
         halo, listed, counts = given
         out_shape = (sums, jax.ShapeDtypeStruct((8, LANES), jnp.float32))
-        in_specs = [in_smem()] * 2 + [in_vmem()] * 3
+        in_specs = [in_smem()] * 2 + [in_vmem()] * 2
         out_specs = (in_vmem(), in_vmem())
-        args = (listed, counts, images, halo, looks)
+        args = (listed, counts, images, halo)
     else:
         out_shape = (
             jax.ShapeDtypeStruct(((dates + 1) * 16, LANES), jnp.bfloat16),
@@ -199,9 +203,9 @@
         )
         scratch = [pltpu.VMEM((dates, 8, 16, LANES), jnp.bfloat16)] + scratch
         scratch += [pltpu.SemaphoreType.DMA((dates // step,)), pltpu.VMEM(sums.shape, sums.dtype)]
-        in_specs = [in_smem(), in_hbm(), in_vmem()]
+        in_specs = [in_smem(), in_hbm()]
         out_specs = (in_vmem(), in_smem(), in_smem())
-        args = (pairs, images, looks)
+        args = (pairs, images)
     return pl.pallas_call(
         lambda *refs: pair_kernel(pair_count, given is not None, step, *refs),
         out_shape=out_shape,
@@ -307,14 +311,15 @@
     scale, error = centre((largest - RIDGE) / (largest + RIDGE))
     first = 2.0 / (largest + RIDGE)
     state[...] = (scale * first) * (2.0 * eye - first * normal)
-    progress[0] = error
-    progress[1] = largest
+    progress[0:1, :] = jnp.broadcast_to(error, (1, LANES))
+    progress[1:2, :] = jnp.broadcast_to(largest, (1, LANES))
 
 
 def go_on_inverse_kernel(last, state, normal_high, normal_low, progress, *refs):
     residual, now_state = refs[-2:]
     eye = unit(state.shape[0])
-    careful = progress[1] > 128.0
+    largest = jnp.max(progress[1:2, :])
+    careful = largest > 128.0
     now_state[...] = state[...]
 
     def step(scale):
@@ -334,7 +339,7 @@
             now_state[...] += scale * (dot32(now, lower, NN) + dot32(rest, upper, NN))
 
     def unfinished(carry):
-        return (carry[0] > 5e-4) & (last | (carry[1] < SOME_STEPS))
+        return (carry[0] > 2e-3) & (last | (carry[1] < SOME_STEPS))
 
     def body(carry):
         error, count = carry
@@ -342,14 +347,14 @@
         step(scale)
         return jnp.maximum(left, 0.05 * error), count + 1
 
-    error, _ = lax.while_loop(unfinished, body, (progress[0], jnp.int32(0)))
+    error, _ = lax.while_loop(unfinished, body, (jnp.max(progress[0:1, :]), jnp.int32(0)))
     if last:
         step(jnp.float32(1.0))
         refs[0][...], refs[1][...] = split_bf16(now_state[...])
     else:
         refs[0][...] = now_state[...]
-        refs[1][0] = error
-        refs[1][1] = progress[1]
+        refs[1][0:1, :] = jnp.broadcast_to(error, (1, LANES))
+        refs[1][1:2, :] = progress[1:2, :]
 
 
 def unit(size):
@@ -366,7 +371,7 @@
     return pl.pallas_call(
         kernel,
         out_shape=out_shape,
-        in_specs=[in_vmem()] * min(len(args), 3) + [in_smem()] * (len(args) - 3),
+        in_specs=[in_vmem()] * len(args),
         out_specs=out_specs,
         scratch_shapes=scratch,
         compiler_params=pltpu.CompilerParams(vmem_limit_bytes=SMALL_VMEM),
@@ -379,11 +384,11 @@
     padded = pad_dates(count)
     full = jax.ShapeDtypeStruct((padded, padded), jnp.float32)
     half = jax.ShapeDtypeStruct((padded, padded), jnp.bfloat16)
-    progress = jax.ShapeDtypeStruct((2,), jnp.float32)
+    progress = jax.ShapeDtypeStruct((2, LANES), jnp.float32)
     return inverse_call(
         start_inverse_kernel,
         (full, half, half, progress),
-        (in_vmem(), in_vmem(), in_vmem(), in_smem()),
+        (in_vmem(),) * 4,
         [],
         "start_inverse",
         (pair_rows,),
@@ -396,19 +401,19 @@
     return inverse_call(
         lambda *refs: go_on_inverse_kernel(last, *refs),
         tuple(jax.ShapeDtypeStruct(like.shape, like.dtype) for like in out_shape),
-        (in_vmem(), in_vmem() if last else in_smem()),
+        (in_vmem(),) * 2,
         [full, full],
         "end_inverse" if last else "go_on_inverse",
         (state, normal_high, normal_low, progress),
     )
 
 
-def solve_kernel(inverse_high, inverse_low, high, low, series):
+def solve_kernel(part, inverse_high, inverse_low, high, low, series):
     padded = high.shape[0]
     lane = lax.broadcasted_iota(jnp.int32, (padded, LANES), 1)
     width = LANES // SPLIT
-    for group in range(4):
-        cols = pl.ds(group * SPLIT * LANES, SPLIT * LANES)
+    for half in range(2):
+        cols = pl.ds((part * 2 + half) * SPLIT * LANES, SPLIT * LANES)
         solved = (
             dot32(inverse_high[...], high[:, cols], NN)
             + dot32(inverse_high[...], low[:, cols], NN)
@@ -425,16 +430,15 @@
                     swapped[k] = jnp.where(even, first, pltpu.roll(second, shift, 1))
                     swapped[k | bit] = jnp.where(even, pltpu.roll(first, LANES - shift, 1), second)
             blocks = swapped
-        part, half = group // 2, group % 2
         for k in range(SPLIT):
-            series[(half * SPLIT + k) * 2 + part] = blocks[k]
-
-
-def call_solve(inverse, values):
+            series[half * SPLIT + k] = blocks[k]
+
+
+def call_solve(part, inverse, values):
     padded = values[0].shape[0]
     return pl.pallas_call(
-        solve_kernel,
-        out_shape=jax.ShapeDtypeStruct((16, padded, LANES), jnp.float32),
+        lambda *refs: solve_kernel(part, *refs),
+        out_shape=jax.ShapeDtypeStruct((8, padded, LANES), jnp.float32),
         in_specs=[in_vmem()] * 4,
         out_specs=in_vmem(),
         compiler_params=pltpu.CompilerParams(vmem_limit_bytes=SMALL_VMEM),
@@ -446,8 +450,8 @@
 
 
 def refine_kernel(count, row_total, col_total, *refs):
-    (series, moments, inverse_high, inverse_low, refined) = refs
-    padded = series.shape[1]
+    (*series, moments, inverse_high, inverse_low, refined) = refs
+    padded = moments.shape[1]
     normal = [
         [moments[at : at + 1, count + k : count + k + 1] for k in range(3)] for at in range(3)
     ]
@@ -486,7 +490,7 @@
         level = level + along_x * x_row
         for row in range(8):
             y = centred(row_start + row, row_total)
-            refined[pl.ds(row * 2 + part, count, stride=16), :] = series[row * 2 + part, :count] - (
+            refined[pl.ds(row * 2 + part, count, stride=16), :] = series[part][row, :count] - (
                 level + along_y * y
             )
 
@@ -495,22 +499,21 @@
     return pl.pallas_call(
         lambda *refs: refine_kernel(count, row_total, col_total, *refs),
         out_shape=jax.ShapeDtypeStruct((count * 16, LANES), jnp.float32),
-        in_specs=[in_vmem()] * 4,
+        in_specs=[in_vmem()] * 5,
         out_specs=in_vmem(),
         compiler_params=pltpu.CompilerParams(vmem_limit_bytes=SMALL_VMEM),
         cost_estimate=pl.CostEstimate(flops=count * 16 * LANES * 6, bytes_accessed=16 << 20, transcendentals=0),
         name="refine",
-    )(series, moments, *inverse)
-
-
-def sum_beside(value, work):
+    )(*series, moments, *inverse)
+
+
+def sum_beside(value, state, work):
     cols = lax.axis_size("cols")
     pairings = [("dates", [(0, 1), (1, 0)])]
     bit = cols // 2
     while bit and not cols & (cols - 1):
         pairings.append(("cols", [(at, at ^ bit) for at in range(cols)]))
         bit //= 2
-    state = ()
     for at in range(max(len(pairings), len(work))):
         value, state = lax.optimization_barrier((value, state))
         if at < len(pairings):
@@ -549,27 +552,27 @@
     )
     edge, packed = lax.optimization_barrier((edge, packed))
     halo = swap_dates(edge)
-    looks = jnp.asarray(look_matrix(), jnp.bfloat16)
-    other, listed, counts = call_pairs(packed, images, looks)
+    other, listed, counts = call_pairs(packed, images)
     other, halo = lax.optimization_barrier((other, halo))
     other = swap_dates(other)
-    own, own_weights = call_pairs(packed, images, looks, (halo, listed, counts))
+    own, own_weights = call_pairs(packed, images, (halo, listed, counts))
+    own, pair_rows = lax.optimization_barrier((own, pair_list.T))
+    started = start_inverse(pair_rows, dates * 2)
+    own, started = lax.optimization_barrier((own, started))
     high, lowpart, moments = call_combine(own, own_weights, other, dates, row_total, col_total)
 
-    def first(state):
-        return start_inverse(pair_list.T, dates * 2)
-
-    def second(state):
+    def go_on(state):
         values, progress = go_on_inverse(*state, last=False)
         return (values,) + state[1:3] + (progress,)
 
-    def third(state):
-        return go_on_inverse(*state, last=True)
-
-    def fourth(state):
-        return state, call_solve(state, (high, lowpart))
-
-    moments, (inverse, series) = sum_beside(moments, [first, second, third, fourth])
+    def end(state):
+        return go_on_inverse(*state, last=True), ()
+
+    def solve(state):
+        inverse, solved = state
+        return inverse, solved + (call_solve(len(solved), inverse, (high, lowpart)),)
+
+    moments, (inverse, series) = sum_beside(moments, started, [go_on, go_on, end, solve, solve])
     refined = call_refine(series, moments, inverse, dates * 2, row_total, col_total)
     return refined.reshape(dates * 2, half, 2, LANES)
 

time: 64 us -> 59 us (0.922)
  Pallas kernels: 45.3 us -> 43.6 us
  local copies, waits for them, and re-layouts: 2.08 us -> 1.04 us
  waiting for transfers between devices: 4.72 us -> 3.77 us
  starting transfers between devices: 10.3 us -> 9.53 us
    pallas_call x4 -> x6, Pallas kernels: 11.1 us -> 9.65 us  [the longest x4 6.76 us: inverse_call(): pl.pallas_call(kernel, out_shape=out_shape, in_specs=[in_vmem()] * len(ar...]
    unnamed x6 -> x4, local copies, waits for them, and re-layouts: 1.05 us -> 0.01 us
    ppermute x2, waiting for transfers between devices: 2.25 us -> 1.48 us  [swap_dates(): return lax.ppermute(value, 'dates', [(0, 1), (1, 0)])]
  transfers between devices with their start and end apart: 7 -> 7, of which waited for: 3 -> 5; matrix products, arithmetic and copies ran while one was open for 0% -> 0% of each run, Pallas kernels for 64% -> 65%
where the time goes in v5:
time: 59 us; the launch traced here: 58.9 us
  Pallas kernels  43.6 us (74%)
  starting transfers between devices  9.53 us (16%)
  waiting for transfers between devices  3.77 us (6%)
  local copies, waits for them, and re-layouts  1.04 us (2%)
  other arithmetic  0.86 us (1%)
    pallas_call x2, Pallas kernels, call_pairs(): pl.pallas_call(lambda *refs: pair_kernel(pair_count, given is not None, s...  28.8 us
    pallas_call x4, Pallas kernels, inverse_call(): pl.pallas_call(kernel, out_shape=out_shape, in_specs=[in_vmem()] * len(ar...  6.76 us
    ppermute x5, starting transfers between devices, sum_beside(): other = lax.ppermute(value, *pairings[at])  6.25 us
    ppermute x2, starting transfers between devices, swap_dates(): return lax.ppermute(value, 'dates', [(0, 1), (1, 0)])  3.28 us
    pallas_call x1, Pallas kernels, call_refine(): pl.pallas_call(lambda *refs: refine_kernel(count, row_total, col_total, *...  3.05 us
    pallas_call x2, Pallas kernels, call_solve(): pl.pallas_call(lambda *refs: solve_kernel(part, *refs), out_shape=jax.Sha...  2.89 us
    ppermute x5, waiting for transfers between devices, sum_beside(): other = lax.ppermute(value, *pairings[at])  2.28 us
    pallas_call x1, Pallas kernels, call_combine(): pl.pallas_call(lambda *refs: combine_kernel(dates, row_total, col_total,...  2.08 us
  transfers between devices with their start and end apart: 7, of which 5 were waited for; matrix products, arithmetic and copies ran while one was open for 0% of the time, Pallas kernels for 65%

profile of v5, /device:TPU:0, one launch (start us, length us, event | category | flops | bytes accessed | tf_op | source)
XLA Modules:
  0.0 58.9 jit_solution(10845523941448905563)
XLA Ops:
  0.0 0.8 %fusion.refs_0_ = s32[1480]{0:T(1024)S(1)} fusion(s32[1480,2]{0,1:T(2,128)} %param.3, s32[]{:T(128)S(6)} %mul.11, s32[]{:T(128)S(6)} %add.27, s32[]{:T(128)S(6)} %mul.10), kind=kLoop, calls=%fused_computation.5 | loop fusion | flops 29600 | bytes 17772 | tf_op jit(solution)/shard_map/jit(_where)/select_n | solution.py:548
  0.8 1.0 %constant_dynamic-slice_fusion = bf16[12,8,16,128]{3,2,1,0:T(8,128)(2,1)S(1)} fusion(bf16[148,16,16,128]{3,2,1,0:T(8,128)(2,1)} %bitcast.7, s32[]{:T(128)S(6)} %select_n.10, s32[]{:T(128)S(6)} %select_n.11), kind=kLoop, calls=%fused_computation.10 | loop fusion | bytes 786440 | tf_op jit(solution)/shard_map/dynamic_slice | solution.py:550
  1.9 3.0 %collective-permute-start = (bf16[12,8,16,128]{3,2,1,0:T(8,128)(2,1)S(1)}, bf16[12,8,16,128]{3,2,1,0:T(8,128)(2,1)S(1)}, u32[]{:S(2)}, u32[]{:S(2)}) collective-permute-start(bf16[12,8,16,128]{3,2,1,0:T(8,128)(2,1)S(1)} %constant_dynamic-slice_fusion), channel_id=1, source_target_pairs={{0,16},{16,0},{1,17},{17,1},{2,18},{18,2},{3,19},{19,3},{4,20},{20... | collective-permute-start | bytes 1179656 | tf_op jit(solution)/shard_map/ppermute | solution.py:531
  4.9 16.3 %pairs_other.1 = (bf16[2384,128]{1,0:T(8,128)(2,1)S(1)}, s32[2992]{0:T(1024)S(1)}, s32[2]{0:T(128)S(1)}) custom-call(s32[1480]{0:T(1024)S(1)} %fusion.refs_0_, bf16[148,16,16,128]{3,2,1,0:T(8,128)(2,1)} %bitcast.8), custom_call_target="tpu_custom_call" | custom-call | flops 106086400 | bytes 72744960 | tf_op jit(solution)/shard_map/pairs_other/pallas_call | solution.py:209
  21.2 0.0 collective-permute-done.refs_3_
  21.2 0.3 collective-permute-start.1
  21.5 12.5 %pairs_own.1 = (f32[2576,128]{1,0:T(8,128)S(1)}, f32[8,128]{1,0:T(8,128)S(1)}) custom-call(s32[2992]{0:T(1024)S(1)} %get-tuple-element.57.refs_0_, s32[2]{0:T(128)S(1)} %get-tuple-element.58.refs_1_, bf16[148,16,16,128]{3,2,1,0:T(8,128)(2,1)S(1)} %bitcast.9, bf16[12,8,16,128]{3,2,1,0:T(8,128)(2,1)S(1)} %collective-permute-done.refs_3_), custom_call_target="tpu_custom_call" | custom-call | flops 106086400 | bytes 72744960 | tf_op jit(solution)/shard_map/pairs_own/pallas_call | solution.py:209
  34.0 1.0 %start_inverse.1 = (f32[304,304]{1,0:T(8,128)S(1)}, bf16[304,304]{1,0:T(8,128)(2,1)S(1)}, bf16[304,304]{1,0:T(8,128)(2,1)S(1)}, f32[2,128]{1,0:T(2,128)S(1)}) custom-call(s32[2,1480]{1,0:T(2,128)S(1)} %bitcast.10), custom_call_target="tpu_custom_call" | custom-call | flops 1073741824 | bytes 8388608 | tf_op jit(solution)/shard_map/start_inverse/pallas_call | solution.py:371
  35.0 1.5 %collective-permute-done.1.refs_2_ = bf16[2384,128]{1,0:T(8,128)(2,1)S(1)} collective-permute-done((bf16[2384,128]{1,0:T(8,128)(2,1)S(1)}, bf16[2384,128]{1,0:T(8,128)(2,1)S(1)}, u32[]{:S(2)}, u32[]{:S(2)}) %collective-permute-start.1) | collective-permute-done | bytes 610336 | tf_op jit(solution)/shard_map/ppermute | solution.py:531
  36.5 2.1 %combine.1 = (bf16[304,2048]{1,0:T(8,128)(2,1)S(1)}, bf16[304,2048]{1,0:T(8,128)(2,1)S(1)}, f32[8,304]{1,0:T(8,128)S(1)}) custom-call(f32[2576,128]{1,0:T(8,128)S(1)} %get-tuple-element.69.refs_0_, f32[8,128]{1,0:T(8,128)S(1)} %get-tuple-element.70.refs_1_, bf16[2384,128]{1,0:T(8,128)(2,1)S(1)} %collective-permute-done.1.refs_2_), custom_call_target="tpu_custom_call" | custom-call | flops 29884416 | bytes 16777216 | tf_op jit(solution)/shard_map/combine/pallas_call | solution.py:282
  38.6 0.6 collective-permute-start.2
  39.2 2.0 %go_on_inverse.2 = (f32[304,304]{1,0:T(8,128)S(1)}, f32[2,128]{1,0:T(2,128)S(1)}) custom-call(f32[304,304]{1,0:T(8,128)S(1)} %get-tuple-element.78.refs_0_, bf16[304,304]{1,0:T(8,128)(2,1)S(1)} %get-tuple-element.93.refs_1_, bf16[304,304]{1,0:T(8,128)(2,1)S(1)} %get-tuple-element.94.refs_2_, f32[2,128]{1,0:T(2,128)S(1)} %get-tuple-element.81.refs_3_), custom_call_target="tpu_custom_call" | custom-call | flops 1073741824 | bytes 8388608 | tf_op jit(solution)/shard_map/go_on_inverse/pallas_call | solution.py:371
  41.2 1.1 %collective-permute-done.2 = f32[8,304]{1,0:T(8,128)S(1)} collective-permute-done((f32[8,304]{1,0:T(8,128)S(1)}, f32[8,304]{1,0:T(8,128)S(1)}, u32[]{:S(2)}, u32[]{:S(2)}) %collective-permute-start.2) | collective-permute-done | bytes 9760 | tf_op jit(solution)/shard_map/ppermute | solution.py:520
  42.3 2.6 %collective-permute-start.3 = (f32[8,304]{1,0:T(8,128)S(1)}, f32[8,304]{1,0:T(8,128)S(1)}, u32[]{:S(2)}, u32[]{:S(2)}) collective-permute-start(f32[8,304]{1,0:T(8,128)S(1)} %add.28), channel_id=1, source_target_pairs={{0,8},{1,9},{2,10},{3,11},{4,12},{5,13},{6,14},{7,15},{8,0},{9,1},... | collective-permute-start | bytes 29192 | tf_op jit(solution)/shard_map/ppermute | solution.py:520
  44.9 1.8 %go_on_inverse.3 = (f32[304,304]{1,0:T(8,128)S(1)}, f32[2,128]{1,0:T(2,128)S(1)}) custom-call(f32[304,304]{1,0:T(8,128)S(1)} %get-tuple-element.85.refs_0_, bf16[304,304]{1,0:T(8,128)(2,1)S(1)} %get-tuple-element.93.refs_1_, bf16[304,304]{1,0:T(8,128)(2,1)S(1)} %get-tuple-element.94.refs_2_, f32[2,128]{1,0:T(2,128)S(1)} %get-tuple-element.88.refs_3_), custom_call_target="tpu_custom_call" | custom-call | flops 1073741824 | bytes 8388608 | tf_op jit(solution)/shard_map/go_on_inverse/pallas_call | solution.py:371
  46.8 0.2 collective-permute-done.3
  46.9 1.6 %collective-permute-start.4 = (f32[8,304]{1,0:T(8,128)S(1)}, f32[8,304]{1,0:T(8,128)S(1)}, u32[]{:S(2)}, u32[]{:S(2)}) collective-permute-start(f32[8,304]{1,0:T(8,128)S(1)} %add.29), channel_id=1, source_target_pairs={{0,4},{1,5},{2,6},{3,7},{4,0},{5,1},{6,2},{7,3},{8,12},{9,13},{10,... | collective-permute-start | bytes 29192 | tf_op jit(solution)/shard_map/ppermute | solution.py:520
  48.5 1.9 %end_inverse.1 = (bf16[304,304]{1,0:T(8,128)(2,1)S(1)}, bf16[304,304]{1,0:T(8,128)(2,1)S(1)}) custom-call(f32[304,304]{1,0:T(8,128)S(1)} %get-tuple-element.92.refs_0_, bf16[304,304]{1,0:T(8,128)(2,1)S(1)} %get-tuple-element.93.refs_1_, bf16[304,304]{1,0:T(8,128)(2,1)S(1)} %get-tuple-element.94.refs_2_, f32[2,128]{1,0:T(2,128)S(1)} %get-tuple-element.95.refs_3_), custom_call_target="tpu_custom_call" | custom-call | flops 1073741824 | bytes 8388608 | tf_op jit(solution)/shard_map/end_inverse/pallas_call | solution.py:371
  50.4 0.3 collective-permute-done.4
  50.6 1.5 %collective-permute-start.5 = (f32[8,304]{1,0:T(8,128)S(1)}, f32[8,304]{1,0:T(8,128)S(1)}, u32[]{:S(2)}, u32[]{:S(2)}) collective-permute-start(f32[8,304]{1,0:T(8,128)S(1)} %add.30), channel_id=1, source_target_pairs={{0,2},{1,3},{2,0},{3,1},{4,6},{5,7},{6,4},{7,5},{8,10},{9,11},{10,... | collective-permute-start | bytes 29192 | tf_op jit(solution)/shard_map/ppermute | solution.py:520
  52.2 1.4 %solve.2.refs_0_ = f32[8,304,128]{2,1,0:T(8,128)S(1)} custom-call(bf16[304,304]{1,0:T(8,128)(2,1)S(1)} %get-tuple-element.104.refs_0_.refs_3_, bf16[304,304]{1,0:T(8,128)(2,1)S(1)} %get-tuple-element.105.refs_1_.refs_4_, bf16[304,2048]{1,0:T(8,128)(2,1)S(1)} %get-tuple-element.101.refs_2_, bf16[304,2048]{1,0:T(8,128)(2,1)S(1)} %get-tuple-element.102.refs_3_), custom_call_target="tpu_custom_call" | custom-call | flops 1135607808 | bytes 20971520 | tf_op jit(solution)/shard_map/solve/pallas_call | solution.py:439
  53.6 0.7 %collective-permute-done.5 = f32[8,304]{1,0:T(8,128)S(1)} collective-permute-done((f32[8,304]{1,0:T(8,128)S(1)}, f32[8,304]{1,0:T(8,128)S(1)}, u32[]{:S(2)}, u32[]{:S(2)}) %collective-permute-start.5) | collective-permute-done | bytes 9760 | tf_op jit(solution)/shard_map/ppermute | solution.py:520
  54.3 1.4 %solve.3.refs_1_ = f32[8,304,128]{2,1,0:T(8,128)S(1)} custom-call(bf16[304,304]{1,0:T(8,128)(2,1)S(1)} %get-tuple-element.104.refs_0_.refs_3_, bf16[304,304]{1,0:T(8,128)(2,1)S(1)} %get-tuple-element.105.refs_1_.refs_4_, bf16[304,2048]{1,0:T(8,128)(2,1)S(1)} %get-tuple-element.101.refs_2_, bf16[304,2048]{1,0:T(8,128)(2,1)S(1)} %get-tuple-element.102.refs_3_), custom_call_target="tpu_custom_call" | custom-call | flops 1135607808 | bytes 20971520 | tf_op jit(solution)/shard_map/solve/pallas_call | solution.py:439
  55.8 3.0 %refine.1 = f32[4736,128]{1,0:T(8,128)} custom-call(f32[8,304,128]{2,1,0:T(8,128)S(1)} %solve.2.refs_0_, f32[8,304,128]{2,1,0:T(8,128)S(1)} %solve.3.refs_1_, f32[8,304]{1,0:T(8,128)S(1)} %add.32.refs_2_, bf16[304,304]{1,0:T(8,128)(2,1)S(1)} %get-tuple-element.104.refs_0_.refs_3_, bf16[304,304]{1,0:T(8,128)(2,1)S(1)} %get-tuple-element.105.refs_1_.refs_4_), custom_call_target="tpu_custom_call" | custom-call | flops 3637248 | bytes 16777216 | tf_op jit(solution)/shard_map/refine/pallas_call | solution.py:499
  (11 shorter events, 0.0 us)
Async XLA Ops:
  1.9 19.3 %collective-permute-start = (bf16[12,8,16,128]{3,2,1,0:T(8,128)(2,1)S(1)}, bf16[12,8,16,128]{3,2,1,0:T(8,128)(2,1)S(1)}, u32[]{:S(2)}, u32[]{:S(2)}) collective-permute-start(bf16[12,8,16,128]{3,2,1,0:T(8,128)(2,1)S(1)} %constant_dynamic-slice_fusion), channel_id=1, source_target_pairs={{0,16},{16,0},{1,17},{17,1},{2,18},{18,2},{3,19},{19,3},{4,20},{20... | collective-permute-start | bytes 1179656 | tf_op jit(solution)/shard_map/ppermute | solution.py:531
  4.9 16.6 %copy-start = (bf16[148,32,2,512]{3,2,1,0:T(2,128)(2,1)S(1)}, bf16[148,32,2,512]{3,2,1,0:T(2,128)(2,1)}, u32[]{:S(2)}) copy-start(bf16[148,32,2,512]{3,2,1,0:T(2,128)(2,1)} %param.2) | copy-start | bytes 29097988
  21.2 15.3 %collective-permute-start.1 = (bf16[2384,128]{1,0:T(8,128)(2,1)S(1)}, bf16[2384,128]{1,0:T(8,128)(2,1)S(1)}, u32[]{:S(2)}, u32[]{:S(2)}) collective-permute-start(bf16[2384,128]{1,0:T(8,128)(2,1)S(1)} %get-tuple-element.71), channel_id=1, source_target_pairs={{0,16},{16,0},{1,17},{17,1},{2,18},{18,2},{3,19},{19,3},{4,20},{20... | collective-permute-start | bytes 1830920 | tf_op jit(solution)/shard_map/ppermute | solution.py:531
  21.5 12.5 %copy-start.1 = (s32[1480,2]{0,1:T(2,128)S(1)}, s32[1480,2]{0,1:T(2,128)}, u32[]{:S(2)}) copy-start(s32[1480,2]{0,1:T(2,128)} %param.3) | copy-start | bytes 35524
  38.6 3.7 %collective-permute-start.2 = (f32[8,304]{1,0:T(8,128)S(1)}, f32[8,304]{1,0:T(8,128)S(1)}, u32[]{:S(2)}, u32[]{:S(2)}) collective-permute-start(f32[8,304]{1,0:T(8,128)S(1)} %get-tuple-element.77), channel_id=1, source_target_pairs={{0,16},{16,0},{1,17},{17,1},{2,18},{18,2},{3,19},{19,3},{4,20},{20... | collective-permute-start | bytes 29192 | tf_op jit(solution)/shard_map/ppermute | solution.py:520
  42.3 4.6 %collective-permute-start.3 = (f32[8,304]{1,0:T(8,128)S(1)}, f32[8,304]{1,0:T(8,128)S(1)}, u32[]{:S(2)}, u32[]{:S(2)}) collective-permute-start(f32[8,304]{1,0:T(8,128)S(1)} %add.28), channel_id=1, source_target_pairs={{0,8},{1,9},{2,10},{3,11},{4,12},{5,13},{6,14},{7,15},{8,0},{9,1},... | collective-permute-start | bytes 29192 | tf_op jit(solution)/shard_map/ppermute | solution.py:520
  46.9 3.7 %collective-permute-start.4 = (f32[8,304]{1,0:T(8,128)S(1)}, f32[8,304]{1,0:T(8,128)S(1)}, u32[]{:S(2)}, u32[]{:S(2)}) collective-permute-start(f32[8,304]{1,0:T(8,128)S(1)} %add.29), channel_id=1, source_target_pairs={{0,4},{1,5},{2,6},{3,7},{4,0},{5,1},{6,2},{7,3},{8,12},{9,13},{10,... | collective-permute-start | bytes 29192 | tf_op jit(solution)/shard_map/ppermute | solution.py:520
  50.6 3.7 %collective-permute-start.5 = (f32[8,304]{1,0:T(8,128)S(1)}, f32[8,304]{1,0:T(8,128)S(1)}, u32[]{:S(2)}, u32[]{:S(2)}) collective-permute-start(f32[8,304]{1,0:T(8,128)S(1)} %add.30), channel_id=1, source_target_pairs={{0,2},{1,3},{2,0},{3,1},{4,6},{5,7},{6,4},{7,5},{8,10},{9,11},{10,... | collective-permute-start | bytes 29192 | tf_op jit(solution)/shard_map/ppermute | solution.py:520
  54.3 1.5 %collective-permute-start.6 = (f32[8,304]{1,0:T(8,128)S(1)}, f32[8,304]{1,0:T(8,128)S(1)}, u32[]{:S(2)}, u32[]{:S(2)}) collective-permute-start(f32[8,304]{1,0:T(8,128)S(1)} %add.31), channel_id=1, source_target_pairs={{0,1},{1,0},{2,3},{3,2},{4,5},{5,4},{6,7},{7,6},{8,9},{9,8},{10,11... | collective-permute-start | bytes 29192 | tf_op jit(solution)/shard_map/ppermute | solution.py:520

commit v6 on v5

--- a/solution.py
+++ b/solution.py
@@ -154,13 +154,20 @@
     if with_halo:
         weights[...] = power * (scale * scale / float(pair_count))
     else:
-        def narrow(date, carry):
-            value = sums[pl.ds(pl.multiple_of((own_slot + date) * 16, 16), 16), :] * scale + carry
-            rounded = value.astype(jnp.bfloat16)
-            series[pl.ds(pl.multiple_of(date * 16, 16), 16), :] = rounded
-            return value - rounded.astype(jnp.float32)
-
-        lax.fori_loop(0, dates, narrow, jnp.zeros((16, LANES), jnp.float32), unroll=4)
+        chains = 4 if dates % 4 == 0 else 1
+        length = dates // chains
+
+        def narrow(at, carries):
+            left = []
+            for chain, carry in enumerate(carries):
+                date = chain * length + at
+                value = sums[pl.ds(pl.multiple_of((own_slot + date) * 16, 16), 16), :] * scale + carry
+                rounded = value.astype(jnp.bfloat16)
+                series[pl.ds(pl.multiple_of(date * 16, 16), 16), :] = rounded
+                left.append(value - rounded.astype(jnp.float32))
+            return tuple(left)
+
+        lax.fori_loop(0, length, narrow, (jnp.zeros((16, LANES), jnp.float32),) * chains)
         high, low = split_bf16(power * (scale * scale / float(pair_count)))
         series[pl.ds(dates * 16, 16), :] = jnp.concatenate(
             [high.astype(jnp.float32), low.astype(jnp.float32)], axis=0
@@ -450,7 +457,7 @@
 
 
 def refine_kernel(count, row_total, col_total, *refs):
-    (*series, moments, inverse_high, inverse_low, refined) = refs
+    (*series, moments, inverse_high, inverse_low, refined, held, sems) = refs
     padded = moments.shape[1]
     normal = [
         [moments[at : at + 1, count + k : count + k + 1] for k in range(3)] for at in range(3)
@@ -482,17 +489,27 @@
     lane = lax.broadcasted_iota(jnp.int32, (1, LANES), 1)
     x_row = centred(LANES * lax.axis_index("cols") + lane, col_total)
     row_start = 8 * lax.axis_index("dates")
-    for part in range(2):
-        level, along_y, along_x = (
-            jnp.broadcast_to(ramps[:, part * 3 + at : part * 3 + at + 1], (count, LANES))
-            for at in range(3)
-        )
-        level = level + along_x * x_row
-        for row in range(8):
-            y = centred(row_start + row, row_total)
-            refined[pl.ds(row * 2 + part, count, stride=16), :] = series[part][row, :count] - (
-                level + along_y * y
+    middle = (count // 2 + 7) // 8 * 8
+    copies = []
+    for at, (start, size) in enumerate(((0, middle), (middle, count - middle))):
+        for part in range(2):
+            level, along_y, along_x = (
+                jnp.broadcast_to(
+                    ramps[start : start + size, part * 3 + k : part * 3 + k + 1], (size, LANES)
+                )
+                for k in range(3)
             )
+            level = level + along_x * x_row
+            for row in range(8):
+                y = centred(row_start + row, row_total)
+                held[pl.ds(start * 16 + row * 2 + part, size, stride=16), :] = series[part][
+                    row, start : start + size
+                ] - (level + along_y * y)
+        rows = pl.ds(start * 16, size * 16)
+        copies.append(pltpu.make_async_copy(held.at[rows], refined.at[rows], sems.at[at]))
+        copies[-1].start()
+    for copy in copies:
+        copy.wait()
 
 
 def call_refine(series, moments, inverse, count, row_total, col_total):
@@ -500,7 +517,8 @@
         lambda *refs: refine_kernel(count, row_total, col_total, *refs),
         out_shape=jax.ShapeDtypeStruct((count * 16, LANES), jnp.float32),
         in_specs=[in_vmem()] * 5,
-        out_specs=in_vmem(),
+        out_specs=in_hbm(),
+        scratch_shapes=[pltpu.VMEM((count * 16, LANES), jnp.float32), pltpu.SemaphoreType.DMA((2,))],
         compiler_params=pltpu.CompilerParams(vmem_limit_bytes=SMALL_VMEM),
         cost_estimate=pl.CostEstimate(flops=count * 16 * LANES * 6, bytes_accessed=16 << 20, transcendentals=0),
         name="refine",

time: 59 us -> 58.3 us (0.988)
  starting transfers between devices: 9.53 us -> 11.3 us
  waiting for transfers between devices: 3.77 us -> 2.34 us
  Pallas kernels: 43.6 us -> 42.2 us
    pallas_call x2, Pallas kernels: 28.8 us -> 27.9 us  [call_pairs(): pl.pallas_call(lambda *refs: pair_kernel(pair_count, given is not None, s...]
    ppermute x2, starting transfers between devices: 3.28 us -> 4.16 us  [swap_dates(): return lax.ppermute(value, 'dates', [(0, 1), (1, 0)])]
    ppermute x5, starting transfers between devices: 6.25 us -> 7.12 us  [sum_beside(): other = lax.ppermute(value, *pairings[at])]
    ppermute x5, waiting for transfers between devices: 2.28 us -> 1.41 us  [sum_beside(): other = lax.ppermute(value, *pairings[at])]
where the time goes in v6:
time: 58.3 us; the launch traced here: 58 us
  Pallas kernels  42.2 us (72%)
  starting transfers between devices  11.3 us (19%)
  waiting for transfers between devices  2.34 us (4%)
  local copies, waits for them, and re-layouts  1.04 us (2%)
  other arithmetic  0.86 us (1%)
    pallas_call x2, Pallas kernels, call_pairs(): pl.pallas_call(lambda *refs: pair_kernel(pair_count, given is not None, s...  27.9 us
    ppermute x5, starting transfers between devices, sum_beside(): other = lax.ppermute(value, *pairings[at])  7.12 us
    pallas_call x4, Pallas kernels, inverse_call(): pl.pallas_call(kernel, out_shape=out_shape, in_specs=[in_vmem()] * len(ar...  6.75 us
    ppermute x2, starting transfers between devices, swap_dates(): return lax.ppermute(value, 'dates', [(0, 1), (1, 0)])  4.16 us
    pallas_call x2, Pallas kernels, call_solve(): pl.pallas_call(lambda *refs: solve_kernel(part, *refs), out_shape=jax.Sha...  2.9 us
    pallas_call x1, Pallas kernels, call_refine(): pl.pallas_call(lambda *refs: refine_kernel(count, row_total, col_total, *...  2.62 us
    pallas_call x1, Pallas kernels, call_combine(): pl.pallas_call(lambda *refs: combine_kernel(dates, row_total, col_total,...  2.08 us
    ppermute x5, waiting for transfers between devices, sum_beside(): other = lax.ppermute(value, *pairings[at])  1.41 us
  transfers between devices with their start and end apart: 7, of which 5 were waited for; matrix products, arithmetic and copies ran while one was open for 0% of the time, Pallas kernels for 65%

profile of v6, /device:TPU:0, one launch (start us, length us, event | category | flops | bytes accessed | tf_op | source)
XLA Modules:
  0.0 58.0 jit_solution(12126875265811694245)
XLA Ops:
  0.0 0.8 %fusion.refs_0_ = s32[1480]{0:T(1024)S(1)} fusion(s32[1480,2]{0,1:T(2,128)} %param.3, s32[]{:T(128)S(6)} %mul.11, s32[]{:T(128)S(6)} %add.27, s32[]{:T(128)S(6)} %mul.10), kind=kLoop, calls=%fused_computation.5 | loop fusion | flops 29600 | bytes 17772 | tf_op jit(solution)/shard_map/jit(_where)/select_n | solution.py:566
  0.8 1.0 %constant_dynamic-slice_fusion = bf16[12,8,16,128]{3,2,1,0:T(8,128)(2,1)S(1)} fusion(bf16[148,16,16,128]{3,2,1,0:T(8,128)(2,1)} %bitcast.7, s32[]{:T(128)S(6)} %select_n.10, s32[]{:T(128)S(6)} %select_n.11), kind=kLoop, calls=%fused_computation.10 | loop fusion | bytes 786440 | tf_op jit(solution)/shard_map/dynamic_slice | solution.py:568
  1.9 3.0 %collective-permute-start = (bf16[12,8,16,128]{3,2,1,0:T(8,128)(2,1)S(1)}, bf16[12,8,16,128]{3,2,1,0:T(8,128)(2,1)S(1)}, u32[]{:S(2)}, u32[]{:S(2)}) collective-permute-start(bf16[12,8,16,128]{3,2,1,0:T(8,128)(2,1)S(1)} %constant_dynamic-slice_fusion), channel_id=1, source_target_pairs={{0,16},{16,0},{1,17},{17,1},{2,18},{18,2},{3,19},{19,3},{4,20},{20... | collective-permute-start | bytes 1179656 | tf_op jit(solution)/shard_map/ppermute | solution.py:549
  4.9 15.7 %pairs_other.1 = (bf16[2384,128]{1,0:T(8,128)(2,1)S(1)}, s32[2992]{0:T(1024)S(1)}, s32[2]{0:T(128)S(1)}) custom-call(s32[1480]{0:T(1024)S(1)} %fusion.refs_0_, bf16[148,16,16,128]{3,2,1,0:T(8,128)(2,1)} %bitcast.8), custom_call_target="tpu_custom_call" | custom-call | flops 106086400 | bytes 72744960 | tf_op jit(solution)/shard_map/pairs_other/pallas_call | solution.py:216
  20.6 1.2 %collective-permute-start.1 = (bf16[2384,128]{1,0:T(8,128)(2,1)S(1)}, bf16[2384,128]{1,0:T(8,128)(2,1)S(1)}, u32[]{:S(2)}, u32[]{:S(2)}) collective-permute-start(bf16[2384,128]{1,0:T(8,128)(2,1)S(1)} %get-tuple-element.71), channel_id=1, source_target_pairs={{0,16},{16,0},{1,17},{17,1},{2,18},{18,2},{3,19},{19,3},{4,20},{20... | collective-permute-start | bytes 1830920 | tf_op jit(solution)/shard_map/ppermute | solution.py:549
  21.8 12.2 %pairs_own.1 = (f32[2576,128]{1,0:T(8,128)S(1)}, f32[8,128]{1,0:T(8,128)S(1)}) custom-call(s32[2992]{0:T(1024)S(1)} %get-tuple-element.57.refs_0_, s32[2]{0:T(128)S(1)} %get-tuple-element.58.refs_1_, bf16[148,16,16,128]{3,2,1,0:T(8,128)(2,1)S(1)} %bitcast.9, bf16[12,8,16,128]{3,2,1,0:T(8,128)(2,1)S(1)} %collective-permute-done.refs_3_), custom_call_target="tpu_custom_call" | custom-call | flops 106086400 | bytes 72744960 | tf_op jit(solution)/shard_map/pairs_own/pallas_call | solution.py:216
  33.9 1.0 %start_inverse.1 = (f32[304,304]{1,0:T(8,128)S(1)}, bf16[304,304]{1,0:T(8,128)(2,1)S(1)}, bf16[304,304]{1,0:T(8,128)(2,1)S(1)}, f32[2,128]{1,0:T(2,128)S(1)}) custom-call(s32[2,1480]{1,0:T(2,128)S(1)} %bitcast.10), custom_call_target="tpu_custom_call" | custom-call | flops 1073741824 | bytes 8388608 | tf_op jit(solution)/shard_map/start_inverse/pallas_call | solution.py:378
  35.0 0.9 %collective-permute-done.1.refs_2_ = bf16[2384,128]{1,0:T(8,128)(2,1)S(1)} collective-permute-done((bf16[2384,128]{1,0:T(8,128)(2,1)S(1)}, bf16[2384,128]{1,0:T(8,128)(2,1)S(1)}, u32[]{:S(2)}, u32[]{:S(2)}) %collective-permute-start.1) | collective-permute-done | bytes 610336 | tf_op jit(solution)/shard_map/ppermute | solution.py:549
  35.9 2.1 %combine.1 = (bf16[304,2048]{1,0:T(8,128)(2,1)S(1)}, bf16[304,2048]{1,0:T(8,128)(2,1)S(1)}, f32[8,304]{1,0:T(8,128)S(1)}) custom-call(f32[2576,128]{1,0:T(8,128)S(1)} %get-tuple-element.69.refs_0_, f32[8,128]{1,0:T(8,128)S(1)} %get-tuple-element.70.refs_1_, bf16[2384,128]{1,0:T(8,128)(2,1)S(1)} %collective-permute-done.1.refs_2_), custom_call_target="tpu_custom_call" | custom-call | flops 29884416 | bytes 16777216 | tf_op jit(solution)/shard_map/combine/pallas_call | solution.py:289
  38.0 1.4 %collective-permute-start.2 = (f32[8,304]{1,0:T(8,128)S(1)}, f32[8,304]{1,0:T(8,128)S(1)}, u32[]{:S(2)}, u32[]{:S(2)}) collective-permute-start(f32[8,304]{1,0:T(8,128)S(1)} %get-tuple-element.77), channel_id=1, source_target_pairs={{0,16},{16,0},{1,17},{17,1},{2,18},{18,2},{3,19},{19,3},{4,20},{20... | collective-permute-start | bytes 29192 | tf_op jit(solution)/shard_map/ppermute | solution.py:538
  39.4 2.0 %go_on_inverse.2 = (f32[304,304]{1,0:T(8,128)S(1)}, f32[2,128]{1,0:T(2,128)S(1)}) custom-call(f32[304,304]{1,0:T(8,128)S(1)} %get-tuple-element.78.refs_0_, bf16[304,304]{1,0:T(8,128)(2,1)S(1)} %get-tuple-element.93.refs_1_, bf16[304,304]{1,0:T(8,128)(2,1)S(1)} %get-tuple-element.94.refs_2_, f32[2,128]{1,0:T(2,128)S(1)} %get-tuple-element.81.refs_3_), custom_call_target="tpu_custom_call" | custom-call | flops 1073741824 | bytes 8388608 | tf_op jit(solution)/shard_map/go_on_inverse/pallas_call | solution.py:378
  41.4 0.3 collective-permute-done.2
  41.7 2.6 %collective-permute-start.3 = (f32[8,304]{1,0:T(8,128)S(1)}, f32[8,304]{1,0:T(8,128)S(1)}, u32[]{:S(2)}, u32[]{:S(2)}) collective-permute-start(f32[8,304]{1,0:T(8,128)S(1)} %add.28), channel_id=1, source_target_pairs={{0,8},{1,9},{2,10},{3,11},{4,12},{5,13},{6,14},{7,15},{8,0},{9,1},... | collective-permute-start | bytes 29192 | tf_op jit(solution)/shard_map/ppermute | solution.py:538
  44.3 1.8 %go_on_inverse.3 = (f32[304,304]{1,0:T(8,128)S(1)}, f32[2,128]{1,0:T(2,128)S(1)}) custom-call(f32[304,304]{1,0:T(8,128)S(1)} %get-tuple-element.85.refs_0_, bf16[304,304]{1,0:T(8,128)(2,1)S(1)} %get-tuple-element.93.refs_1_, bf16[304,304]{1,0:T(8,128)(2,1)S(1)} %get-tuple-element.94.refs_2_, f32[2,128]{1,0:T(2,128)S(1)} %get-tuple-element.88.refs_3_), custom_call_target="tpu_custom_call" | custom-call | flops 1073741824 | bytes 8388608 | tf_op jit(solution)/shard_map/go_on_inverse/pallas_call | solution.py:378
  46.2 0.2 collective-permute-done.3
  46.3 1.6 %collective-permute-start.4 = (f32[8,304]{1,0:T(8,128)S(1)}, f32[8,304]{1,0:T(8,128)S(1)}, u32[]{:S(2)}, u32[]{:S(2)}) collective-permute-start(f32[8,304]{1,0:T(8,128)S(1)} %add.29), channel_id=1, source_target_pairs={{0,4},{1,5},{2,6},{3,7},{4,0},{5,1},{6,2},{7,3},{8,12},{9,13},{10,... | collective-permute-start | bytes 29192 | tf_op jit(solution)/shard_map/ppermute | solution.py:538
  47.9 1.9 %end_inverse.1 = (bf16[304,304]{1,0:T(8,128)(2,1)S(1)}, bf16[304,304]{1,0:T(8,128)(2,1)S(1)}) custom-call(f32[304,304]{1,0:T(8,128)S(1)} %get-tuple-element.92.refs_0_, bf16[304,304]{1,0:T(8,128)(2,1)S(1)} %get-tuple-element.93.refs_1_, bf16[304,304]{1,0:T(8,128)(2,1)S(1)} %get-tuple-element.94.refs_2_, f32[2,128]{1,0:T(2,128)S(1)} %get-tuple-element.95.refs_3_), custom_call_target="tpu_custom_call" | custom-call | flops 1073741824 | bytes 8388608 | tf_op jit(solution)/shard_map/end_inverse/pallas_call | solution.py:378
  49.8 0.2 collective-permute-done.4
  50.0 1.5 %collective-permute-start.5 = (f32[8,304]{1,0:T(8,128)S(1)}, f32[8,304]{1,0:T(8,128)S(1)}, u32[]{:S(2)}, u32[]{:S(2)}) collective-permute-start(f32[8,304]{1,0:T(8,128)S(1)} %add.30), channel_id=1, source_target_pairs={{0,2},{1,3},{2,0},{3,1},{4,6},{5,7},{6,4},{7,5},{8,10},{9,11},{10,... | collective-permute-start | bytes 29192 | tf_op jit(solution)/shard_map/ppermute | solution.py:538
  51.6 1.4 %solve.2.refs_0_ = f32[8,304,128]{2,1,0:T(8,128)S(1)} custom-call(bf16[304,304]{1,0:T(8,128)(2,1)S(1)} %get-tuple-element.104.refs_0_.refs_3_, bf16[304,304]{1,0:T(8,128)(2,1)S(1)} %get-tuple-element.105.refs_1_.refs_4_, bf16[304,2048]{1,0:T(8,128)(2,1)S(1)} %get-tuple-element.101.refs_2_, bf16[304,2048]{1,0:T(8,128)(2,1)S(1)} %get-tuple-element.102.refs_3_), custom_call_target="tpu_custom_call" | custom-call | flops 1135607808 | bytes 20971520 | tf_op jit(solution)/shard_map/solve/pallas_call | solution.py:446
  53.0 0.7 %collective-permute-done.5 = f32[8,304]{1,0:T(8,128)S(1)} collective-permute-done((f32[8,304]{1,0:T(8,128)S(1)}, f32[8,304]{1,0:T(8,128)S(1)}, u32[]{:S(2)}, u32[]{:S(2)}) %collective-permute-start.5) | collective-permute-done | bytes 9760 | tf_op jit(solution)/shard_map/ppermute | solution.py:538
  53.7 0.0 collective-permute-start.6
  53.7 1.4 %solve.3.refs_1_ = f32[8,304,128]{2,1,0:T(8,128)S(1)} custom-call(bf16[304,304]{1,0:T(8,128)(2,1)S(1)} %get-tuple-element.104.refs_0_.refs_3_, bf16[304,304]{1,0:T(8,128)(2,1)S(1)} %get-tuple-element.105.refs_1_.refs_4_, bf16[304,2048]{1,0:T(8,128)(2,1)S(1)} %get-tuple-element.101.refs_2_, bf16[304,2048]{1,0:T(8,128)(2,1)S(1)} %get-tuple-element.102.refs_3_), custom_call_target="tpu_custom_call" | custom-call | flops 1135607808 | bytes 20971520 | tf_op jit(solution)/shard_map/solve/pallas_call | solution.py:446
  55.2 2.6 %refine.1 = f32[4736,128]{1,0:T(8,128)} custom-call(f32[8,304,128]{2,1,0:T(8,128)S(1)} %solve.2.refs_0_, f32[8,304,128]{2,1,0:T(8,128)S(1)} %solve.3.refs_1_, f32[8,304]{1,0:T(8,128)S(1)} %add.32.refs_2_, bf16[304,304]{1,0:T(8,128)(2,1)S(1)} %get-tuple-element.104.refs_0_.refs_3_, bf16[304,304]{1,0:T(8,128)(2,1)S(1)} %get-tuple-element.105.refs_1_.refs_4_), custom_call_target="tpu_custom_call" | custom-call | flops 3637248 | bytes 16777216 | tf_op jit(solution)/shard_map/refine/pallas_call | solution.py:516
  (11 shorter events, 0.0 us)
Async XLA Ops:
  1.9 18.7 %collective-permute-start = (bf16[12,8,16,128]{3,2,1,0:T(8,128)(2,1)S(1)}, bf16[12,8,16,128]{3,2,1,0:T(8,128)(2,1)S(1)}, u32[]{:S(2)}, u32[]{:S(2)}) collective-permute-start(bf16[12,8,16,128]{3,2,1,0:T(8,128)(2,1)S(1)} %constant_dynamic-slice_fusion), channel_id=1, source_target_pairs={{0,16},{16,0},{1,17},{17,1},{2,18},{18,2},{3,19},{19,3},{4,20},{20... | collective-permute-start | bytes 1179656 | tf_op jit(solution)/shard_map/ppermute | solution.py:549
  4.9 16.9 %copy-start = (bf16[148,32,2,512]{3,2,1,0:T(2,128)(2,1)S(1)}, bf16[148,32,2,512]{3,2,1,0:T(2,128)(2,1)}, u32[]{:S(2)}) copy-start(bf16[148,32,2,512]{3,2,1,0:T(2,128)(2,1)} %param.2) | copy-start | bytes 29097988
  20.6 15.3 %collective-permute-start.1 = (bf16[2384,128]{1,0:T(8,128)(2,1)S(1)}, bf16[2384,128]{1,0:T(8,128)(2,1)S(1)}, u32[]{:S(2)}, u32[]{:S(2)}) collective-permute-start(bf16[2384,128]{1,0:T(8,128)(2,1)S(1)} %get-tuple-element.71), channel_id=1, source_target_pairs={{0,16},{16,0},{1,17},{17,1},{2,18},{18,2},{3,19},{19,3},{4,20},{20... | collective-permute-start | bytes 1830920 | tf_op jit(solution)/shard_map/ppermute | solution.py:549
  21.8 12.2 %copy-start.1 = (s32[1480,2]{0,1:T(2,128)S(1)}, s32[1480,2]{0,1:T(2,128)}, u32[]{:S(2)}) copy-start(s32[1480,2]{0,1:T(2,128)} %param.3) | copy-start | bytes 35524
  38.0 3.7 %collective-permute-start.2 = (f32[8,304]{1,0:T(8,128)S(1)}, f32[8,304]{1,0:T(8,128)S(1)}, u32[]{:S(2)}, u32[]{:S(2)}) collective-permute-start(f32[8,304]{1,0:T(8,128)S(1)} %get-tuple-element.77), channel_id=1, source_target_pairs={{0,16},{16,0},{1,17},{17,1},{2,18},{18,2},{3,19},{19,3},{4,20},{20... | collective-permute-start | bytes 29192 | tf_op jit(solution)/shard_map/ppermute | solution.py:538
  41.7 4.6 %collective-permute-start.3 = (f32[8,304]{1,0:T(8,128)S(1)}, f32[8,304]{1,0:T(8,128)S(1)}, u32[]{:S(2)}, u32[]{:S(2)}) collective-permute-start(f32[8,304]{1,0:T(8,128)S(1)} %add.28), channel_id=1, source_target_pairs={{0,8},{1,9},{2,10},{3,11},{4,12},{5,13},{6,14},{7,15},{8,0},{9,1},... | collective-permute-start | bytes 29192 | tf_op jit(solution)/shard_map/ppermute | solution.py:538
  46.3 3.7 %collective-permute-start.4 = (f32[8,304]{1,0:T(8,128)S(1)}, f32[8,304]{1,0:T(8,128)S(1)}, u32[]{:S(2)}, u32[]{:S(2)}) collective-permute-start(f32[8,304]{1,0:T(8,128)S(1)} %add.29), channel_id=1, source_target_pairs={{0,4},{1,5},{2,6},{3,7},{4,0},{5,1},{6,2},{7,3},{8,12},{9,13},{10,... | collective-permute-start | bytes 29192 | tf_op jit(solution)/shard_map/ppermute | solution.py:538
  50.0 3.7 %collective-permute-start.5 = (f32[8,304]{1,0:T(8,128)S(1)}, f32[8,304]{1,0:T(8,128)S(1)}, u32[]{:S(2)}, u32[]{:S(2)}) collective-permute-start(f32[8,304]{1,0:T(8,128)S(1)} %add.30), channel_id=1, source_target_pairs={{0,2},{1,3},{2,0},{3,1},{4,6},{5,7},{6,4},{7,5},{8,10},{9,11},{10,... | collective-permute-start | bytes 29192 | tf_op jit(solution)/shard_map/ppermute | solution.py:538
  53.7 1.5 %collective-permute-start.6 = (f32[8,304]{1,0:T(8,128)S(1)}, f32[8,304]{1,0:T(8,128)S(1)}, u32[]{:S(2)}, u32[]{:S(2)}) collective-permute-start(f32[8,304]{1,0:T(8,128)S(1)} %add.31), channel_id=1, source_target_pairs={{0,1},{1,0},{2,3},{3,2},{4,5},{5,4},{6,7},{7,6},{8,9},{9,8},{10,11... | collective-permute-start | bytes 29192 | tf_op jit(solution)/shard_map/ppermute | solution.py:538

commit v7 on v6

--- a/solution.py
+++ b/solution.py
@@ -39,7 +39,7 @@
     return lax.dot_general(first, second, dims, preferred_element_type=jnp.float32)
 
 
-def spread_looks(source, row, date, slot, step, looks, planes, choose=None, start=0, share=0, found=None):
+def spread_looks(source, row, date, slot, step, looks, planes, choose=None, pairs=None, start=0, share=0, found=None):
     raw = source[pl.ds(date, step), pl.ds(row, 8)].reshape(step, 2, SPLIT, 16, LANES)
     left = jnp.concatenate(
         [raw[:, :, sub].reshape(step * 32, LANES) for sub in range(SPLIT)], axis=1
@@ -54,8 +54,8 @@
                     planes[pl.ds(base + (rlook * LOOKC + look) * 16 + group * 8, 8), :] = spread[
                         top : top + 8, look * LANES : (look + 1) * LANES
                     ]
-        for k in range(share):
-            found = choose(start + at * share + k, found)
+        for packed in [pairs[start + at * share + k] for k in range(share)]:
+            found = choose(packed, found)
     return found
 
 
@@ -76,7 +76,7 @@
             copies.append(
                 pltpu.make_async_copy(images.at[part, pl.ds(row_start, 8)], raw.at[part], sems.at[at])
             )
-    for copy in copies:
+    for copy in copies[:2]:
         copy.start()
 
     total = series if with_halo else sums
@@ -87,8 +87,7 @@
 
     second_list = pair_count + UNROLL
 
-    def choose(at, found):
-        packed = pairs[at]
+    def choose(packed, found):
         listed[found[0]] = packed
         listed[second_list + found[1]] = packed
         return (found[0] + ((packed >> 20) & 1), found[1] + (packed >> 21))
@@ -100,14 +99,16 @@
             source, row = images, row_start
         else:
             copies[at].wait()
+            if at + 2 < steps:
+                copies[at + 2].start()
             source, row = raw, 0
         found = spread_looks(
             source, row, at * step, own_slot + at * step, step, looks, planes,
-            choose, at * step * share, share, found,
+            choose, None if with_halo else pairs, at * step * share, share, found,
         )
     if not with_halo:
         for at in range(dates * share, pair_count):
-            found = choose(at, found)
+            found = choose(pairs[at], found)
         for part in range(2):
             counts[part] = found[part]
             for at in range(UNROLL):

time: 58.3 us -> 59.8 us (1.026)
  Pallas kernels: 42.2 us -> 43.4 us
    pallas_call x2, Pallas kernels: 27.9 us -> 29.2 us  [call_pairs(): pl.pallas_call(lambda *refs: pair_kernel(pair_count, given is not None, s...]
where the time goes in v7:
time: 59.8 us; the launch traced here: 59.2 us
  Pallas kernels  43.4 us (73%)
  starting transfers between devices  10.9 us (18%)
  waiting for transfers between devices  2.74 us (5%)
  local copies, waits for them, and re-layouts  1.04 us (2%)
  other arithmetic  0.86 us (1%)
    pallas_call x2, Pallas kernels, call_pairs(): pl.pallas_call(lambda *refs: pair_kernel(pair_count, given is not None, s...  29.2 us
    ppermute x5, starting transfers between devices, sum_beside(): other = lax.ppermute(value, *pairings[at])  6.9 us
    pallas_call x4, Pallas kernels, inverse_call(): pl.pallas_call(kernel, out_shape=out_shape, in_specs=[in_vmem()] * len(ar...  6.6 us
    ppermute x2, starting transfers between devices, swap_dates(): return lax.ppermute(value, 'dates', [(0, 1), (1, 0)])  3.97 us
    pallas_call x2, Pallas kernels, call_solve(): pl.pallas_call(lambda *refs: solve_kernel(part, *refs), out_shape=jax.Sha...  2.9 us
    pallas_call x1, Pallas kernels, call_refine(): pl.pallas_call(lambda *refs: refine_kernel(count, row_total, col_total, *...  2.62 us
    pallas_call x1, Pallas kernels, call_combine(): pl.pallas_call(lambda *refs: combine_kernel(dates, row_total, col_total,...  2.08 us
    ppermute x5, waiting for transfers between devices, sum_beside(): other = lax.ppermute(value, *pairings[at])  1.79 us
  transfers between devices with their start and end apart: 7, of which 5 were waited for; matrix products, arithmetic and copies ran while one was open for 0% of the time, Pallas kernels for 65%

profile of v7, /device:TPU:0, one launch (start us, length us, event | category | flops | bytes accessed | tf_op | source)
XLA Modules:
  0.0 59.2 jit_solution(826308518936018939)
XLA Ops:
  0.0 0.8 %fusion.refs_0_ = s32[1480]{0:T(1024)S(1)} fusion(s32[1480,2]{0,1:T(2,128)} %param.3, s32[]{:T(128)S(6)} %mul.11, s32[]{:T(128)S(6)} %add.27, s32[]{:T(128)S(6)} %mul.10), kind=kLoop, calls=%fused_computation.5 | loop fusion | flops 29600 | bytes 17772 | tf_op jit(solution)/shard_map/jit(_where)/select_n | solution.py:567
  0.8 1.0 %constant_dynamic-slice_fusion = bf16[12,8,16,128]{3,2,1,0:T(8,128)(2,1)S(1)} fusion(bf16[148,16,16,128]{3,2,1,0:T(8,128)(2,1)} %bitcast.7, s32[]{:T(128)S(6)} %select_n.10, s32[]{:T(128)S(6)} %select_n.11), kind=kLoop, calls=%fused_computation.10 | loop fusion | bytes 786440 | tf_op jit(solution)/shard_map/dynamic_slice | solution.py:569
  1.9 3.0 %collective-permute-start = (bf16[12,8,16,128]{3,2,1,0:T(8,128)(2,1)S(1)}, bf16[12,8,16,128]{3,2,1,0:T(8,128)(2,1)S(1)}, u32[]{:S(2)}, u32[]{:S(2)}) collective-permute-start(bf16[12,8,16,128]{3,2,1,0:T(8,128)(2,1)S(1)} %constant_dynamic-slice_fusion), channel_id=1, source_target_pairs={{0,16},{16,0},{1,17},{17,1},{2,18},{18,2},{3,19},{19,3},{4,20},{20... | collective-permute-start | bytes 1179656 | tf_op jit(solution)/shard_map/ppermute | solution.py:550
  4.9 16.9 %pairs_other.1 = (bf16[2384,128]{1,0:T(8,128)(2,1)S(1)}, s32[2992]{0:T(1024)S(1)}, s32[2]{0:T(128)S(1)}) custom-call(s32[1480]{0:T(1024)S(1)} %fusion.refs_0_, bf16[148,16,16,128]{3,2,1,0:T(8,128)(2,1)} %bitcast.8), custom_call_target="tpu_custom_call" | custom-call | flops 106086400 | bytes 72744960 | tf_op jit(solution)/shard_map/pairs_other/pallas_call | solution.py:217
  21.8 0.0 collective-permute-done.refs_3_
  21.8 1.0 %collective-permute-start.1 = (bf16[2384,128]{1,0:T(8,128)(2,1)S(1)}, bf16[2384,128]{1,0:T(8,128)(2,1)S(1)}, u32[]{:S(2)}, u32[]{:S(2)}) collective-permute-start(bf16[2384,128]{1,0:T(8,128)(2,1)S(1)} %get-tuple-element.71), channel_id=1, source_target_pairs={{0,16},{16,0},{1,17},{17,1},{2,18},{18,2},{3,19},{19,3},{4,20},{20... | collective-permute-start | bytes 1830920 | tf_op jit(solution)/shard_map/ppermute | solution.py:550
  22.8 12.3 %pairs_own.1 = (f32[2576,128]{1,0:T(8,128)S(1)}, f32[8,128]{1,0:T(8,128)S(1)}) custom-call(s32[2992]{0:T(1024)S(1)} %get-tuple-element.57.refs_0_, s32[2]{0:T(128)S(1)} %get-tuple-element.58.refs_1_, bf16[148,16,16,128]{3,2,1,0:T(8,128)(2,1)S(1)} %bitcast.9, bf16[12,8,16,128]{3,2,1,0:T(8,128)(2,1)S(1)} %collective-permute-done.refs_3_), custom_call_target="tpu_custom_call" | custom-call | flops 106086400 | bytes 72744960 | tf_op jit(solution)/shard_map/pairs_own/pallas_call | solution.py:217
  35.1 1.0 %start_inverse.1 = (f32[304,304]{1,0:T(8,128)S(1)}, bf16[304,304]{1,0:T(8,128)(2,1)S(1)}, bf16[304,304]{1,0:T(8,128)(2,1)S(1)}, f32[2,128]{1,0:T(2,128)S(1)}) custom-call(s32[2,1480]{1,0:T(2,128)S(1)} %bitcast.10), custom_call_target="tpu_custom_call" | custom-call | flops 1073741824 | bytes 8388608 | tf_op jit(solution)/shard_map/start_inverse/pallas_call | solution.py:379
  36.1 1.0 %collective-permute-done.1.refs_2_ = bf16[2384,128]{1,0:T(8,128)(2,1)S(1)} collective-permute-done((bf16[2384,128]{1,0:T(8,128)(2,1)S(1)}, bf16[2384,128]{1,0:T(8,128)(2,1)S(1)}, u32[]{:S(2)}, u32[]{:S(2)}) %collective-permute-start.1) | collective-permute-done | bytes 610336 | tf_op jit(solution)/shard_map/ppermute | solution.py:550
  37.1 2.1 %combine.1 = (bf16[304,2048]{1,0:T(8,128)(2,1)S(1)}, bf16[304,2048]{1,0:T(8,128)(2,1)S(1)}, f32[8,304]{1,0:T(8,128)S(1)}) custom-call(f32[2576,128]{1,0:T(8,128)S(1)} %get-tuple-element.69.refs_0_, f32[8,128]{1,0:T(8,128)S(1)} %get-tuple-element.70.refs_1_, bf16[2384,128]{1,0:T(8,128)(2,1)S(1)} %collective-permute-done.1.refs_2_), custom_call_target="tpu_custom_call" | custom-call | flops 29884416 | bytes 16777216 | tf_op jit(solution)/shard_map/combine/pallas_call | solution.py:290
  39.2 1.2 %collective-permute-start.2 = (f32[8,304]{1,0:T(8,128)S(1)}, f32[8,304]{1,0:T(8,128)S(1)}, u32[]{:S(2)}, u32[]{:S(2)}) collective-permute-start(f32[8,304]{1,0:T(8,128)S(1)} %get-tuple-element.77), channel_id=1, source_target_pairs={{0,16},{16,0},{1,17},{17,1},{2,18},{18,2},{3,19},{19,3},{4,20},{20... | collective-permute-start | bytes 29192 | tf_op jit(solution)/shard_map/ppermute | solution.py:539
  40.4 1.8 %go_on_inverse.2 = (f32[304,304]{1,0:T(8,128)S(1)}, f32[2,128]{1,0:T(2,128)S(1)}) custom-call(f32[304,304]{1,0:T(8,128)S(1)} %get-tuple-element.78.refs_0_, bf16[304,304]{1,0:T(8,128)(2,1)S(1)} %get-tuple-element.93.refs_1_, bf16[304,304]{1,0:T(8,128)(2,1)S(1)} %get-tuple-element.94.refs_2_, f32[2,128]{1,0:T(2,128)S(1)} %get-tuple-element.81.refs_3_), custom_call_target="tpu_custom_call" | custom-call | flops 1073741824 | bytes 8388608 | tf_op jit(solution)/shard_map/go_on_inverse/pallas_call | solution.py:379
  42.2 0.7 %collective-permute-done.2 = f32[8,304]{1,0:T(8,128)S(1)} collective-permute-done((f32[8,304]{1,0:T(8,128)S(1)}, f32[8,304]{1,0:T(8,128)S(1)}, u32[]{:S(2)}, u32[]{:S(2)}) %collective-permute-start.2) | collective-permute-done | bytes 9760 | tf_op jit(solution)/shard_map/ppermute | solution.py:539
  42.9 2.6 %collective-permute-start.3 = (f32[8,304]{1,0:T(8,128)S(1)}, f32[8,304]{1,0:T(8,128)S(1)}, u32[]{:S(2)}, u32[]{:S(2)}) collective-permute-start(f32[8,304]{1,0:T(8,128)S(1)} %add.28), channel_id=1, source_target_pairs={{0,8},{1,9},{2,10},{3,11},{4,12},{5,13},{6,14},{7,15},{8,0},{9,1},... | collective-permute-start | bytes 29192 | tf_op jit(solution)/shard_map/ppermute | solution.py:539
  45.5 1.8 %go_on_inverse.3 = (f32[304,304]{1,0:T(8,128)S(1)}, f32[2,128]{1,0:T(2,128)S(1)}) custom-call(f32[304,304]{1,0:T(8,128)S(1)} %get-tuple-element.85.refs_0_, bf16[304,304]{1,0:T(8,128)(2,1)S(1)} %get-tuple-element.93.refs_1_, bf16[304,304]{1,0:T(8,128)(2,1)S(1)} %get-tuple-element.94.refs_2_, f32[2,128]{1,0:T(2,128)S(1)} %get-tuple-element.88.refs_3_), custom_call_target="tpu_custom_call" | custom-call | flops 1073741824 | bytes 8388608 | tf_op jit(solution)/shard_map/go_on_inverse/pallas_call | solution.py:379
  47.4 0.1 collective-permute-done.3
  47.5 1.6 %collective-permute-start.4 = (f32[8,304]{1,0:T(8,128)S(1)}, f32[8,304]{1,0:T(8,128)S(1)}, u32[]{:S(2)}, u32[]{:S(2)}) collective-permute-start(f32[8,304]{1,0:T(8,128)S(1)} %add.29), channel_id=1, source_target_pairs={{0,4},{1,5},{2,6},{3,7},{4,0},{5,1},{6,2},{7,3},{8,12},{9,13},{10,... | collective-permute-start | bytes 29192 | tf_op jit(solution)/shard_map/ppermute | solution.py:539
  49.1 1.9 %end_inverse.1 = (bf16[304,304]{1,0:T(8,128)(2,1)S(1)}, bf16[304,304]{1,0:T(8,128)(2,1)S(1)}) custom-call(f32[304,304]{1,0:T(8,128)S(1)} %get-tuple-element.92.refs_0_, bf16[304,304]{1,0:T(8,128)(2,1)S(1)} %get-tuple-element.93.refs_1_, bf16[304,304]{1,0:T(8,128)(2,1)S(1)} %get-tuple-element.94.refs_2_, f32[2,128]{1,0:T(2,128)S(1)} %get-tuple-element.95.refs_3_), custom_call_target="tpu_custom_call" | custom-call | flops 1073741824 | bytes 8388608 | tf_op jit(solution)/shard_map/end_inverse/pallas_call | solution.py:379
  51.0 0.2 collective-permute-done.4
  51.2 1.5 %collective-permute-start.5 = (f32[8,304]{1,0:T(8,128)S(1)}, f32[8,304]{1,0:T(8,128)S(1)}, u32[]{:S(2)}, u32[]{:S(2)}) collective-permute-start(f32[8,304]{1,0:T(8,128)S(1)} %add.30), channel_id=1, source_target_pairs={{0,2},{1,3},{2,0},{3,1},{4,6},{5,7},{6,4},{7,5},{8,10},{9,11},{10,... | collective-permute-start | bytes 29192 | tf_op jit(solution)/shard_map/ppermute | solution.py:539
  52.7 1.5 %solve.2.refs_0_ = f32[8,304,128]{2,1,0:T(8,128)S(1)} custom-call(bf16[304,304]{1,0:T(8,128)(2,1)S(1)} %get-tuple-element.104.refs_0_.refs_3_, bf16[304,304]{1,0:T(8,128)(2,1)S(1)} %get-tuple-element.105.refs_1_.refs_4_, bf16[304,2048]{1,0:T(8,128)(2,1)S(1)} %get-tuple-element.101.refs_2_, bf16[304,2048]{1,0:T(8,128)(2,1)S(1)} %get-tuple-element.102.refs_3_), custom_call_target="tpu_custom_call" | custom-call | flops 1135607808 | bytes 20971520 | tf_op jit(solution)/shard_map/solve/pallas_call | solution.py:447
  54.2 0.7 %collective-permute-done.5 = f32[8,304]{1,0:T(8,128)S(1)} collective-permute-done((f32[8,304]{1,0:T(8,128)S(1)}, f32[8,304]{1,0:T(8,128)S(1)}, u32[]{:S(2)}, u32[]{:S(2)}) %collective-permute-start.5) | collective-permute-done | bytes 9760 | tf_op jit(solution)/shard_map/ppermute | solution.py:539
  54.9 1.4 %solve.3.refs_1_ = f32[8,304,128]{2,1,0:T(8,128)S(1)} custom-call(bf16[304,304]{1,0:T(8,128)(2,1)S(1)} %get-tuple-element.104.refs_0_.refs_3_, bf16[304,304]{1,0:T(8,128)(2,1)S(1)} %get-tuple-element.105.refs_1_.refs_4_, bf16[304,2048]{1,0:T(8,128)(2,1)S(1)} %get-tuple-element.101.refs_2_, bf16[304,2048]{1,0:T(8,128)(2,1)S(1)} %get-tuple-element.102.refs_3_), custom_call_target="tpu_custom_call" | custom-call | flops 1135607808 | bytes 20971520 | tf_op jit(solution)/shard_map/solve/pallas_call | solution.py:447
  56.4 2.6 %refine.1 = f32[4736,128]{1,0:T(8,128)} custom-call(f32[8,304,128]{2,1,0:T(8,128)S(1)} %solve.2.refs_0_, f32[8,304,128]{2,1,0:T(8,128)S(1)} %solve.3.refs_1_, f32[8,304]{1,0:T(8,128)S(1)} %add.32.refs_2_, bf16[304,304]{1,0:T(8,128)(2,1)S(1)} %get-tuple-element.104.refs_0_.refs_3_, bf16[304,304]{1,0:T(8,128)(2,1)S(1)} %get-tuple-element.105.refs_1_.refs_4_), custom_call_target="tpu_custom_call" | custom-call | flops 3637248 | bytes 16777216 | tf_op jit(solution)/shard_map/refine/pallas_call | solution.py:517
  (11 shorter events, 0.0 us)
Async XLA Ops:
  1.9 19.9 %collective-permute-start = (bf16[12,8,16,128]{3,2,1,0:T(8,128)(2,1)S(1)}, bf16[12,8,16,128]{3,2,1,0:T(8,128)(2,1)S(1)}, u32[]{:S(2)}, u32[]{:S(2)}) collective-permute-start(bf16[12,8,16,128]{3,2,1,0:T(8,128)(2,1)S(1)} %constant_dynamic-slice_fusion), channel_id=1, source_target_pairs={{0,16},{16,0},{1,17},{17,1},{2,18},{18,2},{3,19},{19,3},{4,20},{20... | collective-permute-start | bytes 1179656 | tf_op jit(solution)/shard_map/ppermute | solution.py:550
  4.9 17.9 %copy-start = (bf16[148,32,2,512]{3,2,1,0:T(2,128)(2,1)S(1)}, bf16[148,32,2,512]{3,2,1,0:T(2,128)(2,1)}, u32[]{:S(2)}) copy-start(bf16[148,32,2,512]{3,2,1,0:T(2,128)(2,1)} %param.2) | copy-start | bytes 29097988
  21.8 15.3 %collective-permute-start.1 = (bf16[2384,128]{1,0:T(8,128)(2,1)S(1)}, bf16[2384,128]{1,0:T(8,128)(2,1)S(1)}, u32[]{:S(2)}, u32[]{:S(2)}) collective-permute-start(bf16[2384,128]{1,0:T(8,128)(2,1)S(1)} %get-tuple-element.71), channel_id=1, source_target_pairs={{0,16},{16,0},{1,17},{17,1},{2,18},{18,2},{3,19},{19,3},{4,20},{20... | collective-permute-start | bytes 1830920 | tf_op jit(solution)/shard_map/ppermute | solution.py:550
  22.8 12.3 %copy-start.1 = (s32[1480,2]{0,1:T(2,128)S(1)}, s32[1480,2]{0,1:T(2,128)}, u32[]{:S(2)}) copy-start(s32[1480,2]{0,1:T(2,128)} %param.3) | copy-start | bytes 35524
  39.2 3.7 %collective-permute-start.2 = (f32[8,304]{1,0:T(8,128)S(1)}, f32[8,304]{1,0:T(8,128)S(1)}, u32[]{:S(2)}, u32[]{:S(2)}) collective-permute-start(f32[8,304]{1,0:T(8,128)S(1)} %get-tuple-element.77), channel_id=1, source_target_pairs={{0,16},{16,0},{1,17},{17,1},{2,18},{18,2},{3,19},{19,3},{4,20},{20... | collective-permute-start | bytes 29192 | tf_op jit(solution)/shard_map/ppermute | solution.py:539
  42.9 4.6 %collective-permute-start.3 = (f32[8,304]{1,0:T(8,128)S(1)}, f32[8,304]{1,0:T(8,128)S(1)}, u32[]{:S(2)}, u32[]{:S(2)}) collective-permute-start(f32[8,304]{1,0:T(8,128)S(1)} %add.28), channel_id=1, source_target_pairs={{0,8},{1,9},{2,10},{3,11},{4,12},{5,13},{6,14},{7,15},{8,0},{9,1},... | collective-permute-start | bytes 29192 | tf_op jit(solution)/shard_map/ppermute | solution.py:539
  47.5 3.7 %collective-permute-start.4 = (f32[8,304]{1,0:T(8,128)S(1)}, f32[8,304]{1,0:T(8,128)S(1)}, u32[]{:S(2)}, u32[]{:S(2)}) collective-permute-start(f32[8,304]{1,0:T(8,128)S(1)} %add.29), channel_id=1, source_target_pairs={{0,4},{1,5},{2,6},{3,7},{4,0},{5,1},{6,2},{7,3},{8,12},{9,13},{10,... | collective-permute-start | bytes 29192 | tf_op jit(solution)/shard_map/ppermute | solution.py:539
  51.2 3.7 %collective-permute-start.5 = (f32[8,304]{1,0:T(8,128)S(1)}, f32[8,304]{1,0:T(8,128)S(1)}, u32[]{:S(2)}, u32[]{:S(2)}) collective-permute-start(f32[8,304]{1,0:T(8,128)S(1)} %add.30), channel_id=1, source_target_pairs={{0,2},{1,3},{2,0},{3,1},{4,6},{5,7},{6,4},{7,5},{8,10},{9,11},{10,... | collective-permute-start | bytes 29192 | tf_op jit(solution)/shard_map/ppermute | solution.py:539
  54.9 1.5 %collective-permute-start.6 = (f32[8,304]{1,0:T(8,128)S(1)}, f32[8,304]{1,0:T(8,128)S(1)}, u32[]{:S(2)}, u32[]{:S(2)}) collective-permute-start(f32[8,304]{1,0:T(8,128)S(1)} %add.31), channel_id=1, source_target_pairs={{0,1},{1,0},{2,3},{3,2},{4,5},{5,4},{6,7},{7,6},{8,9},{9,8},{10,11... | collective-permute-start | bytes 29192 | tf_op jit(solution)/shard_map/ppermute | solution.py:539

commit v8 on v6

--- a/solution.py
+++ b/solution.py
@@ -94,7 +94,10 @@
         return (found[0] + ((packed >> 20) & 1), found[1] + (packed >> 21))
 
     found = (jnp.int32(0), jnp.int32(0))
-    share = 0 if with_halo else pair_count // dates
+    early = min(2 * dates, pair_count)
+    share = 0 if with_halo else (pair_count - early) // dates
+    if not with_halo:
+        found = lax.fori_loop(0, early, choose, found, unroll=8)
     for at in range(steps):
         if with_halo:
             source, row = images, row_start
@@ -103,10 +106,10 @@
             source, row = raw, 0
         found = spread_looks(
             source, row, at * step, own_slot + at * step, step, looks, planes,
-            choose, at * step * share, share, found,
+            choose, early + at * step * share, share, found,
         )
     if not with_halo:
-        for at in range(dates * share, pair_count):
+        for at in range(early + dates * share, pair_count):
             found = choose(at, found)
         for part in range(2):
             counts[part] = found[part]

time: 58.3 us -> 57.8 us (level)
  Pallas kernels: 42.2 us -> 41.2 us
    pallas_call x2, Pallas kernels: 27.9 us -> 26.8 us  [call_pairs(): pl.pallas_call(lambda *refs: pair_kernel(pair_count, given is not None, s...]
  transfers between devices with their start and end apart: 7 -> 7, of which waited for: 5 -> 4; matrix products, arithmetic and copies ran while one was open for 0% -> 0% of each run, Pallas kernels for 65% -> 64%
where the time goes in v8:
time: 57.8 us; the launch traced here: 57.2 us
  Pallas kernels  41.2 us (71%)
  starting transfers between devices  11.3 us (20%)
  waiting for transfers between devices  2.61 us (5%)
  local copies, waits for them, and re-layouts  1.04 us (2%)
  other arithmetic  0.86 us (1%)
    pallas_call x2, Pallas kernels, call_pairs(): pl.pallas_call(lambda *refs: pair_kernel(pair_count, given is not None, s...  26.8 us
    ppermute x5, starting transfers between devices, sum_beside(): other = lax.ppermute(value, *pairings[at])  7.15 us
    pallas_call x4, Pallas kernels, inverse_call(): pl.pallas_call(kernel, out_shape=out_shape, in_specs=[in_vmem()] * len(ar...  6.75 us
    ppermute x2, starting transfers between devices, swap_dates(): return lax.ppermute(value, 'dates', [(0, 1), (1, 0)])  4.16 us
    pallas_call x2, Pallas kernels, call_solve(): pl.pallas_call(lambda *refs: solve_kernel(part, *refs), out_shape=jax.Sha...  2.9 us
    pallas_call x1, Pallas kernels, call_refine(): pl.pallas_call(lambda *refs: refine_kernel(count, row_total, col_total, *...  2.62 us
    pallas_call x1, Pallas kernels, call_combine(): pl.pallas_call(lambda *refs: combine_kernel(dates, row_total, col_total,...  2.08 us
    ppermute x5, waiting for transfers between devices, sum_beside(): other = lax.ppermute(value, *pairings[at])  1.46 us
  transfers between devices with their start and end apart: 7, of which 4 were waited for; matrix products, arithmetic and copies ran while one was open for 0% of the time, Pallas kernels for 64%

profile of v8, /device:TPU:0, one launch (start us, length us, event | category | flops | bytes accessed | tf_op | source)
XLA Modules:
  0.0 57.2 jit_solution(9202302124305397825)
XLA Ops:
  0.0 0.8 %fusion.refs_0_ = s32[1480]{0:T(1024)S(1)} fusion(s32[1480,2]{0,1:T(2,128)} %param.3, s32[]{:T(128)S(6)} %mul.11, s32[]{:T(128)S(6)} %add.27, s32[]{:T(128)S(6)} %mul.10), kind=kLoop, calls=%fused_computation.5 | loop fusion | flops 29600 | bytes 17772 | tf_op jit(solution)/shard_map/jit(_where)/select_n | solution.py:569
  0.8 1.0 %constant_dynamic-slice_fusion = bf16[12,8,16,128]{3,2,1,0:T(8,128)(2,1)S(1)} fusion(bf16[148,16,16,128]{3,2,1,0:T(8,128)(2,1)} %bitcast.7, s32[]{:T(128)S(6)} %select_n.10, s32[]{:T(128)S(6)} %select_n.11), kind=kLoop, calls=%fused_computation.10 | loop fusion | bytes 786440 | tf_op jit(solution)/shard_map/dynamic_slice | solution.py:571
  1.9 3.0 %collective-permute-start = (bf16[12,8,16,128]{3,2,1,0:T(8,128)(2,1)S(1)}, bf16[12,8,16,128]{3,2,1,0:T(8,128)(2,1)S(1)}, u32[]{:S(2)}, u32[]{:S(2)}) collective-permute-start(bf16[12,8,16,128]{3,2,1,0:T(8,128)(2,1)S(1)} %constant_dynamic-slice_fusion), channel_id=1, source_target_pairs={{0,16},{16,0},{1,17},{17,1},{2,18},{18,2},{3,19},{19,3},{4,20},{20... | collective-permute-start | bytes 1179656 | tf_op jit(solution)/shard_map/ppermute | solution.py:552
  4.9 14.9 %pairs_other.1 = (bf16[2384,128]{1,0:T(8,128)(2,1)S(1)}, s32[2992]{0:T(1024)S(1)}, s32[2]{0:T(128)S(1)}) custom-call(s32[1480]{0:T(1024)S(1)} %fusion.refs_0_, bf16[148,16,16,128]{3,2,1,0:T(8,128)(2,1)} %bitcast.8), custom_call_target="tpu_custom_call" | custom-call | flops 106086400 | bytes 72744960 | tf_op jit(solution)/shard_map/pairs_other/pallas_call | solution.py:219
  19.8 0.0 collective-permute-done.refs_3_
  19.8 1.2 %collective-permute-start.1 = (bf16[2384,128]{1,0:T(8,128)(2,1)S(1)}, bf16[2384,128]{1,0:T(8,128)(2,1)S(1)}, u32[]{:S(2)}, u32[]{:S(2)}) collective-permute-start(bf16[2384,128]{1,0:T(8,128)(2,1)S(1)} %get-tuple-element.71), channel_id=1, source_target_pairs={{0,16},{16,0},{1,17},{17,1},{2,18},{18,2},{3,19},{19,3},{4,20},{20... | collective-permute-start | bytes 1830920 | tf_op jit(solution)/shard_map/ppermute | solution.py:552
  20.9 11.9 %pairs_own.1 = (f32[2576,128]{1,0:T(8,128)S(1)}, f32[8,128]{1,0:T(8,128)S(1)}) custom-call(s32[2992]{0:T(1024)S(1)} %get-tuple-element.57.refs_0_, s32[2]{0:T(128)S(1)} %get-tuple-element.58.refs_1_, bf16[148,16,16,128]{3,2,1,0:T(8,128)(2,1)S(1)} %bitcast.9, bf16[12,8,16,128]{3,2,1,0:T(8,128)(2,1)S(1)} %collective-permute-done.refs_3_), custom_call_target="tpu_custom_call" | custom-call | flops 106086400 | bytes 72744960 | tf_op jit(solution)/shard_map/pairs_own/pallas_call | solution.py:219
  32.9 1.0 %start_inverse.1 = (f32[304,304]{1,0:T(8,128)S(1)}, bf16[304,304]{1,0:T(8,128)(2,1)S(1)}, bf16[304,304]{1,0:T(8,128)(2,1)S(1)}, f32[2,128]{1,0:T(2,128)S(1)}) custom-call(s32[2,1480]{1,0:T(2,128)S(1)} %bitcast.10), custom_call_target="tpu_custom_call" | custom-call | flops 1073741824 | bytes 8388608 | tf_op jit(solution)/shard_map/start_inverse/pallas_call | solution.py:381
  33.9 1.1 %collective-permute-done.1.refs_2_ = bf16[2384,128]{1,0:T(8,128)(2,1)S(1)} collective-permute-done((bf16[2384,128]{1,0:T(8,128)(2,1)S(1)}, bf16[2384,128]{1,0:T(8,128)(2,1)S(1)}, u32[]{:S(2)}, u32[]{:S(2)}) %collective-permute-start.1) | collective-permute-done | bytes 610336 | tf_op jit(solution)/shard_map/ppermute | solution.py:552
  35.1 2.1 %combine.1 = (bf16[304,2048]{1,0:T(8,128)(2,1)S(1)}, bf16[304,2048]{1,0:T(8,128)(2,1)S(1)}, f32[8,304]{1,0:T(8,128)S(1)}) custom-call(f32[2576,128]{1,0:T(8,128)S(1)} %get-tuple-element.69.refs_0_, f32[8,128]{1,0:T(8,128)S(1)} %get-tuple-element.70.refs_1_, bf16[2384,128]{1,0:T(8,128)(2,1)S(1)} %collective-permute-done.1.refs_2_), custom_call_target="tpu_custom_call" | custom-call | flops 29884416 | bytes 16777216 | tf_op jit(solution)/shard_map/combine/pallas_call | solution.py:292
  37.2 1.4 %collective-permute-start.2 = (f32[8,304]{1,0:T(8,128)S(1)}, f32[8,304]{1,0:T(8,128)S(1)}, u32[]{:S(2)}, u32[]{:S(2)}) collective-permute-start(f32[8,304]{1,0:T(8,128)S(1)} %get-tuple-element.77), channel_id=1, source_target_pairs={{0,16},{16,0},{1,17},{17,1},{2,18},{18,2},{3,19},{19,3},{4,20},{20... | collective-permute-start | bytes 29192 | tf_op jit(solution)/shard_map/ppermute | solution.py:541
  38.6 1.8 %go_on_inverse.2 = (f32[304,304]{1,0:T(8,128)S(1)}, f32[2,128]{1,0:T(2,128)S(1)}) custom-call(f32[304,304]{1,0:T(8,128)S(1)} %get-tuple-element.78.refs_0_, bf16[304,304]{1,0:T(8,128)(2,1)S(1)} %get-tuple-element.93.refs_1_, bf16[304,304]{1,0:T(8,128)(2,1)S(1)} %get-tuple-element.94.refs_2_, f32[2,128]{1,0:T(2,128)S(1)} %get-tuple-element.81.refs_3_), custom_call_target="tpu_custom_call" | custom-call | flops 1073741824 | bytes 8388608 | tf_op jit(solution)/shard_map/go_on_inverse/pallas_call | solution.py:381
  40.4 0.5 collective-permute-done.2
  40.9 2.6 %collective-permute-start.3 = (f32[8,304]{1,0:T(8,128)S(1)}, f32[8,304]{1,0:T(8,128)S(1)}, u32[]{:S(2)}, u32[]{:S(2)}) collective-permute-start(f32[8,304]{1,0:T(8,128)S(1)} %add.28), channel_id=1, source_target_pairs={{0,8},{1,9},{2,10},{3,11},{4,12},{5,13},{6,14},{7,15},{8,0},{9,1},... | collective-permute-start | bytes 29192 | tf_op jit(solution)/shard_map/ppermute | solution.py:541
  43.5 2.0 %go_on_inverse.3 = (f32[304,304]{1,0:T(8,128)S(1)}, f32[2,128]{1,0:T(2,128)S(1)}) custom-call(f32[304,304]{1,0:T(8,128)S(1)} %get-tuple-element.85.refs_0_, bf16[304,304]{1,0:T(8,128)(2,1)S(1)} %get-tuple-element.93.refs_1_, bf16[304,304]{1,0:T(8,128)(2,1)S(1)} %get-tuple-element.94.refs_2_, f32[2,128]{1,0:T(2,128)S(1)} %get-tuple-element.88.refs_3_), custom_call_target="tpu_custom_call" | custom-call | flops 1073741824 | bytes 8388608 | tf_op jit(solution)/shard_map/go_on_inverse/pallas_call | solution.py:381
  45.5 1.6 %collective-permute-start.4 = (f32[8,304]{1,0:T(8,128)S(1)}, f32[8,304]{1,0:T(8,128)S(1)}, u32[]{:S(2)}, u32[]{:S(2)}) collective-permute-start(f32[8,304]{1,0:T(8,128)S(1)} %add.29), channel_id=1, source_target_pairs={{0,4},{1,5},{2,6},{3,7},{4,0},{5,1},{6,2},{7,3},{8,12},{9,13},{10,... | collective-permute-start | bytes 29192 | tf_op jit(solution)/shard_map/ppermute | solution.py:541
  47.2 1.9 %end_inverse.1 = (bf16[304,304]{1,0:T(8,128)(2,1)S(1)}, bf16[304,304]{1,0:T(8,128)(2,1)S(1)}) custom-call(f32[304,304]{1,0:T(8,128)S(1)} %get-tuple-element.92.refs_0_, bf16[304,304]{1,0:T(8,128)(2,1)S(1)} %get-tuple-element.93.refs_1_, bf16[304,304]{1,0:T(8,128)(2,1)S(1)} %get-tuple-element.94.refs_2_, f32[2,128]{1,0:T(2,128)S(1)} %get-tuple-element.95.refs_3_), custom_call_target="tpu_custom_call" | custom-call | flops 1073741824 | bytes 8388608 | tf_op jit(solution)/shard_map/end_inverse/pallas_call | solution.py:381
  49.0 0.3 collective-permute-done.4
  49.3 1.5 %collective-permute-start.5 = (f32[8,304]{1,0:T(8,128)S(1)}, f32[8,304]{1,0:T(8,128)S(1)}, u32[]{:S(2)}, u32[]{:S(2)}) collective-permute-start(f32[8,304]{1,0:T(8,128)S(1)} %add.30), channel_id=1, source_target_pairs={{0,2},{1,3},{2,0},{3,1},{4,6},{5,7},{6,4},{7,5},{8,10},{9,11},{10,... | collective-permute-start | bytes 29192 | tf_op jit(solution)/shard_map/ppermute | solution.py:541
  50.8 1.4 %solve.2.refs_0_ = f32[8,304,128]{2,1,0:T(8,128)S(1)} custom-call(bf16[304,304]{1,0:T(8,128)(2,1)S(1)} %get-tuple-element.104.refs_0_.refs_3_, bf16[304,304]{1,0:T(8,128)(2,1)S(1)} %get-tuple-element.105.refs_1_.refs_4_, bf16[304,2048]{1,0:T(8,128)(2,1)S(1)} %get-tuple-element.101.refs_2_, bf16[304,2048]{1,0:T(8,128)(2,1)S(1)} %get-tuple-element.102.refs_3_), custom_call_target="tpu_custom_call" | custom-call | flops 1135607808 | bytes 20971520 | tf_op jit(solution)/shard_map/solve/pallas_call | solution.py:449
  52.3 0.7 %collective-permute-done.5 = f32[8,304]{1,0:T(8,128)S(1)} collective-permute-done((f32[8,304]{1,0:T(8,128)S(1)}, f32[8,304]{1,0:T(8,128)S(1)}, u32[]{:S(2)}, u32[]{:S(2)}) %collective-permute-start.5) | collective-permute-done | bytes 9760 | tf_op jit(solution)/shard_map/ppermute | solution.py:541
  53.0 1.4 %solve.3.refs_1_ = f32[8,304,128]{2,1,0:T(8,128)S(1)} custom-call(bf16[304,304]{1,0:T(8,128)(2,1)S(1)} %get-tuple-element.104.refs_0_.refs_3_, bf16[304,304]{1,0:T(8,128)(2,1)S(1)} %get-tuple-element.105.refs_1_.refs_4_, bf16[304,2048]{1,0:T(8,128)(2,1)S(1)} %get-tuple-element.101.refs_2_, bf16[304,2048]{1,0:T(8,128)(2,1)S(1)} %get-tuple-element.102.refs_3_), custom_call_target="tpu_custom_call" | custom-call | flops 1135607808 | bytes 20971520 | tf_op jit(solution)/shard_map/solve/pallas_call | solution.py:449
  54.4 0.0 collective-permute-done.6
  54.5 2.6 %refine.1 = f32[4736,128]{1,0:T(8,128)} custom-call(f32[8,304,128]{2,1,0:T(8,128)S(1)} %solve.2.refs_0_, f32[8,304,128]{2,1,0:T(8,128)S(1)} %solve.3.refs_1_, f32[8,304]{1,0:T(8,128)S(1)} %add.32.refs_2_, bf16[304,304]{1,0:T(8,128)(2,1)S(1)} %get-tuple-element.104.refs_0_.refs_3_, bf16[304,304]{1,0:T(8,128)(2,1)S(1)} %get-tuple-element.105.refs_1_.refs_4_), custom_call_target="tpu_custom_call" | custom-call | flops 3637248 | bytes 16777216 | tf_op jit(solution)/shard_map/refine/pallas_call | solution.py:519
  (11 shorter events, 0.0 us)
Async XLA Ops:
  1.9 17.9 %collective-permute-start = (bf16[12,8,16,128]{3,2,1,0:T(8,128)(2,1)S(1)}, bf16[12,8,16,128]{3,2,1,0:T(8,128)(2,1)S(1)}, u32[]{:S(2)}, u32[]{:S(2)}) collective-permute-start(bf16[12,8,16,128]{3,2,1,0:T(8,128)(2,1)S(1)} %constant_dynamic-slice_fusion), channel_id=1, source_target_pairs={{0,16},{16,0},{1,17},{17,1},{2,18},{18,2},{3,19},{19,3},{4,20},{20... | collective-permute-start | bytes 1179656 | tf_op jit(solution)/shard_map/ppermute | solution.py:552
  4.9 16.0 %copy-start = (bf16[148,32,2,512]{3,2,1,0:T(2,128)(2,1)S(1)}, bf16[148,32,2,512]{3,2,1,0:T(2,128)(2,1)}, u32[]{:S(2)}) copy-start(bf16[148,32,2,512]{3,2,1,0:T(2,128)(2,1)} %param.2) | copy-start | bytes 29097988
  19.8 15.3 %collective-permute-start.1 = (bf16[2384,128]{1,0:T(8,128)(2,1)S(1)}, bf16[2384,128]{1,0:T(8,128)(2,1)S(1)}, u32[]{:S(2)}, u32[]{:S(2)}) collective-permute-start(bf16[2384,128]{1,0:T(8,128)(2,1)S(1)} %get-tuple-element.71), channel_id=1, source_target_pairs={{0,16},{16,0},{1,17},{17,1},{2,18},{18,2},{3,19},{19,3},{4,20},{20... | collective-permute-start | bytes 1830920 | tf_op jit(solution)/shard_map/ppermute | solution.py:552
  20.9 11.9 %copy-start.1 = (s32[1480,2]{0,1:T(2,128)S(1)}, s32[1480,2]{0,1:T(2,128)}, u32[]{:S(2)}) copy-start(s32[1480,2]{0,1:T(2,128)} %param.3) | copy-start | bytes 35524
  37.2 3.7 %collective-permute-start.2 = (f32[8,304]{1,0:T(8,128)S(1)}, f32[8,304]{1,0:T(8,128)S(1)}, u32[]{:S(2)}, u32[]{:S(2)}) collective-permute-start(f32[8,304]{1,0:T(8,128)S(1)} %get-tuple-element.77), channel_id=1, source_target_pairs={{0,16},{16,0},{1,17},{17,1},{2,18},{18,2},{3,19},{19,3},{4,20},{20... | collective-permute-start | bytes 29192 | tf_op jit(solution)/shard_map/ppermute | solution.py:541
  40.9 4.6 %collective-permute-start.3 = (f32[8,304]{1,0:T(8,128)S(1)}, f32[8,304]{1,0:T(8,128)S(1)}, u32[]{:S(2)}, u32[]{:S(2)}) collective-permute-start(f32[8,304]{1,0:T(8,128)S(1)} %add.28), channel_id=1, source_target_pairs={{0,8},{1,9},{2,10},{3,11},{4,12},{5,13},{6,14},{7,15},{8,0},{9,1},... | collective-permute-start | bytes 29192 | tf_op jit(solution)/shard_map/ppermute | solution.py:541
  45.5 3.8 %collective-permute-start.4 = (f32[8,304]{1,0:T(8,128)S(1)}, f32[8,304]{1,0:T(8,128)S(1)}, u32[]{:S(2)}, u32[]{:S(2)}) collective-permute-start(f32[8,304]{1,0:T(8,128)S(1)} %add.29), channel_id=1, source_target_pairs={{0,4},{1,5},{2,6},{3,7},{4,0},{5,1},{6,2},{7,3},{8,12},{9,13},{10,... | collective-permute-start | bytes 29192 | tf_op jit(solution)/shard_map/ppermute | solution.py:541
  49.3 3.7 %collective-permute-start.5 = (f32[8,304]{1,0:T(8,128)S(1)}, f32[8,304]{1,0:T(8,128)S(1)}, u32[]{:S(2)}, u32[]{:S(2)}) collective-permute-start(f32[8,304]{1,0:T(8,128)S(1)} %add.30), channel_id=1, source_target_pairs={{0,2},{1,3},{2,0},{3,1},{4,6},{5,7},{6,4},{7,5},{8,10},{9,11},{10,... | collective-permute-start | bytes 29192 | tf_op jit(solution)/shard_map/ppermute | solution.py:541
  53.0 1.5 %collective-permute-start.6 = (f32[8,304]{1,0:T(8,128)S(1)}, f32[8,304]{1,0:T(8,128)S(1)}, u32[]{:S(2)}, u32[]{:S(2)}) collective-permute-start(f32[8,304]{1,0:T(8,128)S(1)} %add.31), channel_id=1, source_target_pairs={{0,1},{1,0},{2,3},{3,2},{4,5},{5,4},{6,7},{7,6},{8,9},{9,8},{10,11... | collective-permute-start | bytes 29192 | tf_op jit(solution)/shard_map/ppermute | solution.py:541
